TPU v7x, 256 devices: a whole 4x4x8 slice. The times are simulated.
256 devices in a mesh: hst: 32 (over y, x, core), head: 8 (over z).
Axes of the slice: x: 4, y: 4, z: 8, core: 2. Of those that a mesh axis runs over, the one named last changes fastest.
Arguments:
- ctx_query: bfloat16 [24576, 8192], P('hst', 'head'), may hold values from -88 to 88
- context_key: bfloat16 [24576, 1024], P('hst', 'head'), may hold values from -4 to 4
- context_value: bfloat16 [24576, 1024], P('hst', 'head'), may hold values from -6 to 6
- query: bfloat16 [512, 8192], P(None, 'head'), may hold values from -88 to 88
- out_weight: bfloat16 [8192, 8192], P('head', 'hst'), may hold values from -0.125 to 0.125
Outputs:
- ctx_out: bfloat16 [24576, 8192], P('hst', 'head')
- answer: bfloat16 [512, 8192], P('head', 'hst')
All inputs are finite; a program needn't handle non-finite values.
Results may differ from a plain program's by a relative error of at most 0.007.
Values may be sent and summed in bfloat16 or wider, within the bound.
No kernel may reach another device: no remote copies, remote signals or barrier semaphores. Data moves between devices by JAX's collectives and lax.ppermute only.
A program may use at most 320 MiB of HBM per device.

v0:
```python
import jax
import jax.numpy as jnp
from jax import lax
from jax.sharding import PartitionSpec as P

HEAD_SIZE = 128


def from_root(value, axis, source):
    kept = jnp.where(lax.axis_index(axis) == source, value, 0).astype(value.dtype)
    return lax.psum(kept, axis)


def context_heads(query_rows, rows_of_keys, rows_of_values, visible, group_width):
    row_count = query_rows.shape[0]
    head_count = query_rows.shape[1] // HEAD_SIZE
    scaling = HEAD_SIZE ** (-0.5)
    q_heads = query_rows.reshape(row_count, head_count, HEAD_SIZE).transpose(1, 0, 2)
    key_heads = rows_of_keys.reshape(rows_of_keys.shape[0], -1, HEAD_SIZE).transpose(1, 0, 2)
    value_heads = rows_of_values.reshape(rows_of_values.shape[0], -1, HEAD_SIZE).transpose(1, 0, 2)

    def one_head(head_index):
        q_single = lax.dynamic_index_in_dim(q_heads, head_index, 0, keepdims=False)
        k_single = lax.dynamic_index_in_dim(key_heads, head_index // group_width, 0, keepdims=False)
        v_single = lax.dynamic_index_in_dim(
            value_heads, head_index // group_width, 0, keepdims=False
        )
        scores = (
            jnp.einsum("qd,kd->qk", q_single, k_single, preferred_element_type=jnp.float32)
            * scaling
        )
        scores = jnp.where(visible, scores, -jnp.inf)
        row_peak = jnp.max(scores, axis=1, keepdims=True)
        weights = jnp.exp(scores - row_peak)
        denominator = jnp.sum(weights, axis=1, keepdims=True)
        mixture = jnp.dot(
            weights.astype(jnp.bfloat16), v_single, preferred_element_type=jnp.float32
        )
        return (mixture / denominator).astype(jnp.bfloat16)

    stacked = lax.map(one_head, jnp.arange(head_count, dtype=jnp.int32))
    return stacked.transpose(1, 0, 2).reshape(row_count, head_count * HEAD_SIZE)


def per_device(ctx_query, context_key, context_value, query, out_weight):
    row_count = context_key.shape[0]
    kv_local = context_key.shape[1] // HEAD_SIZE
    head_count = ctx_query.shape[1] // HEAD_SIZE
    group_width = head_count // kv_local
    query_count = query.shape[0]
    scaling = HEAD_SIZE ** (-0.5)
    anchor_pair = from_root(jnp.stack([context_key, context_value]), "hst", 0)
    rows_of_keys = jnp.concatenate([anchor_pair[0], context_key], 0)
    rows_of_values = jnp.concatenate([anchor_pair[1], context_value], 0)
    position = jnp.arange(row_count, dtype=jnp.int32)
    causal = position[None, :] <= position[:, None]
    remote = jnp.broadcast_to(lax.axis_index("hst") > 0, causal.shape)
    visible = jnp.concatenate([remote, causal], 1)
    ctx_out = context_heads(ctx_query, rows_of_keys, rows_of_values, visible, group_width)
    grouped_queries = query.reshape(query_count, kv_local, group_width, HEAD_SIZE)
    key_groups = context_key.reshape(row_count, kv_local, HEAD_SIZE)
    value_groups = context_value.reshape(row_count, kv_local, HEAD_SIZE)
    scores = (
        jnp.einsum(
            "qcgd,kcd->cgqk", grouped_queries, key_groups, preferred_element_type=jnp.float32
        )
        * scaling
    )
    row_peak = jnp.max(scores, axis=3)
    weights = jnp.exp(scores - row_peak[..., None])
    denominator = jnp.sum(weights, axis=3)
    partial_value = jnp.einsum(
        "cgqk,kcd->cgqd",
        weights.astype(jnp.bfloat16),
        value_groups,
        preferred_element_type=jnp.float32,
    )
    global_peak = lax.pmax(row_peak, "hst")
    factor = jnp.exp(row_peak - global_peak)
    total_all, acc_all = lax.psum((denominator * factor, partial_value * factor[..., None]), "hst")
    attended = (acc_all / total_all[..., None]).astype(jnp.bfloat16)
    attended = attended.transpose(2, 0, 1, 3).reshape(query_count, head_count * HEAD_SIZE)
    summed = lax.psum_scatter(
        jnp.dot(attended, out_weight, preferred_element_type=jnp.float32),
        "head",
        scatter_dimension=0,
        tiled=True,
    )
    return (ctx_out, summed.astype(jnp.bfloat16))


def solution(mesh):
    in_specs = (
        P("hst", "head"),
        P("hst", "head"),
        P("hst", "head"),
        P(None, "head"),
        P("head", "hst"),
    )
    out_specs = (P("hst", "head"), P("head", "hst"))
    return jax.shard_map(
        per_device, mesh=mesh, in_specs=in_specs, out_specs=out_specs, check_vma=False
    )
```

profile of v0, /device:TPU:1, one launch (start us, length us, event | category | flops | bytes accessed | tf_op | source)
XLA Modules:
  0.0 349.7 jit_solution(470721400796063899)
XLA Ops:
  7.2 1.9 maximum_select_fusion
  9.2 2.7 bitcast_reduce_fusion
  12.0 2.1 fusion.23
  14.0 2.5 copy-done.1
  16.5 124.3 %pmax.7 = f32[1,8,512]{2,1,0:T(8,128)S(1)} all-reduce(f32[1,8,512]{2,1,0:T(8,128)S(1)} %bitcast.108), channel_id=1, replica_groups=mesh['hst'=32,'head'=8] {'hst'}, use_global_device_ids=true, to_apply=%region_6.7 | all-reduce | flops 4096 | bytes 32768 | tf_op jit(solution)/shard_map/pmax | solution.py:78
  140.9 8.5 %multiply_bitcast_fusion = f32[1,8,512,128]{3,2,1,0:T(8,128)} fusion(f32[768,512,8]{1,0,2:T(8,128)} %copy-done.1, f32[8,512]{1,0:T(8,128)S(1)} %get-tuple-element.67, f32[8,512]{1,0:T(8,128)S(1)} %get-tuple-element.66, bf16[768,128]{1,0:T(8,128)(2,1)S(1)} %copy-done.2), kind=kOutput, calls=%fused_computation.26 | convolution fusion | flops 815267840 | bytes 14909440 | tf_op jit(solution)/shard_map/cgqk,kcd->cgqd/dot_general | solution.py:72
  149.9 0.4 copy.36
  150.3 2.6 copy.10
  152.9 124.5 %psum.23 = f32[8,512]{1,0:T(8,128)S(1)} all-reduce(f32[8,512]{1,0:T(8,128)S(1)} %get-tuple-element.65), channel_id=1, replica_groups=mesh['hst'=32,'head'=8] {'hst'}, use_global_device_ids=true, to_apply=%region_9.10 | all-reduce | flops 4096 | bytes 32768 | tf_op jit(solution)/shard_map/psum | solution.py:80
  277.4 1.0 slice_bitcast_fusion
  278.6 2.8 fusion.35
  281.4 2.3 copy.15
  283.7 2.6 fusion.42
  286.3 52.5 %while.10 = (s32[]{:T(128)}, bf16[8,768,128]{2,1,0:T(8,128)(2,1)}, s32[8]{0:T(128)S(1)}, bf16[8,768,128]{1,2,0:T(8,128)(2,1)}, bf16[1,1536,128]{2,1,0:T(8,128)(2...) while((s32[]{:T(128)}, bf16[8,768,128]{2,1,0:T(8,128)(2,1)}, ...), condition=%wide.region_4.5_spmd, body=%wide.region_1.4_spmd.sunk | while | flops 612432384 | bytes 16531095 | solution.py:41
  286.4 0.6 dynamic_slice.20
  288.6 2.0 fusion.54
  290.6 0.8 fusion.55
  291.4 1.6 fusion.56
  292.9 0.6 dynamic_slice.20
  295.1 2.0 fusion.54
  297.2 0.8 fusion.55
  297.9 1.6 fusion.56
  299.5 0.6 dynamic_slice.20
  301.7 2.0 fusion.54
  303.7 0.8 fusion.55
  304.5 1.6 fusion.56
  306.1 0.6 dynamic_slice.20
  308.2 2.0 fusion.54
  310.3 0.8 fusion.55
  311.1 1.6 fusion.56
  312.6 0.6 dynamic_slice.20
  314.8 2.0 fusion.54
  316.8 0.8 fusion.55
  317.6 1.6 fusion.56
  319.2 0.6 dynamic_slice.20
  321.4 2.0 fusion.54
  323.4 0.8 fusion.55
  324.2 1.6 fusion.56
  325.8 0.6 dynamic_slice.20
  328.0 2.0 fusion.54
  330.0 0.8 fusion.55
  330.8 1.6 fusion.56
  332.3 0.6 dynamic_slice.20
  334.5 2.0 fusion.54
  336.5 0.8 fusion.55
  337.3 1.6 fusion.56
  338.9 2.8 copy_bitcast_fusion
  341.7 1.5 convert_element_type.19
  (23 shorter events, 0.7 us)
Async XLA Ops:
  7.2 2.0 copy-start
  7.2 270.3 %all-reduce.4.cloned.1.call-start = ((), (), s32[]{:S(2)}) async-start(), calls=%async_computation.1 | async-start | bytes 786432 | tf_op jit(solution)/shard_map/psum | solution.py:11
  9.2 269.4 %all-reduce.6.cloned.1.call-start = ((), (), s32[]{:S(2)}) async-start(), calls=%async_computation.2 | async-start | bytes 4194304 | tf_op jit(solution)/shard_map/psum | solution.py:80
  12.0 4.6 %copy-start.1 = (f32[768,512,8]{1,0,2:T(8,128)}, f32[768,512,8]{1,0,2:T(8,128)S(1)}, u32[]{:S(2)}) copy-start(f32[768,512,8]{1,0,2:T(8,128)S(1)} %get-tuple-element.68) | copy-start | bytes 37748740
  12.0 128.9 %copy-start.2 = (bf16[768,128]{1,0:T(8,128)(2,1)S(1)}, bf16[768,128]{1,0:T(8,128)(2,1)}, u32[]{:S(2)}) copy-start(bf16[768,128]{1,0:T(8,128)(2,1)} %param.9) | copy-start | bytes 589828
  149.4 129.1 %copy-start.3 = (bf16[768,128]{1,0:T(8,128)(2,1)S(1)}, bf16[768,128]{1,0:T(8,128)(2,1)}, u32[]{:S(2)}) copy-start(bf16[768,128]{1,0:T(8,128)(2,1)} %param.8) | copy-start | bytes 589828
  149.5 192.2 %reduce-scatter.2.cloned.1.call-start = ((), (), s32[]{:S(2)}) async-start(), calls=%async_computation.3 | async-start | bytes 589824 | tf_op jit(solution)/shard_map/reduce_scatter | solution.py:83
Sparse Core Ops, SparseCore 0:
  11.2 116.5 all-reduce.3
  149.6 120.2 all-reduce.5
  286.5 34.9 reduce-scatter.1
where the time goes:
time: 354 us; the launch traced here: 350 us
  blocking collectives  249 us (70%)
  matrix products  42.7 us (12%)
  local copies, waits for them, and re-layouts  16.2 us (5%)
  other arithmetic  14.6 us (4%)
  between operations  13.9 us (4%)
  loops' own time  13.2 us (4%)
    psum x1, blocking collectives, per_device(): lax.psum((denominator * factor, partial_value * factor[..., None]), 'hst')  125 us
    pmax x1, blocking collectives, per_device(): global_peak = lax.pmax(row_peak, 'hst')  124 us
    dot_general x8, matrix products, one_head(): jnp.einsum('qd,kd->qk', q_single, k_single, preferred_element_type=jnp.fl...  16.2 us
    another operation x1, loops' own time, context_heads(): stacked = lax.map(one_head, jnp.arange(head_count, dtype=jnp.int32))  13.2 us
    dot_general x8, matrix products, one_head(): jnp.dot(weights.astype(jnp.bfloat16), v_single, preferred_element_type=jn...  12.6 us
    dot_general x1, matrix products, per_device(): jnp.einsum('cgqk,kcd->cgqd', weights.astype(jnp.bfloat16), value_groups,...  8.54 us
  transfers between devices with their start and end apart: 3, of which 0 were waited for; matrix products, arithmetic and copies ran while one was open for 17% of the time, Pallas kernels for 0%

commit v1 on v0

v1 whole, which is shorter than its diff:
```python
import jax
import jax.numpy as jnp
from jax import lax
from jax.experimental import pallas as pl
from jax.experimental.pallas import tpu as pltpu
from jax.sharding import Mesh, PartitionSpec as P

HEAD = 128
BLOCK = 768
HEADS = 8
QROWS = 512
HALF = 256
ANCHOR_ROWS = 48
SEND1 = 192
SEND2 = 176
HIDDEN = 1e30
LOG2_SCALE = 1.4426950408889634 * HEAD ** (-0.5)
BF = jnp.bfloat16
F32 = jnp.float32
VMEM_LIMIT = 24 * 1024 * 1024


def fill_keys(keys_t, column, k_ref):
    k = k_ref[...].astype(F32) * LOG2_SCALE
    high = k.astype(BF)
    low = (k - high.astype(F32)).astype(BF)
    keys_t[0:HEAD, column : column + BLOCK] = high.astype(F32).T.astype(BF)
    keys_t[HEAD : 2 * HEAD, column : column + BLOCK] = low.astype(F32).T.astype(BF)


def fill_values(values, row, v_ref):
    values[row : row + BLOCK, 0:HEAD] = v_ref[...]
    values[row : row + BLOCK, HEAD : 2 * HEAD] = jnp.ones((BLOCK, HEAD), BF)


def eye_mask():
    r = lax.broadcasted_iota(jnp.int32, (HEAD, HEAD), 0)
    c = lax.broadcasted_iota(jnp.int32, (HEAD, HEAD), 1)
    return r == c


def to_lanes(column):
    return jnp.sum(jnp.where(eye_mask(), column, 0.0), axis=0, keepdims=True)


def query_kernel(q_ref, k_ref, v_ref, kp_ref, vp_ref, out_ref, keys_t, values):
    j = pl.program_id(0)
    core = lax.axis_index("c")

    @pl.when(j == 0)
    def _():
        fill_keys(keys_t, 0, k_ref)
        fill_keys(keys_t, BLOCK, kp_ref)
        fill_values(values, 0, v_ref)
        fill_values(values, BLOCK, vp_ref)

    q = jnp.concatenate(
        [q_ref[pl.ds(pl.multiple_of(64 * z + 32 * core, 32), 32), :] for z in range(8)], axis=0
    )
    s = jnp.dot(jnp.concatenate([q, q], axis=1), keys_t[...], preferred_element_type=F32)
    peak = jnp.max(s, axis=1, keepdims=True).astype(BF).astype(F32)
    p = jnp.exp2(s - peak).astype(BF)
    acc = jnp.dot(p, values[...], preferred_element_type=F32)
    total = acc[:, HEAD : HEAD + 1]
    row_id = lax.broadcasted_iota(jnp.int32, (16, HEAD), 0)
    for half in range(2):
        rows = slice(half * HEAD, half * HEAD + HEAD)
        out_ref[half, 0:HEAD, :] = acc[rows, 0:HEAD].astype(BF)
        peak_l = to_lanes(peak[rows])
        total_l = to_lanes(total[rows])
        high = total_l.astype(BF).astype(F32)
        stats = jnp.where(row_id == 0, peak_l, 0.0)
        stats = jnp.where(row_id == 1, high, stats)
        stats = jnp.where(row_id == 2, total_l - high, stats)
        out_ref[half, HEAD : HEAD + 16, :] = stats.astype(BF)
        at = pl.multiple_of((2 * j + half) * ANCHOR_ROWS, ANCHOR_ROWS)
        own = k_ref[pl.ds(at, ANCHOR_ROWS), :]
        other = vp_ref[pl.ds(at, ANCHOR_ROWS), :]
        out_ref[half, HEAD + 16 : SEND1, :] = jnp.where(core == 0, own, other)


def combine_kernel(in_ref, out_ref):
    stats = in_ref[:, HEAD : HEAD + 16, :].astype(F32)
    peak = stats[:, 0, :]
    total = stats[:, 1, :] + stats[:, 2, :]
    top = jnp.max(peak, axis=0, keepdims=True)
    weight = jnp.exp2(peak - top)
    weight = weight / jnp.sum(weight * total, axis=0, keepdims=True)
    weight_t = jnp.concatenate([weight, jnp.zeros((HEAD - 16, HEAD), F32)], axis=0).T
    out = jnp.zeros((HEAD, HEAD), F32)
    for g in range(16):
        out = out + weight_t[:, g : g + 1] * in_ref[g, 0:HEAD, :].astype(F32)
    out = out.astype(BF)
    anchor = in_ref[0, HEAD + 16 : SEND1, :]
    for g in range(16):
        out_ref[g, 0:HEAD, :] = out
        out_ref[g, HEAD:SEND2, :] = anchor


def project_kernel(in_ref, w_ref, wp_ref, out_ref, anchor_ref):
    core = lax.axis_index("c")
    for g in range(16):
        anchor_ref[g * ANCHOR_ROWS : (g + 1) * ANCHOR_ROWS, :] = in_ref[g, HEAD:SEND2, :]
    a = jnp.concatenate(
        [
            jnp.concatenate([in_ref[2 * j + half, 0:HEAD, :] for j in range(HEADS)], axis=1)
            for half in range(2)
        ],
        axis=0,
    )
    for w, dest in ((w_ref, core), (wp_ref, 1 - core)):
        y = jnp.dot(a, w[...], preferred_element_type=F32).astype(BF)
        for z in range(8):
            out_ref[2 * z + dest] = y[32 * z : 32 * z + 32, :]


def final_kernel(in_ref, out_ref):
    for half in range(2):
        total = in_ref[half].astype(F32)
        for z in range(1, 8):
            total = total + in_ref[2 * z + half].astype(F32)
        out_ref[32 * half : 32 * half + 32, :] = total.astype(BF)


def context_kernel(q_ref, k_ref, v_ref, ka_ref, va_ref, out_ref, keys_t, values):
    @pl.when(pl.program_id(0) == 0)
    def _():
        fill_keys(keys_t, 0, k_ref)
        fill_keys(keys_t, BLOCK, ka_ref)
        fill_values(values, 0, v_ref)
        fill_values(values, BLOCK, va_ref)

    first = jnp.logical_and(
        lax.axis_index("c") == 0,
        jnp.logical_and(lax.axis_index("x") == 0, lax.axis_index("y") == 0),
    )
    r = lax.broadcasted_iota(jnp.int32, (HALF, HALF), 0)
    c = lax.broadcasted_iota(jnp.int32, (HALF, HALF), 1)
    for i in range(3):
        own = (i + 1) * HALF
        q = q_ref[i * HALF : own, :]
        qq = jnp.concatenate([q, q], axis=1)
        s_own = jnp.dot(qq, keys_t[:, 0:own], preferred_element_type=F32)
        s_diag = jnp.where(c <= r, s_own[:, own - HALF : own], -HIDDEN)
        s_anchor = jnp.dot(qq, keys_t[:, BLOCK : 2 * BLOCK], preferred_element_type=F32)
        peak = jnp.max(s_diag, axis=1, keepdims=True)
        if i > 0:
            peak = jnp.maximum(peak, jnp.max(s_own[:, 0 : own - HALF], axis=1, keepdims=True))
        peak_a = jnp.max(s_anchor, axis=1, keepdims=True)
        peak = jnp.where(first, peak, jnp.maximum(peak, peak_a))
        shift = jnp.where(first, HIDDEN, peak)
        acc = jnp.dot(
            jnp.exp2(s_diag - peak).astype(BF),
            values[own - HALF : own, :],
            preferred_element_type=F32,
        )
        if i > 0:
            acc += jnp.dot(
                jnp.exp2(s_own[:, 0 : own - HALF] - peak).astype(BF),
                values[0 : own - HALF, :],
                preferred_element_type=F32,
            )
        acc += jnp.dot(
            jnp.exp2(s_anchor - shift).astype(BF),
            values[BLOCK : 2 * BLOCK, :],
            preferred_element_type=F32,
        )
        out_ref[i * HALF : own, :] = (acc[:, 0:HEAD] / acc[:, HEAD : 2 * HEAD]).astype(BF)


def whole(shape):
    return pl.BlockSpec(shape, lambda *_: (0,) * len(shape))


def params():
    return pltpu.CompilerParams(vmem_limit_bytes=VMEM_LIMIT)


def cost(flops, nbytes, exps=0):
    return pl.CostEstimate(flops=flops, bytes_accessed=nbytes, transcendentals=exps)


def query_call(query, k, v, kp, vp):
    return pl.pallas_call(
        query_kernel,
        grid=(HEADS,),
        in_specs=[pl.BlockSpec((QROWS, HEAD), lambda j: (0, j))] + [whole((BLOCK, HEAD))] * 4,
        out_specs=pl.BlockSpec((2, SEND1, HEAD), lambda j: (j, 0, 0)),
        out_shape=jax.ShapeDtypeStruct((16, SEND1, HEAD), BF),
        scratch_shapes=[pltpu.VMEM((2 * HEAD, 2 * BLOCK), BF), pltpu.VMEM((2 * BLOCK, 2 * HEAD), BF)],
        compiler_params=params(),
        cost_estimate=cost(4 * 2048 * 1536 * 256, 3 << 20, 2048 * 1536),
        name="query_attention",
    )(query, k, v, kp, vp)


def context_call(ctx_query, k, v, ka, va):
    return pl.pallas_call(
        context_kernel,
        grid=(HEADS,),
        in_specs=[pl.BlockSpec((BLOCK, HEAD), lambda j: (0, j))] + [whole((BLOCK, HEAD))] * 4,
        out_specs=pl.BlockSpec((BLOCK, HEAD), lambda j: (0, j)),
        out_shape=jax.ShapeDtypeStruct((BLOCK, HEADS * HEAD), BF),
        scratch_shapes=[pltpu.VMEM((2 * HEAD, 2 * BLOCK), BF), pltpu.VMEM((2 * BLOCK, 2 * HEAD), BF)],
        compiler_params=params(),
        cost_estimate=cost(4 * 6144 * 1280 * 256, 4 << 20, 6144 * 1280),
        name="context_attention",
    )(ctx_query, k, v, ka, va)


def combine_call(received):
    return pl.pallas_call(
        combine_kernel,
        out_shape=jax.ShapeDtypeStruct((16, SEND2, HEAD), BF),
        in_specs=[pl.BlockSpec(memory_space=pltpu.VMEM)],
        out_specs=pl.BlockSpec(memory_space=pltpu.VMEM),
        compiler_params=params(),
        cost_estimate=cost(1 << 20, 3 << 19),
        name="combine",
    )(received)


def project_call(gathered, w, wp):
    return pl.pallas_call(
        project_kernel,
        out_shape=(
            jax.ShapeDtypeStruct((16, 32, 256), BF),
            jax.ShapeDtypeStruct((BLOCK, HEAD), BF),
        ),
        in_specs=[pl.BlockSpec(memory_space=pltpu.VMEM)] * 3,
        out_specs=(pl.BlockSpec(memory_space=pltpu.VMEM),) * 2,
        compiler_params=params(),
        cost_estimate=cost(2 * 256 * 1024 * 512, 2 << 20),
        name="project",
    )(gathered, w, wp)


def final_call(received):
    return pl.pallas_call(
        final_kernel,
        out_shape=jax.ShapeDtypeStruct((64, 256), BF),
        in_specs=[pl.BlockSpec(memory_space=pltpu.VMEM)],
        out_specs=pl.BlockSpec(memory_space=pltpu.VMEM),
        compiler_params=params(),
        cost_estimate=cost(1 << 17, 1 << 18),
        name="final_sum",
    )(received)


def swap(value):
    return lax.ppermute(value, "c", [(0, 1), (1, 0)])


def exchange(value, axes):
    return lax.all_to_all(value, axes, 0, 0, tiled=True)


def per_device(ctx_query, context_key, context_value, query, out_weight):
    key_p, value_p = swap(context_key), swap(context_value)
    weight_p = swap(out_weight)
    sent = query_call(query, context_key, context_value, key_p, value_p)
    received = exchange(sent, ("y", "x"))
    gathered = exchange(combine_call(received), ("y", "x"))
    shares, anchor = project_call(gathered, out_weight, weight_p)
    answer = final_call(exchange(shares, ("z", "c")))
    anchor_p = swap(anchor)
    core = lax.axis_index("c")
    key_a = jnp.where(core == 0, anchor, anchor_p)
    value_a = jnp.where(core == 0, anchor_p, anchor)
    ctx_out = context_call(ctx_query, context_key, context_value, key_a, value_a)
    return ctx_out, answer


def solution(mesh):
    fine = Mesh(mesh.devices.reshape(4, 4, 2, 8), ("y", "x", "c", "z"))
    hst = ("y", "x", "c")
    in_specs = (P(hst, "z"), P(hst, "z"), P(hst, "z"), P(None, "z"), P("z", hst))
    out_specs = (P(hst, "z"), P("z", hst))
    return jax.shard_map(
        per_device, mesh=fine, in_specs=in_specs, out_specs=out_specs, check_vma=False
    )
```

time: 354 us -> 90.2 us (0.25); the launches traced: 350 us -> 89.7 us
  blocking collectives: 249 us -> 18.7 us
  matrix products: 42.7 us -> 0 us
  Pallas kernels: 0 us -> 33.6 us
  starting transfers between devices: 0.12 us -> 19.6 us
  other arithmetic: 14.6 us -> 0.03 us
  between operations: 13.9 us -> 0.7 us
  loops' own time: 13.2 us -> 0 us
  waiting for transfers between devices: 0.07 us -> 12.1 us
  local copies, waits for them, and re-layouts: 16.2 us -> 4.94 us
    psum x1 -> x0, blocking collectives: 125 us -> none  [per_device(): lax.psum((denominator * factor, partial_value * factor[..., None]), 'hst')]
    pmax x1 -> x0, blocking collectives: 124 us -> none  [per_device(): global_peak = lax.pmax(row_peak, 'hst')]
    dot_general x19 -> x0, matrix products: 42.7 us -> none  [the longest x8 16.2 us: one_head(): jnp.einsum('qd,kd->qk', q_single, k_single, preferred_element_type=jnp.fl...]
    pallas_call x0 -> x5, Pallas kernels: none -> 33.6 us  [the longest x1 20.2 us: context_call(): pl.pallas_call(context_kernel, grid=(HEADS,), in_specs=[pl.BlockSpec((BLO...]
    all_to_all x0 -> x1, blocking collectives: none -> 18.7 us  [exchange(): return lax.all_to_all(value, axes, 0, 0, tiled=True)]
    another operation x1 -> x0, loops' own time: 13.2 us -> none  [context_heads(): stacked = lax.map(one_head, jnp.arange(head_count, dtype=jnp.int32))]
    all_to_all x0 -> x2, starting transfers between devices: none -> 12.2 us  [exchange(): return lax.all_to_all(value, axes, 0, 0, tiled=True)]
    all_to_all x0 -> x2, waiting for transfers between devices: none -> 9.04 us  [exchange(): return lax.all_to_all(value, axes, 0, 0, tiled=True)]
  transfers between devices with their start and end apart: 3 -> 6, of which waited for: 0 -> 4; matrix products, arithmetic and copies ran while one was open for 17% -> 0% of each run, Pallas kernels for 0% -> 22%
where the time goes in v1:
time: 90.2 us; the launch traced here: 89.7 us
  Pallas kernels  33.6 us (37%)
  starting transfers between devices  19.6 us (22%)
  blocking collectives  18.7 us (21%)
  waiting for transfers between devices  12.1 us (13%)
  local copies, waits for them, and re-layouts  4.94 us (5%)
    pallas_call x1, Pallas kernels, context_call(): pl.pallas_call(context_kernel, grid=(HEADS,), in_specs=[pl.BlockSpec((BLO...  20.2 us
    all_to_all x1, blocking collectives, exchange(): return lax.all_to_all(value, axes, 0, 0, tiled=True)  18.7 us
    all_to_all x2, starting transfers between devices, exchange(): return lax.all_to_all(value, axes, 0, 0, tiled=True)  12.2 us
    pallas_call x1, Pallas kernels, query_call(): pl.pallas_call(query_kernel, grid=(HEADS,), in_specs=[pl.BlockSpec((QROWS...  10.2 us
    all_to_all x2, waiting for transfers between devices, exchange(): return lax.all_to_all(value, axes, 0, 0, tiled=True)  9.04 us
    ppermute x4, starting transfers between devices, swap(): return lax.ppermute(value, 'c', [(0, 1), (1, 0)])  7.39 us
    unnamed x14, local copies, waits for them, and re-layouts  4.94 us
    ppermute x4, waiting for transfers between devices, swap(): return lax.ppermute(value, 'c', [(0, 1), (1, 0)])  3.09 us
  transfers between devices with their start and end apart: 6, of which 4 were waited for; matrix products, arithmetic and copies ran while one was open for 0% of the time, Pallas kernels for 22%

profile of v1, /device:TPU:1, one launch (start us, length us, event | category | flops | bytes accessed | tf_op | source)
XLA Modules:
  0.0 89.7 jit_solution(3965427906398516791)
XLA Ops:
  0.6 3.3 %collective-permute-start = (bf16[768,128]{1,0:T(8,128)(2,1)}, bf16[768,128]{1,0:T(8,128)(2,1)S(1)}, u32[]{:S(2)}, u32[]{:S(2)}) collective-permute-start(bf16[768,128]{1,0:T(8,128)(2,1)} %k_ref.3), channel_id=1, source_target_pairs={{0,8},{8,0},{1,9},{9,1},{2,10},{10,2},{3,11},{11,3},{4,12},{12,4},... | collective-permute-start | bytes 589832 | tf_op jit(solution)/shard_map/ppermute | solution.py:251
  4.0 0.1 collective-permute-start.1
  4.1 1.2 %collective-permute-done.kp_ref = bf16[768,128]{1,0:T(8,128)(2,1)S(1)} collective-permute-done((bf16[768,128]{1,0:T(8,128)(2,1)}, bf16[768,128]{1,0:T(8,128)(2,1)S(1)}, u32[]{:S(2)}, u32[]{:S(2)}) %collective-permute-start) | collective-permute-done | bytes 196640 | tf_op jit(solution)/shard_map/ppermute | solution.py:251
  5.2 0.4 collective-permute-done.1.vp_ref
  5.6 0.0 copy-start.2
  5.6 1.2 %copy-done.2 = bf16[512,1024]{1,0:T(8,128)(2,1)S(1)} copy-done((bf16[512,1024]{1,0:T(8,128)(2,1)S(1)}, bf16[512,1024]{1,0:T(8,128)(2,1)}, u32[]{:S(2)}) %copy-start.2) | copy-done | bytes 1048600
  6.8 0.0 copy-start.3
  6.8 0.9 %copy-done.3 = bf16[768,128]{1,0:T(8,128)(2,1)S(1)} copy-done((bf16[768,128]{1,0:T(8,128)(2,1)S(1)}, bf16[768,128]{1,0:T(8,128)(2,1)}, u32[]{:S(2)}) %copy-start.3) | copy-done | bytes 196632
  7.8 0.0 copy-start.5
  7.8 0.9 %copy-done.5 = bf16[768,128]{1,0:T(8,128)(2,1)S(1)} copy-done((bf16[768,128]{1,0:T(8,128)(2,1)S(1)}, bf16[768,128]{1,0:T(8,128)(2,1)}, u32[]{:S(2)}) %copy-start.5) | copy-done | bytes 196632
  8.7 10.2 %query_attention.1 = bf16[16,192,128]{2,1,0:T(8,128)(2,1)S(1)} custom-call(bf16[512,1024]{1,0:T(8,128)(2,1)S(1)} %copy-done.2, bf16[768,128]{1,0:T(8,128)(2,1)S(1)} %copy-done.3, bf16[768,128]{1,0:T(8,128)(2,1)S(1)} %copy-done.5, bf16[768,128]{1,0:T(8,128)(2,1)S(1)} %collective-permute-done.kp_ref, bf16[768,128]{1,0:T(8,128)(2,1)S(1)} %collective-permute-done.1.vp_ref), custom_call_target="tpu_custom_call" | custom-call | flops 3221225472 | bytes 3145728 | tf_op jit(solution)/shard_map/query_attention/pallas_call | solution.py:184
  18.9 18.7 %all_to_all.15.in_ref = bf16[16,192,128]{2,1,0:T(8,128)(2,1)S(1)} all-to-all(bf16[16,192,128]{2,1,0:T(8,128)(2,1)S(1)} %query_attention.1), channel_id=1, replica_groups=mesh['y'=4,'x'=4,'c'=2,'z'=8] {'y','x'}, dimensions={0} | all-to-all | bytes 1572864 | tf_op jit(solution)/shard_map/all_to_all | solution.py:255
  37.7 0.0 copy-start
  37.7 1.4 %combine.1 = bf16[16,176,128]{2,1,0:T(8,128)(2,1)} custom-call(bf16[16,192,128]{2,1,0:T(8,128)(2,1)S(1)} %all_to_all.15.in_ref), custom_call_target="tpu_custom_call" | custom-call | flops 1048576 | bytes 1572864 | tf_op jit(solution)/shard_map/combine/pallas_call | solution.py:212
  39.1 3.6 %all-to-all-start.1 = ((bf16[16,176,128]{2,1,0:T(8,128)(2,1)}), bf16[16,176,128]{2,1,0:T(8,128)(2,1)S(1)}, u32[]{:S(2)}, u32[]{:S(2)}) async-start(bf16[16,176,128]{2,1,0:T(8,128)(2,1)} %combine.1), calls=%async_computation.1 | async-start | bytes 1441792 | tf_op jit(solution)/shard_map/all_to_all | solution.py:255
  42.7 0.0 copy-done
  42.7 0.0 copy-start.1
  42.7 1.5 %collective-permute-start.2 = (bf16[1024,256]{1,0:T(8,128)(2,1)S(1)}, bf16[1024,256]{1,0:T(8,128)(2,1)S(1)}, u32[]{:S(2)}, u32[]{:S(2)}) collective-permute-start(bf16[1024,256]{1,0:T(8,128)(2,1)S(1)} %copy-done), channel_id=1, source_target_pairs={{0,8},{8,0},{1,9},{9,1},{2,10},{10,2},{3,11},{11,3},{4,12},{12,4},... | collective-permute-start | bytes 1572872 | tf_op jit(solution)/shard_map/ppermute | solution.py:251
  44.2 1.5 %collective-permute-done.2.wp_ref = bf16[1024,256]{1,0:T(8,128)(2,1)S(1)} collective-permute-done((bf16[1024,256]{1,0:T(8,128)(2,1)S(1)}, bf16[1024,256]{1,0:T(8,128)(2,1)S(1)}, u32[]{:S(2)}, u32[]{:S(2)}) %collective-permute-start.2) | collective-permute-done | bytes 524320 | tf_op jit(solution)/shard_map/ppermute | solution.py:251
  45.7 9.0 %all-to-all-done.1.in_ref = bf16[16,176,128]{2,1,0:T(8,128)(2,1)S(1)} async-done(((bf16[16,176,128]{2,1,0:T(8,128)(2,1)}), bf16[16,176,128]{2,1,0:T(8,128)(2,1)S(1)}, u32[]{:S(2)}, u32[]{:S(2)}) %all-to-all-start.1) | async-done | bytes 720928 | tf_op jit(solution)/shard_map/all_to_all | solution.py:255
  54.8 1.1 %project.1 = (bf16[16,32,256]{2,1,0:T(8,128)(2,1)}, bf16[768,128]{1,0:T(8,128)(2,1)S(1)}) custom-call(bf16[16,176,128]{2,1,0:T(8,128)(2,1)S(1)} %all-to-all-done.1.in_ref, bf16[1024,256]{1,0:T(8,128)(2,1)S(1)} %copy-done, bf16[1024,256]{1,0:T(8,128)(2,1)S(1)} %collective-permute-done.2.wp_ref), custom_call_target="tpu_custom_call" | custom-call | flops 268435456 | bytes 2097152 | tf_op jit(solution)/shard_map/project/pallas_call | solution.py:224
  55.9 2.5 %collective-permute-start.3 = (bf16[768,128]{1,0:T(8,128)(2,1)S(1)}, bf16[768,128]{1,0:T(8,128)(2,1)S(1)}, u32[]{:S(2)}, u32[]{:S(2)}) collective-permute-start(bf16[768,128]{1,0:T(8,128)(2,1)S(1)} %get-tuple-element.4), channel_id=1, source_target_pairs={{0,8},{8,0},{1,9},{9,1},{2,10},{10,2},{3,11},{11,3},{4,12},{12,4},... | collective-permute-start | bytes 589832 | tf_op jit(solution)/shard_map/ppermute | solution.py:251
  58.4 8.6 %all-to-all-start.2 = ((bf16[16,32,256]{2,1,0:T(8,128)(2,1)}), bf16[16,32,256]{2,1,0:T(8,128)(2,1)S(1)}, u32[]{:S(2)}, u32[]{:S(2)}) async-start(bf16[16,32,256]{2,1,0:T(8,128)(2,1)} %get-tuple-element.5), calls=%async_computation.2 | async-start | bytes 524288 | tf_op jit(solution)/shard_map/all_to_all | solution.py:255
  67.0 0.0 collective-permute-done.3
  67.0 0.0 copy-done.1
  67.0 0.0 copy-start.4
  67.0 0.9 %copy-done.4 = bf16[768,128]{1,0:T(8,128)(2,1)S(1)} copy-done((bf16[768,128]{1,0:T(8,128)(2,1)S(1)}, bf16[768,128]{1,0:T(8,128)(2,1)}, u32[]{:S(2)}) %copy-start.4) | copy-done | bytes 196632
  68.0 0.0 copy-start.6
  68.0 0.9 %copy-done.6 = bf16[768,128]{1,0:T(8,128)(2,1)S(1)} copy-done((bf16[768,128]{1,0:T(8,128)(2,1)S(1)}, bf16[768,128]{1,0:T(8,128)(2,1)}, u32[]{:S(2)}) %copy-start.6) | copy-done | bytes 196632
  68.9 20.2 %context_attention.1 = bf16[768,1024]{1,0:T(8,128)(2,1)} custom-call(bf16[768,1024]{1,0:T(8,128)(2,1)S(1)} %copy-done.1, bf16[768,128]{1,0:T(8,128)(2,1)S(1)} %copy-done.4, bf16[768,128]{1,0:T(8,128)(2,1)S(1)} %copy-done.6, bf16[768,128]{1,0:T(8,128)(2,1)S(1)} %get-tuple-element.7.ka_ref, bf16[768,128]{1,0:T(8,128)(2,1)S(1)} %get-tuple-element.6.va_ref), custom_call_target="tpu_custom_call" | custom-call | flops 8053063680 | bytes 4194304 | tf_op jit(solution)/shard_map/context_attention/pallas_call | solution.py:198
  89.1 0.0 all-to-all-done.2.in_ref
  89.1 0.7 final_sum.1
  (1 shorter events, 0.0 us)
Async XLA Ops:
  0.6 4.6 %collective-permute-start = (bf16[768,128]{1,0:T(8,128)(2,1)}, bf16[768,128]{1,0:T(8,128)(2,1)S(1)}, u32[]{:S(2)}, u32[]{:S(2)}) collective-permute-start(bf16[768,128]{1,0:T(8,128)(2,1)} %k_ref.3), channel_id=1, source_target_pairs={{0,8},{8,0},{1,9},{9,1},{2,10},{10,2},{3,11},{11,3},{4,12},{12,4},... | collective-permute-start | bytes 589832 | tf_op jit(solution)/shard_map/ppermute | solution.py:251
  4.0 1.7 %collective-permute-start.1 = (bf16[768,128]{1,0:T(8,128)(2,1)}, bf16[768,128]{1,0:T(8,128)(2,1)S(1)}, u32[]{:S(2)}, u32[]{:S(2)}) collective-permute-start(bf16[768,128]{1,0:T(8,128)(2,1)} %v_ref.3), channel_id=1, source_target_pairs={{0,8},{8,0},{1,9},{9,1},{2,10},{10,2},{3,11},{11,3},{4,12},{12,4},... | collective-permute-start | bytes 589832 | tf_op jit(solution)/shard_map/ppermute | solution.py:251
  5.6 1.2 %copy-start.2 = (bf16[512,1024]{1,0:T(8,128)(2,1)S(1)}, bf16[512,1024]{1,0:T(8,128)(2,1)}, u32[]{:S(2)}) copy-start(bf16[512,1024]{1,0:T(8,128)(2,1)} %q_ref.2) | copy-start | bytes 3145732
  6.8 0.9 %copy-start.3 = (bf16[768,128]{1,0:T(8,128)(2,1)S(1)}, bf16[768,128]{1,0:T(8,128)(2,1)}, u32[]{:S(2)}) copy-start(bf16[768,128]{1,0:T(8,128)(2,1)} %k_ref.3) | copy-start | bytes 589828
  7.8 0.9 %copy-start.5 = (bf16[768,128]{1,0:T(8,128)(2,1)S(1)}, bf16[768,128]{1,0:T(8,128)(2,1)}, u32[]{:S(2)}) copy-start(bf16[768,128]{1,0:T(8,128)(2,1)} %v_ref.3) | copy-start | bytes 589828
  37.7 5.0 %copy-start = (bf16[1024,256]{1,0:T(8,128)(2,1)S(1)}, bf16[1024,256]{1,0:T(8,128)(2,1)}, u32[]{:S(2)}) copy-start(bf16[1024,256]{1,0:T(8,128)(2,1)} %w_ref.1) | copy-start | bytes 1572868
  39.1 15.7 %all-to-all-start.1 = ((bf16[16,176,128]{2,1,0:T(8,128)(2,1)}), bf16[16,176,128]{2,1,0:T(8,128)(2,1)S(1)}, u32[]{:S(2)}, u32[]{:S(2)}) async-start(bf16[16,176,128]{2,1,0:T(8,128)(2,1)} %combine.1), calls=%async_computation.1 | async-start | bytes 1441792 | tf_op jit(solution)/shard_map/all_to_all | solution.py:255
  42.7 24.3 %copy-start.1 = (bf16[768,1024]{1,0:T(8,128)(2,1)S(1)}, bf16[768,1024]{1,0:T(8,128)(2,1)}, u32[]{:S(2)}) copy-start(bf16[768,1024]{1,0:T(8,128)(2,1)} %q_ref.3) | copy-start | bytes 4718596
  42.7 3.0 %collective-permute-start.2 = (bf16[1024,256]{1,0:T(8,128)(2,1)S(1)}, bf16[1024,256]{1,0:T(8,128)(2,1)S(1)}, u32[]{:S(2)}, u32[]{:S(2)}) collective-permute-start(bf16[1024,256]{1,0:T(8,128)(2,1)S(1)} %copy-done), channel_id=1, source_target_pairs={{0,8},{8,0},{1,9},{9,1},{2,10},{10,2},{3,11},{11,3},{4,12},{12,4},... | collective-permute-start | bytes 1572872 | tf_op jit(solution)/shard_map/ppermute | solution.py:251
  55.9 11.1 %collective-permute-start.3 = (bf16[768,128]{1,0:T(8,128)(2,1)S(1)}, bf16[768,128]{1,0:T(8,128)(2,1)S(1)}, u32[]{:S(2)}, u32[]{:S(2)}) collective-permute-start(bf16[768,128]{1,0:T(8,128)(2,1)S(1)} %get-tuple-element.4), channel_id=1, source_target_pairs={{0,8},{8,0},{1,9},{9,1},{2,10},{10,2},{3,11},{11,3},{4,12},{12,4},... | collective-permute-start | bytes 589832 | tf_op jit(solution)/shard_map/ppermute | solution.py:251
  58.4 30.7 %all-to-all-start.2 = ((bf16[16,32,256]{2,1,0:T(8,128)(2,1)}), bf16[16,32,256]{2,1,0:T(8,128)(2,1)S(1)}, u32[]{:S(2)}, u32[]{:S(2)}) async-start(bf16[16,32,256]{2,1,0:T(8,128)(2,1)} %get-tuple-element.5), calls=%async_computation.2 | async-start | bytes 524288 | tf_op jit(solution)/shard_map/all_to_all | solution.py:255
  67.0 0.9 %copy-start.4 = (bf16[768,128]{1,0:T(8,128)(2,1)S(1)}, bf16[768,128]{1,0:T(8,128)(2,1)}, u32[]{:S(2)}) copy-start(bf16[768,128]{1,0:T(8,128)(2,1)} %k_ref.3) | copy-start | bytes 589828
  68.0 0.9 %copy-start.6 = (bf16[768,128]{1,0:T(8,128)(2,1)S(1)}, bf16[768,128]{1,0:T(8,128)(2,1)}, u32[]{:S(2)}) copy-start(bf16[768,128]{1,0:T(8,128)(2,1)} %v_ref.3) | copy-start | bytes 589828

commit v2 on v1

v2 whole, which is shorter than its diff:
```python
import jax
import jax.numpy as jnp
from jax import lax
from jax.experimental import pallas as pl
from jax.experimental.pallas import tpu as pltpu
from jax.sharding import Mesh, PartitionSpec as P

HEAD = 128
BLOCK = 768
HEADS = 8
QROWS = 512
HALF = 256
SEND1 = HEAD + 16
QUERY_STEP = 4
OWN_STEP = 2
HIDDEN = 1e30
LOG2_SCALE = 1.4426950408889634 * HEAD ** (-0.5)
BF = jnp.bfloat16
F32 = jnp.float32


def scores_of(q, k):
    return lax.dot_general(q, k, (((1,), (1,)), ((), ())), preferred_element_type=F32)


def fill_values(values, row, v_ref):
    values[row : row + BLOCK, 0:HEAD] = v_ref[...]
    values[row : row + BLOCK, HEAD : 2 * HEAD] = jnp.ones((BLOCK, HEAD), BF)


def eye_mask():
    r = lax.broadcasted_iota(jnp.int32, (HEAD, HEAD), 0)
    c = lax.broadcasted_iota(jnp.int32, (HEAD, HEAD), 1)
    return r == c


def to_lanes(column):
    return jnp.sum(jnp.where(eye_mask(), column, 0.0), axis=0, keepdims=True)


def query_kernel(q_ref, k_ref, v_ref, kp_ref, vp_ref, out_ref, keys, values):
    core = lax.axis_index("c")

    @pl.when(pl.program_id(0) == 0)
    def _():
        keys[0:BLOCK, :] = k_ref[...]
        keys[BLOCK : 2 * BLOCK, :] = kp_ref[...]
        fill_values(values, 0, v_ref)
        fill_values(values, BLOCK, vp_ref)

    def scores(j):
        q = jnp.concatenate(
            [
                q_ref[pl.ds(pl.multiple_of(64 * z + 32 * core, 32), 32), HEAD * j : HEAD * j + HEAD]
                for z in range(8)
            ],
            axis=0,
        )
        return scores_of(q, keys[...])

    row_id = lax.broadcasted_iota(jnp.int32, (16, HEAD), 0)
    s = scores(0)
    for j in range(QUERY_STEP):
        s_next = scores(j + 1) if j + 1 < QUERY_STEP else None
        s = s * LOG2_SCALE
        peak = jnp.max(s, axis=1, keepdims=True).astype(BF).astype(F32)
        p = jnp.exp2(s - peak).astype(BF)
        acc = jnp.dot(p, values[...], preferred_element_type=F32)
        total = acc[:, HEAD : HEAD + 1]
        for half in range(2):
            rows = slice(half * HEAD, half * HEAD + HEAD)
            out_ref[2 * j + half, 0:HEAD, :] = acc[rows, 0:HEAD].astype(BF)
            peak_l = to_lanes(peak[rows])
            total_l = to_lanes(total[rows])
            high = total_l.astype(BF).astype(F32)
            stats = jnp.where(row_id == 0, peak_l, 0.0)
            stats = jnp.where(row_id == 1, high, stats)
            stats = jnp.where(row_id == 2, total_l - high, stats)
            out_ref[2 * j + half, HEAD:SEND1, :] = stats.astype(BF)
        s = s_next


def combine_kernel(in_ref, after_ref, out_ref):
    stats = in_ref[:, HEAD : HEAD + 16, :].astype(F32)
    peak = stats[:, 0, :]
    total = stats[:, 1, :] + stats[:, 2, :]
    top = jnp.max(peak, axis=0, keepdims=True)
    weight = jnp.exp2(peak - top)
    weight = weight / jnp.sum(weight * total, axis=0, keepdims=True)
    weight_t = jnp.concatenate([weight, jnp.zeros((HEAD - 16, HEAD), F32)], axis=0).T
    out = jnp.zeros((HEAD, HEAD), F32)
    for g in range(16):
        out = out + weight_t[:, g : g + 1] * in_ref[g, 0:HEAD, :].astype(F32)
    out = out.astype(BF)
    for g in range(16):
        out_ref[g] = out


def project_kernel(in_ref, w_ref, wp_ref, out_ref):
    core = lax.axis_index("c")
    a = jnp.concatenate(
        [
            jnp.concatenate([in_ref[2 * j + half] for j in range(HEADS)], axis=1)
            for half in range(2)
        ],
        axis=0,
    )
    for w, dest in ((w_ref, core), (wp_ref, 1 - core)):
        y = jnp.dot(a, w[...], preferred_element_type=F32).astype(BF)
        for z in range(8):
            out_ref[2 * z + dest] = y[32 * z : 32 * z + 32, :]


def final_kernel(in_ref, out_ref):
    for half in range(2):
        total = in_ref[half].astype(F32)
        for z in range(1, 8):
            total = total + in_ref[2 * z + half].astype(F32)
        out_ref[32 * half : 32 * half + 32, :] = total.astype(BF)


def own_kernel(q_ref, k_ref, v_ref, after_ref, acc_ref, stat_ref, values):
    step = pl.program_id(0)

    @pl.when(step == 0)
    def _():
        fill_values(values, 0, v_ref)
        stat_ref[...] = jnp.zeros((BLOCK, HEAD), F32)

    lane = lax.broadcasted_iota(jnp.int32, (HALF, HEAD), 1)
    r = lax.broadcasted_iota(jnp.int32, (HALF, HALF), 0)
    c = lax.broadcasted_iota(jnp.int32, (HALF, HALF), 1)
    blocks = [(j, i) for j in range(OWN_STEP) for i in range(3)]

    def scores(n):
        j, i = blocks[n]
        q = q_ref[i * HALF : (i + 1) * HALF, HEAD * j : HEAD * j + HEAD]
        return scores_of(q, k_ref[0 : (i + 1) * HALF, :])

    s = scores(0)
    for n in range(len(blocks)):
        j, i = blocks[n]
        s_next = scores(n + 1) if n + 1 < len(blocks) else None
        s = s * LOG2_SCALE
        diagonal = jnp.where(c <= r, s[:, i * HALF :], -HIDDEN)
        s = jnp.concatenate([s[:, 0 : i * HALF], diagonal], axis=1) if i else diagonal
        peak = jnp.max(s, axis=1, keepdims=True)
        p = jnp.exp2(s - peak).astype(BF)
        acc = jnp.dot(p, values[0 : (i + 1) * HALF, :], preferred_element_type=F32)
        rows = slice(i * HALF, (i + 1) * HALF)
        acc_ref[rows, HEAD * j : HEAD * j + HEAD] = acc[:, 0:HEAD]
        head = step * OWN_STEP + j
        stat = jnp.where(lane == head, peak, stat_ref[rows, :])
        stat_ref[rows, :] = jnp.where(lane == HEADS + head, acc[:, HEAD : 2 * HEAD], stat)
        s = s_next


def anchor_kernel(q_ref, k_ref, v_ref, acc_ref, stat_ref, out_ref, values):
    step = pl.program_id(0)

    @pl.when(step == 0)
    def _():
        fill_values(values, 0, v_ref)

    first = jnp.logical_and(
        lax.axis_index("c") == 0,
        jnp.logical_and(lax.axis_index("x") == 0, lax.axis_index("y") == 0),
    )
    lane = lax.broadcasted_iota(jnp.int32, (HALF, HEAD), 1)
    blocks = [(j, i) for j in range(OWN_STEP) for i in range(3)]

    def scores(n):
        j, i = blocks[n]
        q = q_ref[i * HALF : (i + 1) * HALF, HEAD * j : HEAD * j + HEAD]
        return scores_of(q, k_ref[...])

    s = scores(0)
    for n in range(len(blocks)):
        j, i = blocks[n]
        s_next = scores(n + 1) if n + 1 < len(blocks) else None
        s = s * LOG2_SCALE
        rows = slice(i * HALF, (i + 1) * HALF)
        stat = stat_ref[rows, :]
        head = step * OWN_STEP + j
        own_peak = jnp.sum(jnp.where(lane == head, stat, 0.0), axis=1, keepdims=True)
        own_total = jnp.sum(jnp.where(lane == HEADS + head, stat, 0.0), axis=1, keepdims=True)
        peak = jnp.maximum(own_peak, jnp.max(s, axis=1, keepdims=True))
        peak = jnp.where(first, own_peak, peak)
        shift = jnp.where(first, HIDDEN, peak)
        p = jnp.exp2(s - shift).astype(BF)
        acc = jnp.dot(p, values[...], preferred_element_type=F32)
        scale = jnp.exp2(own_peak - peak)
        total = acc[:, HEAD : 2 * HEAD] + scale * own_total
        mixture = acc[:, 0:HEAD] + scale * acc_ref[rows, HEAD * j : HEAD * j + HEAD]
        out_ref[rows, HEAD * j : HEAD * j + HEAD] = (mixture / total).astype(BF)
        s = s_next


def whole(shape):
    return pl.BlockSpec(shape, lambda *_: (0,) * len(shape))


def params(limit=24):
    return pltpu.CompilerParams(vmem_limit_bytes=limit * 1024 * 1024)


def cost(flops, nbytes, exps=0):
    return pl.CostEstimate(flops=flops, bytes_accessed=nbytes, transcendentals=exps)


def query_call(query, k, v, kp, vp):
    return pl.pallas_call(
        query_kernel,
        grid=(HEADS // QUERY_STEP,),
        in_specs=[pl.BlockSpec((QROWS, QUERY_STEP * HEAD), lambda j: (0, j))]
        + [whole((BLOCK, HEAD))] * 4,
        out_specs=pl.BlockSpec((2 * QUERY_STEP, SEND1, HEAD), lambda j: (j, 0, 0)),
        out_shape=jax.ShapeDtypeStruct((16, SEND1, HEAD), BF),
        scratch_shapes=[pltpu.VMEM((2 * BLOCK, HEAD), BF), pltpu.VMEM((2 * BLOCK, 2 * HEAD), BF)],
        compiler_params=params(56),
        cost_estimate=cost(4 * 2048 * 1536 * 256, 3 << 20, 2048 * 1536),
        name="query_attention",
    )(query, k, v, kp, vp)


def own_call(ctx_query, k, v, after):
    wide = OWN_STEP * HEAD
    return pl.pallas_call(
        own_kernel,
        grid=(HEADS // OWN_STEP,),
        in_specs=[pl.BlockSpec((BLOCK, wide), lambda j: (0, j))]
        + [whole((BLOCK, HEAD))] * 2
        + [pl.BlockSpec(memory_space=pl.ANY)],
        out_specs=(pl.BlockSpec((BLOCK, wide), lambda j: (0, j)), whole((BLOCK, HEAD))),
        out_shape=(
            jax.ShapeDtypeStruct((BLOCK, HEADS * HEAD), F32),
            jax.ShapeDtypeStruct((BLOCK, HEAD), F32),
        ),
        scratch_shapes=[pltpu.VMEM((BLOCK, 2 * HEAD), BF)],
        compiler_params=params(),
        cost_estimate=cost(4 * 6144 * 512 * 256, 4 << 20, 6144 * 512),
        name="context_own",
    )(ctx_query, k, v, after)


def anchor_call(ctx_query, ka, va, acc, stat):
    wide = OWN_STEP * HEAD
    return pl.pallas_call(
        anchor_kernel,
        grid=(HEADS // OWN_STEP,),
        in_specs=[pl.BlockSpec((BLOCK, wide), lambda j: (0, j))]
        + [whole((BLOCK, HEAD))] * 2
        + [pl.BlockSpec((BLOCK, wide), lambda j: (0, j)), whole((BLOCK, HEAD))],
        out_specs=pl.BlockSpec((BLOCK, wide), lambda j: (0, j)),
        out_shape=jax.ShapeDtypeStruct((BLOCK, HEADS * HEAD), BF),
        scratch_shapes=[pltpu.VMEM((BLOCK, 2 * HEAD), BF)],
        compiler_params=params(),
        cost_estimate=cost(4 * 6144 * 768 * 256, 6 << 20, 6144 * 768),
        name="context_anchor",
    )(ctx_query, ka, va, acc, stat)


def combine_call(received, after):
    return pl.pallas_call(
        combine_kernel,
        out_shape=jax.ShapeDtypeStruct((16, HEAD, HEAD), BF),
        in_specs=[pl.BlockSpec(memory_space=pltpu.VMEM), pl.BlockSpec(memory_space=pl.ANY)],
        out_specs=pl.BlockSpec(memory_space=pltpu.VMEM),
        compiler_params=params(),
        cost_estimate=cost(1 << 20, 3 << 19),
        name="combine",
    )(received, after)


def project_call(gathered, w, wp):
    return pl.pallas_call(
        project_kernel,
        out_shape=jax.ShapeDtypeStruct((16, 32, 256), BF),
        in_specs=[pl.BlockSpec(memory_space=pltpu.VMEM)] * 3,
        out_specs=pl.BlockSpec(memory_space=pltpu.VMEM),
        compiler_params=params(),
        cost_estimate=cost(2 * 256 * 1024 * 512, 2 << 20),
        name="project",
    )(gathered, w, wp)


def final_call(received):
    return pl.pallas_call(
        final_kernel,
        out_shape=jax.ShapeDtypeStruct((64, 256), BF),
        in_specs=[pl.BlockSpec(memory_space=pltpu.VMEM)],
        out_specs=pl.BlockSpec(memory_space=pltpu.VMEM),
        compiler_params=params(),
        cost_estimate=cost(1 << 17, 1 << 18),
        name="final_sum",
    )(received)


def swap(value):
    return lax.ppermute(value, "c", [(0, 1), (1, 0)])


def exchange(value, axes):
    return lax.all_to_all(value, axes, 0, 0, tiled=True)


def chip_copy(value, source, target):
    return lax.ppermute(value, ("y", "x"), [(4 * a + b, 4 * c + d) for (a, b), (c, d) in zip(source, target)])


def per_device(ctx_query, context_key, context_value, query, out_weight):
    core, x, y = (lax.axis_index(name) for name in ("c", "x", "y"))
    key_p, value_p = swap(context_key), swap(context_value)
    piece = jnp.where(core == 0, context_key, value_p)
    along_x = [chip_copy(piece, [(0, 0)], [(0, k)]) for k in (1, 2, 3)]
    weight_p = swap(out_weight)
    sent = query_call(query, context_key, context_value, key_p, value_p)
    received = exchange(sent, ("y", "x"))
    acc, stat = own_call(ctx_query, context_key, context_value, sent)
    row = jnp.where(x == 0, piece, jnp.where(x == 1, along_x[0], jnp.where(x == 2, along_x[1], along_x[2])))
    along_y = [chip_copy(row, [(0, j) for j in range(4)], [(k, j) for j in range(4)]) for k in (1, 2, 3)]
    gathered = exchange(combine_call(received, stat), ("y", "x"))
    half = jnp.where(y == 0, row, jnp.where(y == 1, along_y[0], jnp.where(y == 2, along_y[1], along_y[2])))
    other = swap(half)
    key_a = jnp.where(core == 0, half, other)
    value_a = jnp.where(core == 0, other, half)
    shares = project_call(gathered, out_weight, weight_p)
    ctx_out = anchor_call(ctx_query, key_a, value_a, acc, stat)
    answer = final_call(exchange(shares, ("z", "c")))
    return ctx_out, answer


def solution(mesh):
    fine = Mesh(mesh.devices.reshape(4, 4, 2, 8), ("y", "x", "c", "z"))
    hst = ("y", "x", "c")
    in_specs = (P(hst, "z"), P(hst, "z"), P(hst, "z"), P(None, "z"), P("z", hst))
    out_specs = (P(hst, "z"), P("z", hst))
    return jax.shard_map(
        per_device, mesh=fine, in_specs=in_specs, out_specs=out_specs, check_vma=False
    )
```

time: 90.2 us -> 83.5 us (0.926)
  blocking collectives: 18.7 us -> 0 us
  starting transfers between devices: 19.6 us -> 37.5 us
  Pallas kernels: 33.6 us -> 25.2 us
  local copies, waits for them, and re-layouts: 4.94 us -> 7.02 us
  other arithmetic: 0.03 us -> 2.01 us
  waiting for transfers between devices: 12.1 us -> 10.3 us
    all_to_all x1 -> x0, blocking collectives: 18.7 us -> none  [exchange(): return lax.all_to_all(value, axes, 0, 0, tiled=True)]
    ppermute x0 -> x6, starting transfers between devices: none -> 14 us  [chip_copy(): lax.ppermute(value, ('y', 'x'), [(4 * a + b, 4 * c + d) for (a, b), (c, d...]
    pallas_call x4 -> x5, Pallas kernels: 33 us -> 24.6 us  [the longest x1 9.09 us: anchor_call(): pl.pallas_call(anchor_kernel, grid=(HEADS // OWN_STEP,), in_specs=[pl.Blo...]
    all_to_all x2 -> x3, starting transfers between devices: 12.2 us -> 17.7 us  [exchange(): return lax.all_to_all(value, axes, 0, 0, tiled=True)]
    unnamed x14 -> x20, local copies, waits for them, and re-layouts: 4.94 us -> 7.02 us
    select_n x1 -> x4, other arithmetic: 0.03 us -> 2.01 us  [the longest x1 0.98 us: per_device(): jnp.where(y == 0, row, jnp.where(y == 1, along_y[0], jnp.where(y == 2, al...]
    ppermute x4, waiting for transfers between devices: 3.09 us -> 1.19 us  [swap(): return lax.ppermute(value, 'c', [(0, 1), (1, 0)])]
    ppermute x4, starting transfers between devices: 7.39 us -> 5.84 us  [swap(): return lax.ppermute(value, 'c', [(0, 1), (1, 0)])]
  transfers between devices with their start and end apart: 6 -> 13, of which waited for: 4 -> 2; matrix products, arithmetic and copies ran while one was open for 0% -> 2% of each run, Pallas kernels for 22% -> 30%
where the time goes in v2:
time: 83.5 us; the launch traced here: 82.8 us
  starting transfers between devices  37.5 us (45%)
  Pallas kernels  25.2 us (30%)
  waiting for transfers between devices  10.3 us (12%)
  local copies, waits for them, and re-layouts  7.02 us (8%)
  other arithmetic  2.01 us (2%)
    all_to_all x3, starting transfers between devices, exchange(): return lax.all_to_all(value, axes, 0, 0, tiled=True)  17.7 us
    ppermute x6, starting transfers between devices, chip_copy(): lax.ppermute(value, ('y', 'x'), [(4 * a + b, 4 * c + d) for (a, b), (c, d...  14 us
    pallas_call x1, Pallas kernels, anchor_call(): pl.pallas_call(anchor_kernel, grid=(HEADS // OWN_STEP,), in_specs=[pl.Blo...  9.09 us
    all_to_all x3, waiting for transfers between devices, exchange(): return lax.all_to_all(value, axes, 0, 0, tiled=True)  9.08 us
    unnamed x20, local copies, waits for them, and re-layouts  7.02 us
    pallas_call x1, Pallas kernels, query_call(): pl.pallas_call(query_kernel, grid=(HEADS // QUERY_STEP,), in_specs=[pl.Bl...  6.77 us
    pallas_call x1, Pallas kernels, own_call(): pl.pallas_call(own_kernel, grid=(HEADS // OWN_STEP,), in_specs=[pl.BlockS...  6.18 us
    ppermute x4, starting transfers between devices, swap(): return lax.ppermute(value, 'c', [(0, 1), (1, 0)])  5.84 us
  transfers between devices with their start and end apart: 13, of which 2 were waited for; matrix products, arithmetic and copies ran while one was open for 2% of the time, Pallas kernels for 30%

profile of v2, /device:TPU:1, one launch (start us, length us, event | category | flops | bytes accessed | tf_op | source)
XLA Modules:
  0.0 82.8 jit_solution(3591608026398370549)
XLA Ops:
  0.6 3.3 %collective-permute-start = (bf16[768,128]{1,0:T(8,128)(2,1)}, bf16[768,128]{1,0:T(8,128)(2,1)S(1)}, u32[]{:S(2)}, u32[]{:S(2)}) collective-permute-start(bf16[768,128]{1,0:T(8,128)(2,1)} %v_ref.3), channel_id=1, source_target_pairs={{0,8},{8,0},{1,9},{9,1},{2,10},{10,2},{3,11},{11,3},{4,12},{12,4},... | collective-permute-start | bytes 589832 | tf_op jit(solution)/shard_map/ppermute | solution.py:300
  4.0 0.1 collective-permute-start.8
  4.1 1.2 %collective-permute-done.vp_ref = bf16[768,128]{1,0:T(8,128)(2,1)S(1)} collective-permute-done((bf16[768,128]{1,0:T(8,128)(2,1)}, bf16[768,128]{1,0:T(8,128)(2,1)S(1)}, u32[]{:S(2)}, u32[]{:S(2)}) %collective-permute-start) | collective-permute-done | bytes 196640 | tf_op jit(solution)/shard_map/ppermute | solution.py:300
  5.2 0.0 copy-start.8
  5.3 0.0 copy-start.1
  5.3 1.5 %collective-permute-start.1 = (bf16[768,128]{1,0:T(8,128)(2,1)S(1)}, bf16[768,128]{1,0:T(8,128)(2,1)S(1)}, u32[]{:S(2)}, u32[]{:S(2)}) collective-permute-start(bf16[768,128]{1,0:T(8,128)(2,1)S(1)} %broadcast_select_fusion.2), channel_id=1, source_target_pairs={{0,16},{1,17},{2,18},{3,19},{4,20},{5,21},{6,22},{7,23},{8,24},{9,... | collective-permute-start | bytes 589832 | tf_op jit(solution)/shard_map/ppermute | solution.py:308
  6.8 2.2 %collective-permute-start.2 = (bf16[768,128]{1,0:T(8,128)(2,1)S(1)}, bf16[768,128]{1,0:T(8,128)(2,1)S(1)}, u32[]{:S(2)}, u32[]{:S(2)}) collective-permute-start(bf16[768,128]{1,0:T(8,128)(2,1)S(1)} %broadcast_select_fusion.2), channel_id=1, source_target_pairs={{0,32},{1,33},{2,34},{3,35},{4,36},{5,37},{6,38},{7,39},{8,40},{9,... | collective-permute-start | bytes 589832 | tf_op jit(solution)/shard_map/ppermute | solution.py:308
  9.0 2.0 %collective-permute-start.3 = (bf16[768,128]{1,0:T(8,128)(2,1)S(1)}, bf16[768,128]{1,0:T(8,128)(2,1)}, u32[]{:S(2)}, u32[]{:S(2)}) collective-permute-start(bf16[768,128]{1,0:T(8,128)(2,1)S(1)} %broadcast_select_fusion.2), channel_id=1, source_target_pairs={{0,48},{1,49},{2,50},{3,51},{4,52},{5,53},{6,54},{7,55},{8,56},{9,... | collective-permute-start | bytes 589832 | tf_op jit(solution)/shard_map/ppermute | solution.py:308
  11.0 0.0 collective-permute-done.8.kp_ref
  11.0 0.0 copy-done.8
  11.0 0.7 copy-done.9
  11.7 6.8 %query_attention.1.after_ref = bf16[16,144,128]{2,1,0:T(8,128)(2,1)} custom-call(bf16[512,1024]{1,0:T(8,128)(2,1)} %q_ref.3, bf16[768,128]{1,0:T(8,128)(2,1)} %k_ref.3, bf16[768,128]{1,0:T(8,128)(2,1)} %v_ref.3, bf16[768,128]{1,0:T(8,128)(2,1)} %copy-done.9, bf16[768,128]{1,0:T(8,128)(2,1)} %copy-done.8), custom_call_target="tpu_custom_call" | custom-call | flops 3221225472 | bytes 3145728 | tf_op jit(solution)/shard_map/query_attention/pallas_call | solution.py:212
  18.5 3.7 %all-to-all-start = ((bf16[16,144,128]{2,1,0:T(8,128)(2,1)}), bf16[16,144,128]{2,1,0:T(8,128)(2,1)S(1)}, u32[]{:S(2)}, u32[]{:S(2)}) async-start(bf16[16,144,128]{2,1,0:T(8,128)(2,1)} %query_attention.1.after_ref), calls=%async_computation | async-start | bytes 1179648 | tf_op jit(solution)/shard_map/all_to_all | solution.py:304
  22.2 0.0 copy-done.1
  22.2 1.7 %collective-permute-start.9 = (bf16[1024,256]{1,0:T(8,128)(2,1)S(1)}, bf16[1024,256]{1,0:T(8,128)(2,1)S(1)}, u32[]{:S(2)}, u32[]{:S(2)}) collective-permute-start(bf16[1024,256]{1,0:T(8,128)(2,1)S(1)} %copy-done.1), channel_id=1, source_target_pairs={{0,8},{8,0},{1,9},{9,1},{2,10},{10,2},{3,11},{11,3},{4,12},{12,4},... | collective-permute-start | bytes 1572872 | tf_op jit(solution)/shard_map/ppermute | solution.py:300
  23.9 0.0 collective-permute-done.1
  23.9 0.0 collective-permute-done.2
  24.0 0.0 collective-permute-done.3
  24.0 1.0 %select_select_fusion.1 = bf16[768,128]{1,0:T(8,128)(2,1)S(1)} fusion(bf16[768,128]{1,0:T(8,128)(2,1)S(1)} %broadcast_select_fusion.2, bf16[768,128]{1,0:T(8,128)(2,1)S(1)} %collective-permute-done.1, bf16[768,128]{1,0:T(8,128)(2,1)S(1)} %collective-permute-done.2, bf16[768,128]{1,0:T(8,128)(2,1)} %collective-permute-done.3, pred[]{:T(512)S(6)} %eq.27, ...), kind=kLoop, calls=%fused_computation.1 | loop fusion | flops 294912 | bytes 983043 | tf_op jit(solution)/shard_map/jit(_where)/select_n | solution.py:320
  24.9 3.5 %collective-permute-start.4 = (bf16[768,128]{1,0:T(8,128)(2,1)S(1)}, bf16[768,128]{1,0:T(8,128)(2,1)S(1)}, u32[]{:S(2)}, u32[]{:S(2)}) collective-permute-start(bf16[768,128]{1,0:T(8,128)(2,1)S(1)} %select_select_fusion.1), channel_id=1, source_target_pairs={{0,64},{16,80},{32,96},{48,112},{1,65},{17,81},{33,97},{49,113},{2... | collective-permute-start | bytes 589832 | tf_op jit(solution)/shard_map/ppermute | solution.py:308
  28.4 2.9 %collective-permute-start.5 = (bf16[768,128]{1,0:T(8,128)(2,1)S(1)}, bf16[768,128]{1,0:T(8,128)(2,1)}, u32[]{:S(2)}, u32[]{:S(2)}) collective-permute-start(bf16[768,128]{1,0:T(8,128)(2,1)S(1)} %select_select_fusion.1), channel_id=1, source_target_pairs={{0,128},{16,144},{32,160},{48,176},{1,129},{17,145},{33,161},{49,1... | collective-permute-start | bytes 589832 | tf_op jit(solution)/shard_map/ppermute | solution.py:308
  31.3 2.0 %collective-permute-start.6 = (bf16[768,128]{1,0:T(8,128)(2,1)S(1)}, bf16[768,128]{1,0:T(8,128)(2,1)}, u32[]{:S(2)}, u32[]{:S(2)}) collective-permute-start(bf16[768,128]{1,0:T(8,128)(2,1)S(1)} %select_select_fusion.1), channel_id=1, source_target_pairs={{0,192},{16,208},{32,224},{48,240},{1,193},{17,209},{33,225},{49,2... | collective-permute-start | bytes 589832 | tf_op jit(solution)/shard_map/ppermute | solution.py:308
  33.2 0.0 copy-done
  33.2 0.0 copy-done.2
  33.2 0.0 copy-done.5
  33.2 1.4 %copy-done.3 = bf16[768,1024]{1,0:T(8,128)(2,1)S(1)} copy-done((bf16[768,1024]{1,0:T(8,128)(2,1)S(1)}, bf16[768,1024]{1,0:T(8,128)(2,1)}, u32[]{:S(2)}) %copy-start.3) | copy-done | bytes 1572888
  34.6 6.2 %context_own.1 = (f32[768,1024]{1,0:T(8,128)S(1)}, f32[768,128]{1,0:T(8,128)S(1)}) custom-call(bf16[768,1024]{1,0:T(8,128)(2,1)S(1)} %copy-done.3, bf16[768,128]{1,0:T(8,128)(2,1)S(1)} %copy-done.2, bf16[768,128]{1,0:T(8,128)(2,1)S(1)} %copy-done.5, bf16[16,144,128]{2,1,0:T(8,128)(2,1)S(1)} %copy-done), custom_call_target="tpu_custom_call" | custom-call | flops 3221225472 | bytes 4194304 | tf_op jit(solution)/shard_map/context_own/pallas_call | solution.py:228
  40.8 0.0 copy-start.6
  40.8 1.6 %copy-done.6 = f32[768,1024]{1,0:T(8,128)} copy-done((f32[768,1024]{1,0:T(8,128)}, f32[768,1024]{1,0:T(8,128)S(1)}, u32[]{:S(2)}) %copy-start.6) | copy-done | bytes 3145752
  42.5 0.0 all-to-all-done.in_ref
  42.5 1.4 %combine.1 = bf16[16,128,128]{2,1,0:T(8,128)(2,1)} custom-call(bf16[16,144,128]{2,1,0:T(8,128)(2,1)S(1)} %all-to-all-done.in_ref, f32[768,128]{1,0:T(8,128)S(1)} %get-tuple-element.5.stat_ref.after_ref), custom_call_target="tpu_custom_call" | custom-call | flops 1048576 | bytes 1572864 | tf_op jit(solution)/shard_map/combine/pallas_call | solution.py:264
  43.8 3.8 %all-to-all-start.1 = ((bf16[16,128,128]{2,1,0:T(8,128)(2,1)}), bf16[16,128,128]{2,1,0:T(8,128)(2,1)S(1)}, u32[]{:S(2)}, u32[]{:S(2)}) async-start(bf16[16,128,128]{2,1,0:T(8,128)(2,1)} %combine.1), calls=%async_computation.1 | async-start | bytes 1048576 | tf_op jit(solution)/shard_map/all_to_all | solution.py:304
  47.6 0.0 collective-permute-done.4
  47.6 0.0 collective-permute-done.5
  47.7 0.0 collective-permute-done.6
  47.7 1.0 %select_select_fusion = bf16[768,128]{1,0:T(8,128)(2,1)S(1)} fusion(bf16[768,128]{1,0:T(8,128)(2,1)S(1)} %select_select_fusion.1, bf16[768,128]{1,0:T(8,128)(2,1)S(1)} %collective-permute-done.4, bf16[768,128]{1,0:T(8,128)(2,1)} %collective-permute-done.5, bf16[768,128]{1,0:T(8,128)(2,1)} %collective-permute-done.6, pred[]{:T(512)S(6)} %eq.29, pred[]{:T(512)S(6)} %eq.28, ...), kind=kLoop, calls=%fused_computation | loop fusion | flops 294912 | bytes 983043 | tf_op jit(solution)/shard_map/jit(_where)/select_n | solution.py:323
  48.6 0.7 collective-permute-start.7
  49.3 0.0 collective-permute-done.9.wp_ref
  49.3 9.1 %all-to-all-done.1.in_ref = bf16[16,128,128]{2,1,0:T(8,128)(2,1)S(1)} async-done(((bf16[16,128,128]{2,1,0:T(8,128)(2,1)}), bf16[16,128,128]{2,1,0:T(8,128)(2,1)S(1)}, u32[]{:S(2)}, u32[]{:S(2)}) %all-to-all-start.1) | async-done | bytes 524320 | tf_op jit(solution)/shard_map/all_to_all | solution.py:304
  58.4 1.2 %project.1 = bf16[16,32,256]{2,1,0:T(8,128)(2,1)} custom-call(bf16[16,128,128]{2,1,0:T(8,128)(2,1)S(1)} %all-to-all-done.1.in_ref, bf16[1024,256]{1,0:T(8,128)(2,1)S(1)} %copy-done.1, bf16[1024,256]{1,0:T(8,128)(2,1)S(1)} %collective-permute-done.9.wp_ref), custom_call_target="tpu_custom_call" | custom-call | flops 268435456 | bytes 2097152 | tf_op jit(solution)/shard_map/project/pallas_call | solution.py:276
  59.6 10.2 %all-to-all-start.2 = ((bf16[16,32,256]{2,1,0:T(8,128)(2,1)}), bf16[16,32,256]{2,1,0:T(8,128)(2,1)S(1)}, u32[]{:S(2)}, u32[]{:S(2)}) async-start(bf16[16,32,256]{2,1,0:T(8,128)(2,1)} %project.1), calls=%async_computation.2 | async-start | bytes 524288 | tf_op jit(solution)/shard_map/all_to_all | solution.py:304
  69.7 0.0 collective-permute-done.7
  69.8 0.0 copy-start.4
  69.8 1.4 %copy-done.4 = bf16[768,1024]{1,0:T(8,128)(2,1)S(1)} copy-done((bf16[768,1024]{1,0:T(8,128)(2,1)S(1)}, bf16[768,1024]{1,0:T(8,128)(2,1)}, u32[]{:S(2)}) %copy-start.4) | copy-done | bytes 1572888
  71.2 1.9 %copy-done.7 = f32[768,1024]{1,0:T(8,128)S(1)} copy-done((f32[768,1024]{1,0:T(8,128)S(1)}, f32[768,1024]{1,0:T(8,128)}, u32[]{:S(2)}) %copy-start.7) | copy-done | bytes 3145752
  73.1 9.1 %context_anchor.1 = bf16[768,1024]{1,0:T(8,128)(2,1)} custom-call(bf16[768,1024]{1,0:T(8,128)(2,1)S(1)} %copy-done.4, bf16[768,128]{1,0:T(8,128)(2,1)S(1)} %get-tuple-element.7.k_ref, bf16[768,128]{1,0:T(8,128)(2,1)S(1)} %get-tuple-element.6.v_ref, f32[768,1024]{1,0:T(8,128)S(1)} %copy-done.7, f32[768,128]{1,0:T(8,128)S(1)} %get-tuple-element.5.stat_ref.after_ref), custom_call_target="tpu_custom_call" | custom-call | flops 4831838208 | bytes 6291456 | tf_op jit(solution)/shard_map/context_anchor/pallas_call | solution.py:248
  82.2 0.0 all-to-all-done.2.in_ref
  82.2 0.7 final_sum.1
  (8 shorter events, 0.1 us)
Async XLA Ops:
  0.6 4.6 %collective-permute-start = (bf16[768,128]{1,0:T(8,128)(2,1)}, bf16[768,128]{1,0:T(8,128)(2,1)S(1)}, u32[]{:S(2)}, u32[]{:S(2)}) collective-permute-start(bf16[768,128]{1,0:T(8,128)(2,1)} %v_ref.3), channel_id=1, source_target_pairs={{0,8},{8,0},{1,9},{9,1},{2,10},{10,2},{3,11},{11,3},{4,12},{12,4},... | collective-permute-start | bytes 589832 | tf_op jit(solution)/shard_map/ppermute | solution.py:300
  4.0 7.0 %collective-permute-start.8 = (bf16[768,128]{1,0:T(8,128)(2,1)}, bf16[768,128]{1,0:T(8,128)(2,1)S(1)}, u32[]{:S(2)}, u32[]{:S(2)}) collective-permute-start(bf16[768,128]{1,0:T(8,128)(2,1)} %k_ref.3), channel_id=1, source_target_pairs={{0,8},{8,0},{1,9},{9,1},{2,10},{10,2},{3,11},{11,3},{4,12},{12,4},... | collective-permute-start | bytes 589832 | tf_op jit(solution)/shard_map/ppermute | solution.py:300
  5.2 5.8 %copy-start.8 = (bf16[768,128]{1,0:T(8,128)(2,1)}, bf16[768,128]{1,0:T(8,128)(2,1)S(1)}, u32[]{:S(2)}) copy-start(bf16[768,128]{1,0:T(8,128)(2,1)S(1)} %collective-permute-done.vp_ref) | copy-start | bytes 589828
  5.3 16.9 %copy-start.1 = (bf16[1024,256]{1,0:T(8,128)(2,1)S(1)}, bf16[1024,256]{1,0:T(8,128)(2,1)}, u32[]{:S(2)}) copy-start(bf16[1024,256]{1,0:T(8,128)(2,1)} %w_ref.1) | copy-start | bytes 1572868
  5.3 18.7 %collective-permute-start.1 = (bf16[768,128]{1,0:T(8,128)(2,1)S(1)}, bf16[768,128]{1,0:T(8,128)(2,1)S(1)}, u32[]{:S(2)}, u32[]{:S(2)}) collective-permute-start(bf16[768,128]{1,0:T(8,128)(2,1)S(1)} %broadcast_select_fusion.2), channel_id=1, source_target_pairs={{0,16},{1,17},{2,18},{3,19},{4,20},{5,21},{6,22},{7,23},{8,24},{9,... | collective-permute-start | bytes 589832 | tf_op jit(solution)/shard_map/ppermute | solution.py:308
  6.8 17.1 %collective-permute-start.2 = (bf16[768,128]{1,0:T(8,128)(2,1)S(1)}, bf16[768,128]{1,0:T(8,128)(2,1)S(1)}, u32[]{:S(2)}, u32[]{:S(2)}) collective-permute-start(bf16[768,128]{1,0:T(8,128)(2,1)S(1)} %broadcast_select_fusion.2), channel_id=1, source_target_pairs={{0,32},{1,33},{2,34},{3,35},{4,36},{5,37},{6,38},{7,39},{8,40},{9,... | collective-permute-start | bytes 589832 | tf_op jit(solution)/shard_map/ppermute | solution.py:308
  9.0 14.9 %collective-permute-start.3 = (bf16[768,128]{1,0:T(8,128)(2,1)S(1)}, bf16[768,128]{1,0:T(8,128)(2,1)}, u32[]{:S(2)}, u32[]{:S(2)}) collective-permute-start(bf16[768,128]{1,0:T(8,128)(2,1)S(1)} %broadcast_select_fusion.2), channel_id=1, source_target_pairs={{0,48},{1,49},{2,50},{3,51},{4,52},{5,53},{6,54},{7,55},{8,56},{9,... | collective-permute-start | bytes 589832 | tf_op jit(solution)/shard_map/ppermute | solution.py:308
  11.0 0.7 copy-start.9
  18.5 14.8 %copy-start = (bf16[16,144,128]{2,1,0:T(8,128)(2,1)S(1)}, bf16[16,144,128]{2,1,0:T(8,128)(2,1)}, u32[]{:S(2)}) copy-start(bf16[16,144,128]{2,1,0:T(8,128)(2,1)} %query_attention.1.after_ref) | copy-start | bytes 1769476
  18.5 14.8 %copy-start.2 = (bf16[768,128]{1,0:T(8,128)(2,1)S(1)}, bf16[768,128]{1,0:T(8,128)(2,1)}, u32[]{:S(2)}) copy-start(bf16[768,128]{1,0:T(8,128)(2,1)} %k_ref.3) | copy-start | bytes 589828
  18.5 14.8 %copy-start.5 = (bf16[768,128]{1,0:T(8,128)(2,1)S(1)}, bf16[768,128]{1,0:T(8,128)(2,1)}, u32[]{:S(2)}) copy-start(bf16[768,128]{1,0:T(8,128)(2,1)} %v_ref.3) | copy-start | bytes 589828
  18.5 24.0 %all-to-all-start = ((bf16[16,144,128]{2,1,0:T(8,128)(2,1)}), bf16[16,144,128]{2,1,0:T(8,128)(2,1)S(1)}, u32[]{:S(2)}, u32[]{:S(2)}) async-start(bf16[16,144,128]{2,1,0:T(8,128)(2,1)} %query_attention.1.after_ref), calls=%async_computation | async-start | bytes 1179648 | tf_op jit(solution)/shard_map/all_to_all | solution.py:304
  22.2 27.1 %collective-permute-start.9 = (bf16[1024,256]{1,0:T(8,128)(2,1)S(1)}, bf16[1024,256]{1,0:T(8,128)(2,1)S(1)}, u32[]{:S(2)}, u32[]{:S(2)}) collective-permute-start(bf16[1024,256]{1,0:T(8,128)(2,1)S(1)} %copy-done.1), channel_id=1, source_target_pairs={{0,8},{8,0},{1,9},{9,1},{2,10},{10,2},{3,11},{11,3},{4,12},{12,4},... | collective-permute-start | bytes 1572872 | tf_op jit(solution)/shard_map/ppermute | solution.py:300
  24.9 22.7 %collective-permute-start.4 = (bf16[768,128]{1,0:T(8,128)(2,1)S(1)}, bf16[768,128]{1,0:T(8,128)(2,1)S(1)}, u32[]{:S(2)}, u32[]{:S(2)}) collective-permute-start(bf16[768,128]{1,0:T(8,128)(2,1)S(1)} %select_select_fusion.1), channel_id=1, source_target_pairs={{0,64},{16,80},{32,96},{48,112},{1,65},{17,81},{33,97},{49,113},{2... | collective-permute-start | bytes 589832 | tf_op jit(solution)/shard_map/ppermute | solution.py:308
  28.4 19.2 %collective-permute-start.5 = (bf16[768,128]{1,0:T(8,128)(2,1)S(1)}, bf16[768,128]{1,0:T(8,128)(2,1)}, u32[]{:S(2)}, u32[]{:S(2)}) collective-permute-start(bf16[768,128]{1,0:T(8,128)(2,1)S(1)} %select_select_fusion.1), channel_id=1, source_target_pairs={{0,128},{16,144},{32,160},{48,176},{1,129},{17,145},{33,161},{49,1... | collective-permute-start | bytes 589832 | tf_op jit(solution)/shard_map/ppermute | solution.py:308
  31.3 16.4 %collective-permute-start.6 = (bf16[768,128]{1,0:T(8,128)(2,1)S(1)}, bf16[768,128]{1,0:T(8,128)(2,1)}, u32[]{:S(2)}, u32[]{:S(2)}) collective-permute-start(bf16[768,128]{1,0:T(8,128)(2,1)S(1)} %select_select_fusion.1), channel_id=1, source_target_pairs={{0,192},{16,208},{32,224},{48,240},{1,193},{17,209},{33,225},{49,2... | collective-permute-start | bytes 589832 | tf_op jit(solution)/shard_map/ppermute | solution.py:308
  33.2 1.4 %copy-start.3 = (bf16[768,1024]{1,0:T(8,128)(2,1)S(1)}, bf16[768,1024]{1,0:T(8,128)(2,1)}, u32[]{:S(2)}) copy-start(bf16[768,1024]{1,0:T(8,128)(2,1)} %q_ref.5) | copy-start | bytes 4718596
  40.8 1.6 %copy-start.6 = (f32[768,1024]{1,0:T(8,128)}, f32[768,1024]{1,0:T(8,128)S(1)}, u32[]{:S(2)}) copy-start(f32[768,1024]{1,0:T(8,128)S(1)} %get-tuple-element.4.acc_ref) | copy-start | bytes 9437188
  43.8 14.6 %all-to-all-start.1 = ((bf16[16,128,128]{2,1,0:T(8,128)(2,1)}), bf16[16,128,128]{2,1,0:T(8,128)(2,1)S(1)}, u32[]{:S(2)}, u32[]{:S(2)}) async-start(bf16[16,128,128]{2,1,0:T(8,128)(2,1)} %combine.1), calls=%async_computation.1 | async-start | bytes 1048576 | tf_op jit(solution)/shard_map/all_to_all | solution.py:304
  48.6 21.1 %collective-permute-start.7 = (bf16[768,128]{1,0:T(8,128)(2,1)S(1)}, bf16[768,128]{1,0:T(8,128)(2,1)S(1)}, u32[]{:S(2)}, u32[]{:S(2)}) collective-permute-start(bf16[768,128]{1,0:T(8,128)(2,1)S(1)} %select_select_fusion), channel_id=1, source_target_pairs={{0,8},{8,0},{1,9},{9,1},{2,10},{10,2},{3,11},{11,3},{4,12},{12,4},... | collective-permute-start | bytes 589832 | tf_op jit(solution)/shard_map/ppermute | solution.py:300
  59.6 22.6 %all-to-all-start.2 = ((bf16[16,32,256]{2,1,0:T(8,128)(2,1)}), bf16[16,32,256]{2,1,0:T(8,128)(2,1)S(1)}, u32[]{:S(2)}, u32[]{:S(2)}) async-start(bf16[16,32,256]{2,1,0:T(8,128)(2,1)} %project.1), calls=%async_computation.2 | async-start | bytes 524288 | tf_op jit(solution)/shard_map/all_to_all | solution.py:304
  69.8 1.4 %copy-start.4 = (bf16[768,1024]{1,0:T(8,128)(2,1)S(1)}, bf16[768,1024]{1,0:T(8,128)(2,1)}, u32[]{:S(2)}) copy-start(bf16[768,1024]{1,0:T(8,128)(2,1)} %q_ref.5) | copy-start | bytes 4718596
  71.2 1.9 %copy-start.7 = (f32[768,1024]{1,0:T(8,128)S(1)}, f32[768,1024]{1,0:T(8,128)}, u32[]{:S(2)}) copy-start(f32[768,1024]{1,0:T(8,128)} %copy-done.6) | copy-start | bytes 9437188

commit v3 on v2

v3 whole, which is shorter than its diff:
```python
import functools

import jax
import jax.numpy as jnp
from jax import lax
from jax.experimental import pallas as pl
from jax.experimental.pallas import tpu as pltpu
from jax.sharding import Mesh, PartitionSpec as P

HEAD = 128
BLOCK = 768
HEADS = 8
QROWS = 512
HALF = 256
SEND1 = HEAD + 16
HIDDEN = 1e30
LOG2_SCALE = 1.4426950408889634 * HEAD ** (-0.5)
BF = jnp.bfloat16
F32 = jnp.float32


def scores_of(q, k):
    return lax.dot_general(q, k, (((1,), (1,)), ((), ())), preferred_element_type=F32) * LOG2_SCALE


def pipelined(count, scores, finish):
    s = scores(0)
    for n in range(count):
        s_next = scores(n + 1) if n + 1 < count else None
        finish(n, s)
        s = s_next


def to_lanes(column):
    r = lax.broadcasted_iota(jnp.int32, (HEAD, HEAD), 0)
    c = lax.broadcasted_iota(jnp.int32, (HEAD, HEAD), 1)
    return jnp.sum(jnp.where(r == c, column, 0.0), axis=0, keepdims=True)


def prep_kernel(q_hbm, k_hbm, v_hbm, q_ref, k_ref, values_ref, v_buf, sems):
    core = lax.axis_index("c")
    copies = [pltpu.make_async_copy(v_hbm, v_buf, sems.at[0]), pltpu.make_async_copy(k_hbm, k_ref, sems.at[1])]
    for z in range(8):
        rows = pl.ds(pl.multiple_of(64 * z + 32 * core, 32), 32)
        copies.append(
            pltpu.make_async_copy(q_hbm.at[rows, :], q_ref.at[32 * z : 32 * z + 32, :], sems.at[2 + z])
        )
    for copy in copies:
        copy.start()
    values_ref[:, HEAD : 2 * HEAD] = jnp.ones((BLOCK, HEAD), BF)
    for copy in copies:
        copy.wait()
    values_ref[:, 0:HEAD] = v_buf[...]


def query_kernel(q_ref, k_ref, values_ref, kp_ref, vp_ref, out_ref, piece_ref, values_p):
    core = lax.axis_index("c")
    values_p[:, 0:HEAD] = vp_ref[...]
    values_p[:, HEAD : 2 * HEAD] = jnp.ones((BLOCK, HEAD), BF)
    row_id = lax.broadcasted_iota(jnp.int32, (16, HEAD), 0)

    def scores(j):
        q = q_ref[:, HEAD * j : HEAD * j + HEAD]
        return scores_of(q, k_ref[...]), scores_of(q, kp_ref[...])

    def finish(j, s):
        peak = jnp.maximum(
            jnp.max(s[0], axis=1, keepdims=True), jnp.max(s[1], axis=1, keepdims=True)
        )
        peak = peak.astype(BF).astype(F32)
        acc = jnp.dot(
            jnp.exp2(s[0] - peak).astype(BF), values_ref[...], preferred_element_type=F32
        ) + jnp.dot(jnp.exp2(s[1] - peak).astype(BF), values_p[...], preferred_element_type=F32)
        total = acc[:, HEAD : HEAD + 1]
        for half in range(2):
            rows = slice(half * HEAD, half * HEAD + HEAD)
            out_ref[2 * j + half, 0:HEAD, :] = acc[rows, 0:HEAD].astype(BF)
            peak_l = to_lanes(peak[rows])
            total_l = to_lanes(total[rows])
            high = total_l.astype(BF).astype(F32)
            stats = jnp.where(row_id == 0, peak_l, 0.0)
            stats = jnp.where(row_id == 1, high, stats)
            stats = jnp.where(row_id == 2, total_l - high, stats)
            out_ref[2 * j + half, HEAD:SEND1, :] = stats.astype(BF)

    pipelined(HEADS, scores, finish)
    piece_ref[...] = jnp.where(core == 0, k_ref[...], vp_ref[...])


def combine_kernel(in_ref, after_ref, out_ref):
    stats = in_ref[:, HEAD : HEAD + 16, :].astype(F32)
    peak = stats[:, 0, :]
    total = stats[:, 1, :] + stats[:, 2, :]
    top = jnp.max(peak, axis=0, keepdims=True)
    weight = jnp.exp2(peak - top)
    weight = weight / jnp.sum(weight * total, axis=0, keepdims=True)
    weight_t = jnp.concatenate([weight, jnp.zeros((HEAD - 16, HEAD), F32)], axis=0).T
    out = jnp.zeros((HEAD, HEAD), F32)
    for g in range(16):
        out = out + weight_t[:, g : g + 1] * in_ref[g, 0:HEAD, :].astype(F32)
    out = out.astype(BF)
    for g in range(16):
        out_ref[g] = out


def project_kernel(in_ref, w_ref, wp_ref, out_ref):
    core = lax.axis_index("c")
    a = jnp.concatenate(
        [
            jnp.concatenate([in_ref[2 * j + half] for j in range(HEADS)], axis=1)
            for half in range(2)
        ],
        axis=0,
    )
    for w, dest in ((w_ref, core), (wp_ref, 1 - core)):
        y = jnp.dot(a, w[...], preferred_element_type=F32).astype(BF)
        for z in range(8):
            out_ref[2 * z + dest] = y[32 * z : 32 * z + 32, :]


def final_kernel(in_ref, out_ref):
    for half in range(2):
        total = in_ref[half].astype(F32)
        for z in range(1, 8):
            total = total + in_ref[2 * z + half].astype(F32)
        out_ref[32 * half : 32 * half + 32, :] = total.astype(BF)


def column_copies(make):
    return [make(slice(2 * HEAD * g, 2 * HEAD * g + 2 * HEAD), g) for g in range(HEADS // 2)]


CONTEXT_BLOCKS = [(j, i) for j in range(HEADS) for i in range(3)]


def own_kernel(q_hbm, k_ref, values_ref, after_ref, acc_ref, peak_ref, q_ref, sems):
    copies = column_copies(
        lambda cols, g: pltpu.make_async_copy(q_hbm.at[:, cols], q_ref.at[:, cols], sems.at[g])
    )
    for copy in copies:
        copy.start()
    r = lax.broadcasted_iota(jnp.int32, (HALF, HALF), 0)
    c = lax.broadcasted_iota(jnp.int32, (HALF, HALF), 1)

    def scores(n):
        j, i = CONTEXT_BLOCKS[n]
        if j % 2 == 0 and i == 0:
            copies[j // 2].wait()
        q = q_ref[i * HALF : (i + 1) * HALF, HEAD * j : HEAD * j + HEAD]
        return scores_of(q, k_ref[0 : (i + 1) * HALF, :])

    def finish(n, s):
        j, i = CONTEXT_BLOCKS[n]
        rows = slice(i * HALF, (i + 1) * HALF)
        diagonal = jnp.where(c <= r, s[:, i * HALF :], -HIDDEN)
        s = jnp.concatenate([s[:, 0 : i * HALF], diagonal], axis=1) if i else diagonal
        peak = jnp.max(s, axis=1, keepdims=True)
        p = jnp.exp2(s - peak).astype(BF)
        acc = jnp.dot(p, values_ref[0 : (i + 1) * HALF, :], preferred_element_type=F32)
        acc_ref[rows, 2 * HEAD * j : 2 * HEAD * (j + 1)] = acc
        peak_ref[rows, HEAD * j : HEAD * j + HEAD] = jnp.broadcast_to(peak, (HALF, HEAD))

    pipelined(len(CONTEXT_BLOCKS), scores, finish)


def anchor_kernel(
    q_hbm, half_ref, other_ref, acc_ref, peak_ref, out_hbm, q_ref, out_ref, k_ref, values_ref, sems, out_sems
):
    copies = column_copies(
        lambda cols, g: pltpu.make_async_copy(q_hbm.at[:, cols], q_ref.at[:, cols], sems.at[g])
    )
    for copy in copies:
        copy.start()
    writes = column_copies(
        lambda cols, g: pltpu.make_async_copy(out_ref.at[:, cols], out_hbm.at[:, cols], out_sems.at[g])
    )
    core = lax.axis_index("c")
    first = jnp.logical_and(
        core == 0, jnp.logical_and(lax.axis_index("x") == 0, lax.axis_index("y") == 0)
    )
    k_ref[...] = jnp.where(core == 0, half_ref[...], other_ref[...])
    values_ref[:, 0:HEAD] = jnp.where(core == 0, other_ref[...], half_ref[...])
    values_ref[:, HEAD : 2 * HEAD] = jnp.ones((BLOCK, HEAD), BF)

    def scores(n):
        j, i = CONTEXT_BLOCKS[n]
        if j % 2 == 0 and i == 0:
            copies[j // 2].wait()
        return scores_of(q_ref[i * HALF : (i + 1) * HALF, HEAD * j : HEAD * j + HEAD], k_ref[...])

    def finish(n, s):
        j, i = CONTEXT_BLOCKS[n]
        rows = slice(i * HALF, (i + 1) * HALF)
        own_peak = peak_ref[rows, HEAD * j : HEAD * j + HEAD]
        peak = jnp.maximum(own_peak, jnp.max(s, axis=1, keepdims=True))
        peak = jnp.where(first, own_peak, peak)
        shift = jnp.where(first, HIDDEN, peak)
        p = jnp.exp2(s - jnp.concatenate([shift] * 6, axis=1)).astype(BF)
        acc = jnp.dot(p, values_ref[...], preferred_element_type=F32)
        scale = jnp.exp2(own_peak - peak)
        own = acc_ref[rows, 2 * HEAD * j : 2 * HEAD * (j + 1)]
        total = acc[:, HEAD : 2 * HEAD] + scale * own[:, HEAD : 2 * HEAD]
        mixture = acc[:, 0:HEAD] + scale * own[:, 0:HEAD]
        out_ref[rows, HEAD * j : HEAD * j + HEAD] = (mixture / total).astype(BF)
        if j % 2 == 1 and i == 2:
            writes[j // 2].start()

    pipelined(len(CONTEXT_BLOCKS), scores, finish)
    for copy in writes:
        copy.wait()


def pick_kernel(axis, mine_ref, one_ref, two_ref, three_ref, after_ref, out_ref):
    at = lax.axis_index(axis)
    for k, ref in enumerate((mine_ref, one_ref, two_ref, three_ref)):

        @pl.when(at == k)
        def _(ref=ref):
            out_ref[...] = ref[...]


VMEM = pl.BlockSpec(memory_space=pltpu.VMEM)
HBM = pl.BlockSpec(memory_space=pltpu.HBM)
ANY = pl.BlockSpec(memory_space=pl.ANY)


def params():
    return pltpu.CompilerParams(vmem_limit_bytes=24 * 1024 * 1024)


def cost(flops, nbytes, exps=0):
    return pl.CostEstimate(flops=flops, bytes_accessed=nbytes, transcendentals=exps)


def shape(dims, dtype=BF):
    return jax.ShapeDtypeStruct(dims, dtype)


def in_hbm(value):
    return pltpu.with_memory_space_constraint(value, pltpu.HBM)


def prep_call(query, k, v):
    return pl.pallas_call(
        prep_kernel,
        in_specs=[HBM] * 3,
        out_specs=(VMEM,) * 3,
        out_shape=(shape((HALF, HEADS * HEAD)), shape((BLOCK, HEAD)), shape((BLOCK, 2 * HEAD))),
        scratch_shapes=[pltpu.VMEM((BLOCK, HEAD), BF), pltpu.SemaphoreType.DMA((10,))],
        compiler_params=params(),
        cost_estimate=cost(1 << 18, 2 << 20),
        name="prep",
    )(in_hbm(query), in_hbm(k), in_hbm(v))


def query_call(q, k, values, kp, vp):
    return pl.pallas_call(
        query_kernel,
        in_specs=[VMEM] * 5,
        out_specs=(VMEM,) * 2,
        out_shape=(shape((16, SEND1, HEAD)), shape((BLOCK, HEAD))),
        scratch_shapes=[pltpu.VMEM((BLOCK, 2 * HEAD), BF)],
        compiler_params=params(),
        cost_estimate=cost(4 * 2048 * 1536 * 256, 3 << 20, 2048 * 1536),
        name="query_attention",
    )(q, k, values, kp, vp)


def own_call(ctx_query, k, values, after):
    return pl.pallas_call(
        own_kernel,
        in_specs=[HBM, VMEM, VMEM, ANY],
        out_specs=(VMEM,) * 2,
        out_shape=(shape((BLOCK, 2 * HEADS * HEAD), F32), shape((BLOCK, HEADS * HEAD), F32)),
        scratch_shapes=[pltpu.VMEM((BLOCK, HEADS * HEAD), BF), pltpu.SemaphoreType.DMA((4,))],
        compiler_params=params(),
        cost_estimate=cost(4 * 6144 * 512 * 256, 4 << 20, 6144 * 512),
        name="context_own",
    )(in_hbm(ctx_query), k, values, after)


def anchor_call(ctx_query, half, other, acc, peak):
    return pl.pallas_call(
        anchor_kernel,
        in_specs=[HBM, VMEM, VMEM, VMEM, VMEM],
        out_specs=HBM,
        out_shape=shape((BLOCK, HEADS * HEAD)),
        scratch_shapes=[
            pltpu.VMEM((BLOCK, HEADS * HEAD), BF),
            pltpu.VMEM((BLOCK, HEADS * HEAD), BF),
            pltpu.VMEM((BLOCK, HEAD), BF),
            pltpu.VMEM((BLOCK, 2 * HEAD), BF),
            pltpu.SemaphoreType.DMA((4,)),
            pltpu.SemaphoreType.DMA((4,)),
        ],
        compiler_params=params(),
        cost_estimate=cost(4 * 6144 * 768 * 256, 6 << 20, 6144 * 768),
        name="context_anchor",
    )(in_hbm(ctx_query), half, other, acc, peak)


def pick_call(axis, mine, moved, after):
    return pl.pallas_call(
        functools.partial(pick_kernel, axis),
        in_specs=[VMEM] * 4 + [ANY],
        out_specs=VMEM,
        out_shape=shape((BLOCK, HEAD)),
        compiler_params=params(),
        cost_estimate=cost(1 << 16, 1 << 19),
        name="pick_" + axis,
    )(mine, *moved, after)


def combine_call(received, after):
    return pl.pallas_call(
        combine_kernel,
        out_shape=shape((16, HEAD, HEAD)),
        in_specs=[VMEM, ANY],
        out_specs=VMEM,
        compiler_params=params(),
        cost_estimate=cost(1 << 20, 3 << 19),
        name="combine",
    )(received, after)


def project_call(gathered, w, wp):
    return pl.pallas_call(
        project_kernel,
        out_shape=shape((16, 32, 256)),
        in_specs=[VMEM] * 3,
        out_specs=VMEM,
        compiler_params=params(),
        cost_estimate=cost(2 * 256 * 1024 * 512, 2 << 20),
        name="project",
    )(gathered, w, wp)


def final_call(received):
    return pl.pallas_call(
        final_kernel,
        out_shape=shape((64, 256)),
        in_specs=[VMEM],
        out_specs=VMEM,
        compiler_params=params(),
        cost_estimate=cost(1 << 17, 1 << 18),
        name="final_sum",
    )(received)


def swap(value):
    return lax.ppermute(value, "c", [(0, 1), (1, 0)])


def exchange(value, axes):
    return lax.all_to_all(value, axes, 0, 0, tiled=True)


def chip_copies(value, pairs_of):
    moved = []
    for k in (1, 2, 3):
        to = {(a, b): (a, b) for a in range(4) for b in range(4)}
        for source, target in pairs_of(k):
            to[source], to[target] = target, source
        moved.append(
            lax.ppermute(value, ("y", "x"), [(4 * a + b, 4 * c + d) for (a, b), (c, d) in to.items()])
        )
    return moved


def per_device(ctx_query, context_key, context_value, query, out_weight):
    key_p, value_p = swap(context_key), swap(context_value)
    q, k, values = prep_call(query, context_key, context_value)
    sent, piece = query_call(q, k, values, key_p, value_p)
    received = exchange(sent, ("y", "x"))
    along_x = chip_copies(piece, lambda k: [((0, 0), (0, k))])
    weight_p = swap(out_weight)
    acc, peak = own_call(ctx_query, k, values, sent)
    merged = combine_call(received, peak)
    gathered = exchange(merged, ("y", "x"))
    row = pick_call("x", piece, along_x, merged)
    along_y = chip_copies(row, lambda k: [((0, j), (k, j)) for j in range(4)])
    shares = project_call(gathered, out_weight, weight_p)
    half = pick_call("y", row, along_y, shares)
    ctx_out = anchor_call(ctx_query, half, swap(half), acc, peak)
    answer = final_call(exchange(shares, ("z", "c")))
    return ctx_out, answer


def solution(mesh):
    fine = Mesh(mesh.devices.reshape(4, 4, 2, 8), ("y", "x", "c", "z"))
    hst = ("y", "x", "c")
    in_specs = (P(hst, "z"), P(hst, "z"), P(hst, "z"), P(None, "z"), P("z", hst))
    out_specs = (P(hst, "z"), P("z", hst))
    return jax.shard_map(
        per_device, mesh=fine, in_specs=in_specs, out_specs=out_specs, check_vma=False
    )
```

time: 83.5 us -> 95.5 us (1.14)
  waiting for transfers between devices: 10.3 us -> 20.5 us
  Pallas kernels: 25.2 us -> 30.1 us
  other arithmetic: 2.01 us -> 0 us
    ppermute x6, waiting for transfers between devices: 0.02 us -> 18.9 us  [chip_copies(): lax.ppermute(value, ('y', 'x'), [(4 * a + b, 4 * c + d) for (a, b), (c, d...]
    all_to_all x3, waiting for transfers between devices: 9.08 us -> 1.39 us  [exchange(): return lax.all_to_all(value, axes, 0, 0, tiled=True)]
    pallas_call x6 -> x9, Pallas kernels: 25.2 us -> 30.1 us  [the longest x1 10.4 us: anchor_call(): pl.pallas_call(anchor_kernel, in_specs=[HBM, VMEM, VMEM, VMEM, VMEM], out...]
    select_n x4 -> x0, other arithmetic: 2.01 us -> none  [the longest x1 0.98 us: per_device(): jnp.where(y == 0, row, jnp.where(y == 1, along_y[0], jnp.where(y == 2, al...]
    all_to_all x3, starting transfers between devices: 17.7 us -> 19.1 us  [exchange(): return lax.all_to_all(value, axes, 0, 0, tiled=True)]
    ppermute x4, starting transfers between devices: 5.84 us -> 4.57 us  [swap(): return lax.ppermute(value, 'c', [(0, 1), (1, 0)])]
    ppermute x4, waiting for transfers between devices: 1.19 us -> 0.22 us  [swap(): return lax.ppermute(value, 'c', [(0, 1), (1, 0)])]
    unnamed x20 -> x8, local copies, waits for them, and re-layouts: 7.02 us -> 6.43 us
  transfers between devices with their start and end apart: 13 -> 13, of which waited for: 2 -> 7; matrix products, arithmetic and copies ran while one was open for 2% -> 0% of each run, Pallas kernels for 30% -> 24%
where the time goes in v3:
time: 95.5 us; the launch traced here: 94.7 us
  starting transfers between devices  37 us (39%)
  Pallas kernels  30.1 us (32%)
  waiting for transfers between devices  20.5 us (21%)
  local copies, waits for them, and re-layouts  6.43 us (7%)
    all_to_all x3, starting transfers between devices, exchange(): return lax.all_to_all(value, axes, 0, 0, tiled=True)  19.1 us
    ppermute x6, waiting for transfers between devices, chip_copies(): lax.ppermute(value, ('y', 'x'), [(4 * a + b, 4 * c + d) for (a, b), (c, d...  18.9 us
    ppermute x6, starting transfers between devices, chip_copies(): lax.ppermute(value, ('y', 'x'), [(4 * a + b, 4 * c + d) for (a, b), (c, d...  13.3 us
    pallas_call x1, Pallas kernels, anchor_call(): pl.pallas_call(anchor_kernel, in_specs=[HBM, VMEM, VMEM, VMEM, VMEM], out...  10.4 us
    unnamed x8, local copies, waits for them, and re-layouts  6.43 us
    pallas_call x1, Pallas kernels, own_call(): pl.pallas_call(own_kernel, in_specs=[HBM, VMEM, VMEM, ANY], out_specs=(VM...  5.88 us
    pallas_call x1, Pallas kernels, query_call(): pl.pallas_call(query_kernel, in_specs=[VMEM] * 5, out_specs=(VMEM,) * 2,...  5.17 us
    ppermute x4, starting transfers between devices, swap(): return lax.ppermute(value, 'c', [(0, 1), (1, 0)])  4.57 us
  transfers between devices with their start and end apart: 13, of which 7 were waited for; matrix products, arithmetic and copies ran while one was open for 0% of the time, Pallas kernels for 24%

profile of v3, /device:TPU:1, one launch (start us, length us, event | category | flops | bytes accessed | tf_op | source)
XLA Modules:
  0.0 94.7 jit_solution(6703366907423350322)
XLA Ops:
  0.6 3.3 %collective-permute-start = (bf16[768,128]{1,0:T(8,128)(2,1)}, bf16[768,128]{1,0:T(8,128)(2,1)S(1)}, u32[]{:S(2)}, u32[]{:S(2)}) collective-permute-start(bf16[768,128]{1,0:T(8,128)(2,1)} %k_hbm.1), channel_id=1, source_target_pairs={{0,8},{8,0},{1,9},{9,1},{2,10},{10,2},{3,11},{11,3},{4,12},{12,4},... | collective-permute-start | bytes 589832 | tf_op jit(solution)/shard_map/ppermute | solution.py:351
  4.0 0.1 collective-permute-start.1
  4.1 1.3 %prep.1 = (bf16[256,1024]{1,0:T(8,128)(2,1)S(1)}, bf16[768,128]{1,0:T(8,128)(2,1)S(1)}, bf16[768,256]{1,0:T(8,128)(2,1)S(1)}) custom-call(bf16[512,1024]{1,0:T(8,128)(2,1)} %q_hbm.3, bf16[768,128]{1,0:T(8,128)(2,1)} %k_hbm.1, bf16[768,128]{1,0:T(8,128)(2,1)} %v_hbm.1), custom_call_target="tpu_custom_call" | custom-call | flops 262144 | bytes 2097152 | tf_op jit(solution)/shard_map/prep/pallas_call | solution.py:244
  5.4 0.0 copy-start
  5.4 0.0 collective-permute-done.kp_ref
  5.4 0.2 collective-permute-done.1.vp_ref
  5.6 5.2 %query_attention.1 = (bf16[16,144,128]{2,1,0:T(8,128)(2,1)}, bf16[768,128]{1,0:T(8,128)(2,1)S(1)}) custom-call(bf16[256,1024]{1,0:T(8,128)(2,1)S(1)} %get-tuple-element.9.q_ref, bf16[768,128]{1,0:T(8,128)(2,1)S(1)} %get-tuple-element.10.k_ref, bf16[768,256]{1,0:T(8,128)(2,1)S(1)} %get-tuple-element.11.values_ref, ...), custom_call_target="tpu_custom_call" | custom-call | flops 3221225472 | bytes 3145728 | tf_op jit(solution)/shard_map/query_attention/pallas_call | solution.py:257
  10.8 0.0 copy-done
  10.8 5.1 %all-to-all-start = ((bf16[16,144,128]{2,1,0:T(8,128)(2,1)}), bf16[16,144,128]{2,1,0:T(8,128)(2,1)}, u32[]{:S(2)}, u32[]{:S(2)}) async-start(bf16[16,144,128]{2,1,0:T(8,128)(2,1)} %get-tuple-element.13.after_ref), calls=%async_computation | async-start | bytes 1179648 | tf_op jit(solution)/shard_map/all_to_all | solution.py:355
  15.9 0.7 collective-permute-start.8
  16.5 0.0 copy-start.1
  16.5 1.0 %copy-done.1 = bf16[768,256]{1,0:T(8,128)(2,1)S(1)} copy-done((bf16[768,256]{1,0:T(8,128)(2,1)S(1)}, bf16[768,256]{1,0:T(8,128)(2,1)}, u32[]{:S(2)}) %copy-start.1) | copy-done | bytes 393240
  17.5 5.9 %context_own.1 = (f32[768,2048]{1,0:T(8,128)S(1)}, f32[768,1024]{1,0:T(8,128)S(1)}) custom-call(bf16[768,1024]{1,0:T(8,128)(2,1)} %q_hbm.5, bf16[768,128]{1,0:T(8,128)(2,1)S(1)} %get-tuple-element.10.k_ref, bf16[768,256]{1,0:T(8,128)(2,1)S(1)} %copy-done.1, bf16[16,144,128]{2,1,0:T(8,128)(2,1)} %get-tuple-element.13.after_ref), custom_call_target="tpu_custom_call" | custom-call | flops 3221225472 | bytes 4194304 | tf_op jit(solution)/shard_map/context_own/pallas_call | solution.py:270
  23.4 0.0 copy-start.2
  23.4 2.6 %copy-done.2 = f32[768,2048]{1,0:T(8,128)} copy-done((f32[768,2048]{1,0:T(8,128)}, f32[768,2048]{1,0:T(8,128)S(1)}, u32[]{:S(2)}) %copy-start.2) | copy-done | bytes 6291480
  26.0 1.4 %all-to-all-done.in_ref = bf16[16,144,128]{2,1,0:T(8,128)(2,1)} async-done(((bf16[16,144,128]{2,1,0:T(8,128)(2,1)}), bf16[16,144,128]{2,1,0:T(8,128)(2,1)}, u32[]{:S(2)}, u32[]{:S(2)}) %all-to-all-start) | async-done | bytes 589856 | tf_op jit(solution)/shard_map/all_to_all | solution.py:355
  27.4 2.4 %combine.1.after_ref = bf16[16,128,128]{2,1,0:T(8,128)(2,1)} custom-call(bf16[16,144,128]{2,1,0:T(8,128)(2,1)} %all-to-all-done.in_ref, f32[768,1024]{1,0:T(8,128)S(1)} %get-tuple-element.14.after_ref.peak_ref), custom_call_target="tpu_custom_call" | custom-call | flops 1048576 | bytes 1572864 | tf_op jit(solution)/shard_map/combine/pallas_call | solution.py:315
  29.9 5.5 %all-to-all-start.1 = ((bf16[16,128,128]{2,1,0:T(8,128)(2,1)}), bf16[16,128,128]{2,1,0:T(8,128)(2,1)}, u32[]{:S(2)}, u32[]{:S(2)}) async-start(bf16[16,128,128]{2,1,0:T(8,128)(2,1)} %combine.1.after_ref), calls=%async_computation.1 | async-start | bytes 1048576 | tf_op jit(solution)/shard_map/all_to_all | solution.py:355
  35.3 3.2 %collective-permute-start.2 = (bf16[768,128]{1,0:T(8,128)(2,1)S(1)}, bf16[768,128]{1,0:T(8,128)(2,1)S(1)}, u32[]{:S(2)}, u32[]{:S(2)}) collective-permute-start(bf16[768,128]{1,0:T(8,128)(2,1)S(1)} %get-tuple-element.12.mine_ref), channel_id=1, source_target_pairs={{0,16},{16,0},{32,32},{48,48},{64,64},{80,80},{96,96},{112,112},{1... | collective-permute-start | bytes 589832 | tf_op jit(solution)/shard_map/ppermute | solution.py:365
  38.6 2.2 %collective-permute-start.3 = (bf16[768,128]{1,0:T(8,128)(2,1)S(1)}, bf16[768,128]{1,0:T(8,128)(2,1)S(1)}, u32[]{:S(2)}, u32[]{:S(2)}) collective-permute-start(bf16[768,128]{1,0:T(8,128)(2,1)S(1)} %get-tuple-element.12.mine_ref), channel_id=1, source_target_pairs={{0,32},{16,16},{32,0},{48,48},{64,64},{80,80},{96,96},{112,112},{1... | collective-permute-start | bytes 589832 | tf_op jit(solution)/shard_map/ppermute | solution.py:365
  40.7 2.1 %collective-permute-start.4 = (bf16[768,128]{1,0:T(8,128)(2,1)S(1)}, bf16[768,128]{1,0:T(8,128)(2,1)S(1)}, u32[]{:S(2)}, u32[]{:S(2)}) collective-permute-start(bf16[768,128]{1,0:T(8,128)(2,1)S(1)} %get-tuple-element.12.mine_ref), channel_id=1, source_target_pairs={{0,48},{16,16},{32,32},{48,0},{64,64},{80,80},{96,96},{112,112},{1... | collective-permute-start | bytes 589832 | tf_op jit(solution)/shard_map/ppermute | solution.py:365
  42.9 4.5 %collective-permute-done.2.one_ref = bf16[768,128]{1,0:T(8,128)(2,1)S(1)} collective-permute-done((bf16[768,128]{1,0:T(8,128)(2,1)S(1)}, bf16[768,128]{1,0:T(8,128)(2,1)S(1)}, u32[]{:S(2)}, u32[]{:S(2)}) %collective-permute-start.2) | collective-permute-done | bytes 196640 | tf_op jit(solution)/shard_map/ppermute | solution.py:365
  47.4 2.1 %collective-permute-done.3.two_ref = bf16[768,128]{1,0:T(8,128)(2,1)S(1)} collective-permute-done((bf16[768,128]{1,0:T(8,128)(2,1)S(1)}, bf16[768,128]{1,0:T(8,128)(2,1)S(1)}, u32[]{:S(2)}, u32[]{:S(2)}) %collective-permute-start.3) | collective-permute-done | bytes 196640 | tf_op jit(solution)/shard_map/ppermute | solution.py:365
  49.4 4.2 %collective-permute-done.4.three_ref = bf16[768,128]{1,0:T(8,128)(2,1)S(1)} collective-permute-done((bf16[768,128]{1,0:T(8,128)(2,1)S(1)}, bf16[768,128]{1,0:T(8,128)(2,1)S(1)}, u32[]{:S(2)}, u32[]{:S(2)}) %collective-permute-start.4) | collective-permute-done | bytes 196640 | tf_op jit(solution)/shard_map/ppermute | solution.py:365
  53.6 1.9 %collective-permute-start.5 = (bf16[768,128]{1,0:T(8,128)(2,1)S(1)}, bf16[768,128]{1,0:T(8,128)(2,1)S(1)}, u32[]{:S(2)}, u32[]{:S(2)}) collective-permute-start(bf16[768,128]{1,0:T(8,128)(2,1)S(1)} %pick_x.1.mine_ref), channel_id=1, source_target_pairs={{0,64},{16,80},{32,96},{48,112},{64,0},{80,16},{96,32},{112,48},{1... | collective-permute-start | bytes 589832 | tf_op jit(solution)/shard_map/ppermute | solution.py:365
  55.6 1.9 %collective-permute-start.6 = (bf16[768,128]{1,0:T(8,128)(2,1)S(1)}, bf16[768,128]{1,0:T(8,128)(2,1)}, u32[]{:S(2)}, u32[]{:S(2)}) collective-permute-start(bf16[768,128]{1,0:T(8,128)(2,1)S(1)} %pick_x.1.mine_ref), channel_id=1, source_target_pairs={{0,128},{16,144},{32,160},{48,176},{64,64},{80,80},{96,96},{112,11... | collective-permute-start | bytes 589832 | tf_op jit(solution)/shard_map/ppermute | solution.py:365
  57.5 1.9 %collective-permute-start.7 = (bf16[768,128]{1,0:T(8,128)(2,1)S(1)}, bf16[768,128]{1,0:T(8,128)(2,1)}, u32[]{:S(2)}, u32[]{:S(2)}) collective-permute-start(bf16[768,128]{1,0:T(8,128)(2,1)S(1)} %pick_x.1.mine_ref), channel_id=1, source_target_pairs={{0,192},{16,208},{32,224},{48,240},{64,64},{80,80},{96,96},{112,11... | collective-permute-start | bytes 589832 | tf_op jit(solution)/shard_map/ppermute | solution.py:365
  59.4 0.0 collective-permute-done.8.wp_ref
  59.4 0.0 all-to-all-done.1.in_ref
  59.4 2.5 %project.1.after_ref = bf16[16,32,256]{2,1,0:T(8,128)(2,1)} custom-call(bf16[16,128,128]{2,1,0:T(8,128)(2,1)} %all-to-all-done.1.in_ref, bf16[1024,256]{1,0:T(8,128)(2,1)} %w_ref.1, bf16[1024,256]{1,0:T(8,128)(2,1)} %collective-permute-done.8.wp_ref), custom_call_target="tpu_custom_call" | custom-call | flops 268435456 | bytes 2097152 | tf_op jit(solution)/shard_map/project/pallas_call | solution.py:327
  62.0 0.0 collective-permute-done.5.one_ref
  62.0 3.1 %collective-permute-done.6.two_ref = bf16[768,128]{1,0:T(8,128)(2,1)} collective-permute-done((bf16[768,128]{1,0:T(8,128)(2,1)S(1)}, bf16[768,128]{1,0:T(8,128)(2,1)}, u32[]{:S(2)}, u32[]{:S(2)}) %collective-permute-start.6) | collective-permute-done | bytes 196640 | tf_op jit(solution)/shard_map/ppermute | solution.py:365
  65.1 5.0 %collective-permute-done.7.three_ref = bf16[768,128]{1,0:T(8,128)(2,1)} collective-permute-done((bf16[768,128]{1,0:T(8,128)(2,1)S(1)}, bf16[768,128]{1,0:T(8,128)(2,1)}, u32[]{:S(2)}, u32[]{:S(2)}) %collective-permute-start.7) | collective-permute-done | bytes 196640 | tf_op jit(solution)/shard_map/ppermute | solution.py:365
  70.1 1.7 %pick_y.1.half_ref = bf16[768,128]{1,0:T(8,128)(2,1)} custom-call(bf16[768,128]{1,0:T(8,128)(2,1)S(1)} %pick_x.1.mine_ref, bf16[768,128]{1,0:T(8,128)(2,1)S(1)} %collective-permute-done.5.one_ref, bf16[768,128]{1,0:T(8,128)(2,1)} %collective-permute-done.6.two_ref, bf16[768,128]{1,0:T(8,128)(2,1)} %collective-permute-done.7.three_ref, ...), custom_call_target="tpu_custom_call" | custom-call | flops 65536 | bytes 524288 | tf_op jit(solution)/shard_map/pick_y/pallas_call | solution.py:303
  71.8 0.5 collective-permute-start.9
  72.3 8.6 %all-to-all-start.2 = ((bf16[16,32,256]{2,1,0:T(8,128)(2,1)}), bf16[16,32,256]{2,1,0:T(8,128)(2,1)S(1)}, u32[]{:S(2)}, u32[]{:S(2)}) async-start(bf16[16,32,256]{2,1,0:T(8,128)(2,1)} %project.1.after_ref), calls=%async_computation.2 | async-start | bytes 524288 | tf_op jit(solution)/shard_map/all_to_all | solution.py:355
  80.9 0.0 collective-permute-done.9.other_ref
  80.9 0.0 copy-start.3
  80.9 2.8 %copy-done.3 = f32[768,2048]{1,0:T(8,128)S(1)} copy-done((f32[768,2048]{1,0:T(8,128)S(1)}, f32[768,2048]{1,0:T(8,128)}, u32[]{:S(2)}) %copy-start.3) | copy-done | bytes 6291480
  83.7 10.4 %context_anchor.1 = bf16[768,1024]{1,0:T(8,128)(2,1)} custom-call(bf16[768,1024]{1,0:T(8,128)(2,1)} %q_hbm.5, bf16[768,128]{1,0:T(8,128)(2,1)} %pick_y.1.half_ref, bf16[768,128]{1,0:T(8,128)(2,1)} %collective-permute-done.9.other_ref, f32[768,2048]{1,0:T(8,128)S(1)} %copy-done.3, f32[768,1024]{1,0:T(8,128)S(1)} %get-tuple-element.14.after_ref.peak_ref), custom_call_target="tpu_custom_call" | custom-call | flops 4831838208 | bytes 6291456 | tf_op jit(solution)/shard_map/context_anchor/pallas_call | solution.py:283
  94.1 0.0 all-to-all-done.2.in_ref
  94.1 0.7 final_sum.1
  (1 shorter events, 0.0 us)
Async XLA Ops:
  0.6 4.8 %collective-permute-start = (bf16[768,128]{1,0:T(8,128)(2,1)}, bf16[768,128]{1,0:T(8,128)(2,1)S(1)}, u32[]{:S(2)}, u32[]{:S(2)}) collective-permute-start(bf16[768,128]{1,0:T(8,128)(2,1)} %k_hbm.1), channel_id=1, source_target_pairs={{0,8},{8,0},{1,9},{9,1},{2,10},{10,2},{3,11},{11,3},{4,12},{12,4},... | collective-permute-start | bytes 589832 | tf_op jit(solution)/shard_map/ppermute | solution.py:351
  4.0 1.7 %collective-permute-start.1 = (bf16[768,128]{1,0:T(8,128)(2,1)}, bf16[768,128]{1,0:T(8,128)(2,1)S(1)}, u32[]{:S(2)}, u32[]{:S(2)}) collective-permute-start(bf16[768,128]{1,0:T(8,128)(2,1)} %v_hbm.1), channel_id=1, source_target_pairs={{0,8},{8,0},{1,9},{9,1},{2,10},{10,2},{3,11},{11,3},{4,12},{12,4},... | collective-permute-start | bytes 589832 | tf_op jit(solution)/shard_map/ppermute | solution.py:351
  5.4 5.4 %copy-start = (bf16[768,256]{1,0:T(8,128)(2,1)}, bf16[768,256]{1,0:T(8,128)(2,1)S(1)}, u32[]{:S(2)}) copy-start(bf16[768,256]{1,0:T(8,128)(2,1)S(1)} %get-tuple-element.11.values_ref) | copy-start | bytes 1179652
  10.8 16.6 %all-to-all-start = ((bf16[16,144,128]{2,1,0:T(8,128)(2,1)}), bf16[16,144,128]{2,1,0:T(8,128)(2,1)}, u32[]{:S(2)}, u32[]{:S(2)}) async-start(bf16[16,144,128]{2,1,0:T(8,128)(2,1)} %get-tuple-element.13.after_ref), calls=%async_computation | async-start | bytes 1179648 | tf_op jit(solution)/shard_map/all_to_all | solution.py:355
  15.9 43.6 %collective-permute-start.8 = (bf16[1024,256]{1,0:T(8,128)(2,1)}, bf16[1024,256]{1,0:T(8,128)(2,1)}, u32[]{:S(2)}, u32[]{:S(2)}) collective-permute-start(bf16[1024,256]{1,0:T(8,128)(2,1)} %w_ref.1), channel_id=1, source_target_pairs={{0,8},{8,0},{1,9},{9,1},{2,10},{10,2},{3,11},{11,3},{4,12},{12,4},... | collective-permute-start | bytes 1572872 | tf_op jit(solution)/shard_map/ppermute | solution.py:351
  16.5 1.0 %copy-start.1 = (bf16[768,256]{1,0:T(8,128)(2,1)S(1)}, bf16[768,256]{1,0:T(8,128)(2,1)}, u32[]{:S(2)}) copy-start(bf16[768,256]{1,0:T(8,128)(2,1)} %copy-done) | copy-start | bytes 1179652
  23.4 2.7 %copy-start.2 = (f32[768,2048]{1,0:T(8,128)}, f32[768,2048]{1,0:T(8,128)S(1)}, u32[]{:S(2)}) copy-start(f32[768,2048]{1,0:T(8,128)S(1)} %get-tuple-element.15.acc_ref) | copy-start | bytes 18874372
  29.9 29.6 %all-to-all-start.1 = ((bf16[16,128,128]{2,1,0:T(8,128)(2,1)}), bf16[16,128,128]{2,1,0:T(8,128)(2,1)}, u32[]{:S(2)}, u32[]{:S(2)}) async-start(bf16[16,128,128]{2,1,0:T(8,128)(2,1)} %combine.1.after_ref), calls=%async_computation.1 | async-start | bytes 1048576 | tf_op jit(solution)/shard_map/all_to_all | solution.py:355
  35.3 12.0 %collective-permute-start.2 = (bf16[768,128]{1,0:T(8,128)(2,1)S(1)}, bf16[768,128]{1,0:T(8,128)(2,1)S(1)}, u32[]{:S(2)}, u32[]{:S(2)}) collective-permute-start(bf16[768,128]{1,0:T(8,128)(2,1)S(1)} %get-tuple-element.12.mine_ref), channel_id=1, source_target_pairs={{0,16},{16,0},{32,32},{48,48},{64,64},{80,80},{96,96},{112,112},{1... | collective-permute-start | bytes 589832 | tf_op jit(solution)/shard_map/ppermute | solution.py:365
  38.6 10.9 %collective-permute-start.3 = (bf16[768,128]{1,0:T(8,128)(2,1)S(1)}, bf16[768,128]{1,0:T(8,128)(2,1)S(1)}, u32[]{:S(2)}, u32[]{:S(2)}) collective-permute-start(bf16[768,128]{1,0:T(8,128)(2,1)S(1)} %get-tuple-element.12.mine_ref), channel_id=1, source_target_pairs={{0,32},{16,16},{32,0},{48,48},{64,64},{80,80},{96,96},{112,112},{1... | collective-permute-start | bytes 589832 | tf_op jit(solution)/shard_map/ppermute | solution.py:365
  40.7 12.8 %collective-permute-start.4 = (bf16[768,128]{1,0:T(8,128)(2,1)S(1)}, bf16[768,128]{1,0:T(8,128)(2,1)S(1)}, u32[]{:S(2)}, u32[]{:S(2)}) collective-permute-start(bf16[768,128]{1,0:T(8,128)(2,1)S(1)} %get-tuple-element.12.mine_ref), channel_id=1, source_target_pairs={{0,48},{16,16},{32,32},{48,0},{64,64},{80,80},{96,96},{112,112},{1... | collective-permute-start | bytes 589832 | tf_op jit(solution)/shard_map/ppermute | solution.py:365
  53.6 8.3 %collective-permute-start.5 = (bf16[768,128]{1,0:T(8,128)(2,1)S(1)}, bf16[768,128]{1,0:T(8,128)(2,1)S(1)}, u32[]{:S(2)}, u32[]{:S(2)}) collective-permute-start(bf16[768,128]{1,0:T(8,128)(2,1)S(1)} %pick_x.1.mine_ref), channel_id=1, source_target_pairs={{0,64},{16,80},{32,96},{48,112},{64,0},{80,16},{96,32},{112,48},{1... | collective-permute-start | bytes 589832 | tf_op jit(solution)/shard_map/ppermute | solution.py:365
  55.6 9.5 %collective-permute-start.6 = (bf16[768,128]{1,0:T(8,128)(2,1)S(1)}, bf16[768,128]{1,0:T(8,128)(2,1)}, u32[]{:S(2)}, u32[]{:S(2)}) collective-permute-start(bf16[768,128]{1,0:T(8,128)(2,1)S(1)} %pick_x.1.mine_ref), channel_id=1, source_target_pairs={{0,128},{16,144},{32,160},{48,176},{64,64},{80,80},{96,96},{112,11... | collective-permute-start | bytes 589832 | tf_op jit(solution)/shard_map/ppermute | solution.py:365
  57.5 12.6 %collective-permute-start.7 = (bf16[768,128]{1,0:T(8,128)(2,1)S(1)}, bf16[768,128]{1,0:T(8,128)(2,1)}, u32[]{:S(2)}, u32[]{:S(2)}) collective-permute-start(bf16[768,128]{1,0:T(8,128)(2,1)S(1)} %pick_x.1.mine_ref), channel_id=1, source_target_pairs={{0,192},{16,208},{32,224},{48,240},{64,64},{80,80},{96,96},{112,11... | collective-permute-start | bytes 589832 | tf_op jit(solution)/shard_map/ppermute | solution.py:365
  71.8 9.1 %collective-permute-start.9 = (bf16[768,128]{1,0:T(8,128)(2,1)}, bf16[768,128]{1,0:T(8,128)(2,1)}, u32[]{:S(2)}, u32[]{:S(2)}) collective-permute-start(bf16[768,128]{1,0:T(8,128)(2,1)} %pick_y.1.half_ref), channel_id=1, source_target_pairs={{0,8},{8,0},{1,9},{9,1},{2,10},{10,2},{3,11},{11,3},{4,12},{12,4},... | collective-permute-start | bytes 589832 | tf_op jit(solution)/shard_map/ppermute | solution.py:351
  72.3 21.8 %all-to-all-start.2 = ((bf16[16,32,256]{2,1,0:T(8,128)(2,1)}), bf16[16,32,256]{2,1,0:T(8,128)(2,1)S(1)}, u32[]{:S(2)}, u32[]{:S(2)}) async-start(bf16[16,32,256]{2,1,0:T(8,128)(2,1)} %project.1.after_ref), calls=%async_computation.2 | async-start | bytes 524288 | tf_op jit(solution)/shard_map/all_to_all | solution.py:355
  80.9 2.8 %copy-start.3 = (f32[768,2048]{1,0:T(8,128)S(1)}, f32[768,2048]{1,0:T(8,128)}, u32[]{:S(2)}) copy-start(f32[768,2048]{1,0:T(8,128)} %copy-done.2) | copy-start | bytes 18874372

commit v4 on v0

v4 whole, which is shorter than its diff:
```python
import functools

import jax
import jax.numpy as jnp
from jax import lax
from jax.experimental import pallas as pl
from jax.experimental.pallas import tpu as pltpu
from jax.sharding import Mesh, PartitionSpec as P

HEAD = 128
BLOCK = 768
HEADS = 8
HALF = 256
STATS = HEAD + 16
ANCHOR_ROWS = 48
SEND1 = STATS + ANCHOR_ROWS
SEND2 = HEAD + ANCHOR_ROWS
HIDDEN = 1e30
LOG2_SCALE = 1.4426950408889634 * HEAD ** (-0.5)
BF = jnp.bfloat16
F32 = jnp.float32


def scores_of(q, k):
    return lax.dot_general(q, k, (((1,), (1,)), ((), ())), preferred_element_type=F32) * LOG2_SCALE


def pipelined(count, scores, finish):
    s = scores(0)
    for n in range(count):
        s_next = scores(n + 1) if n + 1 < count else None
        finish(n, s)
        s = s_next


def to_lanes(column):
    r = lax.broadcasted_iota(jnp.int32, (HEAD, HEAD), 0)
    c = lax.broadcasted_iota(jnp.int32, (HEAD, HEAD), 1)
    return jnp.sum(jnp.where(r == c, column, 0.0), axis=0, keepdims=True)


def prep_kernel(q_hbm, k_hbm, v_hbm, q_ref, k_ref, values_ref, v_buf, sems):
    rows = pl.ds(pl.multiple_of(HALF * lax.axis_index("c"), HALF), HALF)
    copies = [
        pltpu.make_async_copy(v_hbm, v_buf, sems.at[0]),
        pltpu.make_async_copy(k_hbm, k_ref, sems.at[1]),
        pltpu.make_async_copy(q_hbm.at[rows, :], q_ref, sems.at[2]),
    ]
    for copy in copies:
        copy.start()
    values_ref[:, HEAD : 2 * HEAD] = jnp.ones((BLOCK, HEAD), BF)
    for copy in copies:
        copy.wait()
    values_ref[:, 0:HEAD] = v_buf[...]


def query_kernel(q_ref, k_ref, values_ref, kp_ref, vp_ref, out_ref, values_p):
    core = lax.axis_index("c")
    values_p[:, 0:HEAD] = vp_ref[...]
    values_p[:, HEAD : 2 * HEAD] = jnp.ones((BLOCK, HEAD), BF)
    row_id = lax.broadcasted_iota(jnp.int32, (16, HEAD), 0)

    def scores(j):
        q = q_ref[:, HEAD * j : HEAD * j + HEAD]
        return scores_of(q, k_ref[...]), scores_of(q, kp_ref[...])

    def finish(j, s):
        peak = jnp.maximum(
            jnp.max(s[0], axis=1, keepdims=True), jnp.max(s[1], axis=1, keepdims=True)
        )
        peak = peak.astype(BF).astype(F32)
        acc = jnp.dot(
            jnp.exp2(s[0] - peak).astype(BF), values_ref[...], preferred_element_type=F32
        ) + jnp.dot(jnp.exp2(s[1] - peak).astype(BF), values_p[...], preferred_element_type=F32)
        total = acc[:, HEAD : HEAD + 1]
        for half in range(2):
            rows = slice(half * HEAD, half * HEAD + HEAD)
            out_ref[2 * j + half, 0:HEAD, :] = acc[rows, 0:HEAD].astype(BF)
            peak_l = to_lanes(peak[rows])
            total_l = to_lanes(total[rows])
            high = total_l.astype(BF).astype(F32)
            stats = jnp.where(row_id == 0, peak_l, 0.0)
            stats = jnp.where(row_id == 1, high, stats)
            stats = jnp.where(row_id == 2, total_l - high, stats)
            out_ref[2 * j + half, HEAD:STATS, :] = stats.astype(BF)
            at = (2 * j + half) * ANCHOR_ROWS
            out_ref[2 * j + half, STATS:SEND1, :] = jnp.where(
                core == 0, k_ref[at : at + ANCHOR_ROWS, :], vp_ref[at : at + ANCHOR_ROWS, :]
            )

    pipelined(HEADS, scores, finish)


def combine_kernel(in_ref, after_ref, out_ref):
    stats = in_ref[:, HEAD:STATS, :].astype(F32)
    peak = stats[:, 0, :]
    total = stats[:, 1, :] + stats[:, 2, :]
    top = jnp.max(peak, axis=0, keepdims=True)
    weight = jnp.exp2(peak - top)
    weight = weight / jnp.sum(weight * total, axis=0, keepdims=True)
    weight_t = jnp.concatenate([weight, jnp.zeros((HEAD - 16, HEAD), F32)], axis=0).T
    out = jnp.zeros((HEAD, HEAD), F32)
    for g in range(16):
        out = out + weight_t[:, g : g + 1] * in_ref[g, 0:HEAD, :].astype(F32)
    out = out.astype(BF)
    anchor = in_ref[0, STATS:SEND1, :]
    for g in range(16):
        out_ref[g, 0:HEAD, :] = out
        out_ref[g, HEAD:SEND2, :] = anchor


def project_kernel(mine_ref, other_ref, w_ref, out_ref, k_hbm, v_hbm, k_ref, v_ref, sems):
    core = lax.axis_index("c")
    for g in range(16):
        rows = slice(g * ANCHOR_ROWS, (g + 1) * ANCHOR_ROWS)
        one, two = mine_ref[g, HEAD:SEND2, :], other_ref[g, HEAD:SEND2, :]
        k_ref[rows, :] = jnp.where(core == 0, one, two)
        v_ref[rows, :] = jnp.where(core == 0, two, one)
    copies = (
        pltpu.make_async_copy(k_ref, k_hbm, sems.at[0]),
        pltpu.make_async_copy(v_ref, v_hbm, sems.at[1]),
    )
    for copy in copies:
        copy.start()
    for ref, owner in ((mine_ref, core), (other_ref, 1 - core)):
        a = jnp.concatenate(
            [
                jnp.concatenate([ref[2 * j + half, 0:HEAD, :] for j in range(HEADS)], axis=1)
                for half in range(2)
            ],
            axis=0,
        )
        y = jnp.dot(a, w_ref[...], preferred_element_type=F32).astype(BF)
        for z in range(4):
            out_ref[4 * owner + z] = y[64 * z : 64 * z + 64, :]
    for copy in copies:
        copy.wait()


def final_kernel(in_ref, out_ref):
    total = in_ref[0].astype(F32)
    for z in range(1, 8):
        total = total + in_ref[z].astype(F32)
    out_ref[...] = total.astype(BF)


EARLY = slice(0, 2 * HEAD)
LATE = slice(2 * HEAD, HEADS * HEAD)


def early_and_late(source, target, sems):
    return [
        pltpu.make_async_copy(source.at[:, cols], target.at[:, cols], sems.at[n])
        for n, cols in enumerate((EARLY, LATE))
    ]


def head_columns(j):
    return pl.ds(pl.multiple_of(HEAD * j, HEAD), HEAD)


def head_loop(scores, finish, s_ref, late, write):
    s_ref[...] = scores(0, 0)

    def body(j, carry):
        @pl.when(j == 1)
        def _():
            for copy in late:
                copy.wait()

        s0 = s_ref[...]
        s1 = scores(j, 1)
        finish(j, 0, s0)
        s2 = scores(j, 2)
        finish(j, 1, s1)
        s_ref[...] = scores(jnp.minimum(j + 1, HEADS - 1), 0)
        finish(j, 2, s2)
        write(j).start()
        return carry

    lax.fori_loop(0, HEADS, body, 0)


def own_kernel(
    q_hbm, k_hbm, v_hbm, after_ref, out_hbm, lse_hbm,
    q_ref, k_ref, values_ref, out_ref, lse_ref, s_ref, v_ref, sems, out_sems,
):
    early, late = early_and_late(q_hbm, q_ref, sems)
    k_copy = pltpu.make_async_copy(k_hbm, k_ref, sems.at[2])
    v_copy = pltpu.make_async_copy(v_hbm, v_ref, sems.at[3])
    for copy in (k_copy, early, v_copy, late):
        copy.start()
    values_ref[:, HEAD : 2 * HEAD] = jnp.ones((BLOCK, HEAD), BF)
    lse_ref[...] = jnp.zeros((BLOCK, HEAD), F32)
    lane = lax.broadcasted_iota(jnp.int32, (HALF, HEAD), 1)
    r = lax.broadcasted_iota(jnp.int32, (HALF, HALF), 0)
    c = lax.broadcasted_iota(jnp.int32, (HALF, HALF), 1)
    for copy in (k_copy, early, v_copy):
        copy.wait()
    values_ref[:, 0:HEAD] = v_ref[...]

    def scores(j, i):
        return scores_of(q_ref[i * HALF : (i + 1) * HALF, head_columns(j)], k_ref[0 : (i + 1) * HALF, :])

    def finish(j, i, s):
        rows = slice(i * HALF, (i + 1) * HALF)
        diagonal = jnp.where(c <= r, s[:, i * HALF :], -HIDDEN)
        s = jnp.concatenate([s[:, 0 : i * HALF], diagonal], axis=1) if i else diagonal
        peak = jnp.max(s, axis=1, keepdims=True)
        p = jnp.exp2(s - peak).astype(BF)
        acc = jnp.dot(p, values_ref[0 : (i + 1) * HALF, :], preferred_element_type=F32)
        total = acc[:, HEAD : 2 * HEAD]
        out_ref[rows, head_columns(j)] = acc[:, 0:HEAD] / total
        lse_ref[rows, :] = jnp.where(lane == j, peak + jnp.log2(total), lse_ref[rows, :])

    def write(j):
        cols = head_columns(j)
        return pltpu.make_async_copy(out_ref.at[:, cols], out_hbm.at[:, cols], out_sems.at[j])

    head_loop(scores, finish, s_ref, [late], write)
    lse_copy = pltpu.make_async_copy(lse_ref, lse_hbm, sems.at[2])
    lse_copy.start()
    for j in range(HEADS):
        write(j).wait()
    lse_copy.wait()


def anchor_kernel(
    q_hbm, k_hbm, v_hbm, own_hbm, lse_hbm, out_hbm,
    q_ref, k_ref, values_ref, own_ref, lse_ref, out_ref, s_ref, v_ref, sems, out_sems,
):
    early, late = early_and_late(q_hbm, q_ref, sems)
    k_copy = pltpu.make_async_copy(k_hbm, k_ref, sems.at[2])
    v_copy = pltpu.make_async_copy(v_hbm, v_ref, sems.at[3])
    own_early, own_late = early_and_late(own_hbm, own_ref, sems.at[4:6])
    lse_copy = pltpu.make_async_copy(lse_hbm, lse_ref, sems.at[6])
    for copy in (k_copy, early, v_copy, lse_copy, own_early, late, own_late):
        copy.start()
    first = jnp.logical_and(
        lax.axis_index("c") == 0,
        jnp.logical_and(lax.axis_index("x") == 0, lax.axis_index("y") == 0),
    )
    lane = lax.broadcasted_iota(jnp.int32, (HALF, HEAD), 1)
    values_ref[:, HEAD : 2 * HEAD] = jnp.ones((BLOCK, HEAD), BF)
    for copy in (k_copy, early, v_copy, lse_copy, own_early):
        copy.wait()
    values_ref[:, 0:HEAD] = v_ref[...]

    def scores(j, i):
        return scores_of(q_ref[i * HALF : (i + 1) * HALF, head_columns(j)], k_ref[...])

    def finish(j, i, s):
        rows = slice(i * HALF, (i + 1) * HALF)
        lse = jnp.sum(jnp.where(lane == j, lse_ref[rows, :], 0.0), axis=1, keepdims=True)
        peak = jnp.maximum(lse, jnp.max(s, axis=1, keepdims=True))
        peak = jnp.where(first, lse, peak)
        p = jnp.exp2(s - jnp.where(first, HIDDEN, peak)).astype(BF)
        acc = jnp.dot(p, values_ref[...], preferred_element_type=F32)
        weight = jnp.exp2(lse - peak)
        mixture = acc[:, 0:HEAD] + weight * own_ref[rows, head_columns(j)]
        out_ref[rows, head_columns(j)] = (mixture / (acc[:, HEAD : 2 * HEAD] + weight)).astype(BF)

    def write(j):
        cols = head_columns(j)
        return pltpu.make_async_copy(out_ref.at[:, cols], out_hbm.at[:, cols], out_sems.at[j])

    head_loop(scores, finish, s_ref, [late, own_late], write)
    for j in range(HEADS):
        write(j).wait()


VMEM = pl.BlockSpec(memory_space=pltpu.VMEM)
HBM = pl.BlockSpec(memory_space=pltpu.HBM)
ANY = pl.BlockSpec(memory_space=pl.ANY)
WIDE = HEADS * HEAD


def in_hbm(*arrays):
    return [pltpu.with_memory_space_constraint(a, pltpu.HBM) for a in arrays]


def shape(dims, dtype=BF):
    return jax.ShapeDtypeStruct(dims, dtype)


def buffer(dims, dtype=BF):
    return pltpu.VMEM(dims, dtype)


def run(kernel, name, operands, in_specs, out_shape, out_specs, scratch, flops, nbytes, exps=0):
    return pl.pallas_call(
        kernel,
        in_specs=in_specs,
        out_specs=out_specs,
        out_shape=out_shape,
        scratch_shapes=scratch,
        compiler_params=pltpu.CompilerParams(vmem_limit_bytes=24 * 1024 * 1024),
        cost_estimate=pl.CostEstimate(flops=flops, bytes_accessed=nbytes, transcendentals=exps),
        name=name,
    )(*operands)


def prep_call(query, k, v):
    return run(
        prep_kernel, "prep", in_hbm(query, k, v), [HBM] * 3,
        (shape((HALF, WIDE)), shape((BLOCK, HEAD)), shape((BLOCK, 2 * HEAD))), (VMEM,) * 3,
        [buffer((BLOCK, HEAD)), pltpu.SemaphoreType.DMA((3,))], 1 << 18, 2 << 20,
    )


def query_call(q, k, values, kp, vp):
    return run(
        query_kernel, "query_attention", (q, k, values, kp, vp), [VMEM] * 5,
        shape((16, SEND1, HEAD)), VMEM, [buffer((BLOCK, 2 * HEAD))],
        4 * 2048 * 1536 * 256, 3 << 20, 2048 * 1536,
    )


def own_call(ctx_query, k, v, after):
    return run(
        own_kernel, "context_own", (*in_hbm(ctx_query, k, v), after), [HBM, HBM, HBM, ANY],
        (pltpu.HBM((BLOCK, WIDE), F32), pltpu.HBM((BLOCK, HEAD), F32)), (HBM, HBM),
        [
            buffer((BLOCK, WIDE)), buffer((BLOCK, HEAD)), buffer((BLOCK, 2 * HEAD)), buffer((BLOCK, WIDE), F32),
            buffer((BLOCK, HEAD), F32), buffer((HALF, HALF), F32), buffer((BLOCK, HEAD)),
            pltpu.SemaphoreType.DMA((4,)), pltpu.SemaphoreType.DMA((HEADS,)),
        ],
        4 * 6144 * 512 * 256, 4 << 20, 6144 * 512,
    )


def anchor_call(ctx_query, k, v, own, lse):
    return run(
        anchor_kernel, "context_anchor", in_hbm(ctx_query, k, v, own, lse), [HBM] * 5,
        shape((BLOCK, WIDE)), HBM,
        [
            buffer((BLOCK, WIDE)), buffer((BLOCK, HEAD)), buffer((BLOCK, 2 * HEAD)), buffer((BLOCK, WIDE), F32),
            buffer((BLOCK, HEAD), F32), buffer((BLOCK, WIDE)), buffer((HALF, BLOCK), F32), buffer((BLOCK, HEAD)),
            pltpu.SemaphoreType.DMA((7,)), pltpu.SemaphoreType.DMA((HEADS,)),
        ],
        4 * 6144 * 768 * 256, 6 << 20, 6144 * 768,
    )


def combine_call(received, after):
    return run(
        combine_kernel, "combine", (received, *in_hbm(after)), [VMEM, HBM],
        shape((16, SEND2, HEAD)), VMEM, [], 1 << 20, 3 << 19,
    )


def project_call(mine, other, w):
    return run(
        project_kernel, "project", (mine, other, w), [VMEM] * 3,
        (shape((8, 64, 256)), pltpu.HBM((BLOCK, HEAD), BF), pltpu.HBM((BLOCK, HEAD), BF)), (VMEM, HBM, HBM),
        [buffer((BLOCK, HEAD)), buffer((BLOCK, HEAD)), pltpu.SemaphoreType.DMA((2,))],
        2 * 512 * 1024 * 256, 2 << 20,
    )


def final_call(received):
    return run(final_kernel, "final_sum", (received,), [VMEM], shape((64, 256)), VMEM, [], 1 << 17, 1 << 18)


def swap(value):
    return lax.ppermute(value, "c", [(0, 1), (1, 0)])


def exchange(value, axes):
    return lax.all_to_all(value, axes, 0, 0, tiled=True)


def per_device(ctx_query, context_key, context_value, query, out_weight):
    key_p, value_p = swap(context_key), swap(context_value)
    q, k, values = prep_call(query, context_key, context_value)
    sent = query_call(q, k, values, key_p, value_p)
    received = exchange(sent, ("y", "x"))
    own, lse = own_call(ctx_query, context_key, context_value, sent)
    gathered = exchange(combine_call(received, lse), ("y", "x"))
    shares, key_a, value_a = project_call(gathered, swap(gathered), out_weight)
    ctx_out = anchor_call(ctx_query, key_a, value_a, own, lse)
    answer = final_call(exchange(shares, "z"))
    return ctx_out, answer


def solution(mesh):
    fine = Mesh(mesh.devices.reshape(4, 4, 2, 8), ("y", "x", "c", "z"))
    hst = ("y", "x", "c")
    in_specs = (P(hst, "z"), P(hst, "z"), P(hst, "z"), P(None, "z"), P("z", hst))
    out_specs = (P(hst, "z"), P("z", hst))
    return jax.shard_map(
        per_device, mesh=fine, in_specs=in_specs, out_specs=out_specs, check_vma=False
    )
```

time: 354 us -> 72.1 us (0.20); the launches traced: 350 us -> 71.8 us
  blocking collectives: 249 us -> 15.8 us
  matrix products: 42.7 us -> 0 us
  Pallas kernels: 0 us -> 29.6 us
  starting transfers between devices: 0.12 us -> 18.9 us
  local copies, waits for them, and re-layouts: 16.2 us -> 0.01 us
  other arithmetic: 14.6 us -> 0 us
  between operations: 13.9 us -> 0.69 us
  loops' own time: 13.2 us -> 0 us
  waiting for transfers between devices: 0.07 us -> 6.77 us
    psum x1 -> x0, blocking collectives: 125 us -> none  [per_device(): lax.psum((denominator * factor, partial_value * factor[..., None]), 'hst')]
    pmax x1 -> x0, blocking collectives: 124 us -> none  [per_device(): global_peak = lax.pmax(row_peak, 'hst')]
    dot_general x19 -> x0, matrix products: 42.7 us -> none  [the longest x8 16.2 us: one_head(): jnp.einsum('qd,kd->qk', q_single, k_single, preferred_element_type=jnp.fl...]
    pallas_call x0 -> x7, Pallas kernels: none -> 29.6 us  [run(): pl.pallas_call(kernel, in_specs=in_specs, out_specs=out_specs, out_shape=...]
    all_to_all x0 -> x1, blocking collectives: none -> 15.8 us  [exchange(): return lax.all_to_all(value, axes, 0, 0, tiled=True)]
    all_to_all x0 -> x2, starting transfers between devices: none -> 13.2 us  [exchange(): return lax.all_to_all(value, axes, 0, 0, tiled=True)]
    another operation x1 -> x0, loops' own time: 13.2 us -> none  [context_heads(): stacked = lax.map(one_head, jnp.arange(head_count, dtype=jnp.int32))]
    reduce_sum x9 -> x0, other arithmetic: 8.23 us -> none  [the longest x8 6.17 us: one_head(): denominator = jnp.sum(weights, axis=1, keepdims=True)]
  transfers between devices with their start and end apart: 3 -> 5, of which waited for: 0 -> 4; matrix products, arithmetic and copies ran while one was open for 17% -> 0% of each run, Pallas kernels for 0% -> 30%
where the time goes in v4:
time: 72.1 us; the launch traced here: 71.8 us
  Pallas kernels  29.6 us (41%)
  starting transfers between devices  18.9 us (26%)
  blocking collectives  15.8 us (22%)
  waiting for transfers between devices  6.77 us (9%)
    pallas_call x7, Pallas kernels, run(): pl.pallas_call(kernel, in_specs=in_specs, out_specs=out_specs, out_shape=...  29.6 us
    all_to_all x1, blocking collectives, exchange(): return lax.all_to_all(value, axes, 0, 0, tiled=True)  15.8 us
    all_to_all x2, starting transfers between devices, exchange(): return lax.all_to_all(value, axes, 0, 0, tiled=True)  13.2 us
    ppermute x3, starting transfers between devices, swap(): return lax.ppermute(value, 'c', [(0, 1), (1, 0)])  5.69 us
    all_to_all x2, waiting for transfers between devices, exchange(): return lax.all_to_all(value, axes, 0, 0, tiled=True)  4.73 us
    ppermute x3, waiting for transfers between devices, swap(): return lax.ppermute(value, 'c', [(0, 1), (1, 0)])  2.05 us
  transfers between devices with their start and end apart: 5, of which 4 were waited for; matrix products, arithmetic and copies ran while one was open for 0% of the time, Pallas kernels for 30%

profile of v4, /device:TPU:1, one launch (start us, length us, event | category | flops | bytes accessed | tf_op | source)
XLA Modules:
  0.0 71.8 jit_solution(7558201072520542712)
XLA Ops:
  0.6 3.3 %collective-permute-start = (bf16[768,128]{1,0:T(8,128)(2,1)}, bf16[768,128]{1,0:T(8,128)(2,1)S(1)}, u32[]{:S(2)}, u32[]{:S(2)}) collective-permute-start(bf16[768,128]{1,0:T(8,128)(2,1)} %k_hbm.3), channel_id=1, source_target_pairs={{0,8},{8,0},{1,9},{9,1},{2,10},{10,2},{3,11},{11,3},{4,12},{12,4},... | collective-permute-start | bytes 589832 | tf_op jit(solution)/shard_map/ppermute | solution.py:366
  4.0 0.1 collective-permute-start.1
  4.1 1.3 %prep.1 = (bf16[256,1024]{1,0:T(8,128)(2,1)S(1)}, bf16[768,128]{1,0:T(8,128)(2,1)S(1)}, bf16[768,256]{1,0:T(8,128)(2,1)S(1)}) custom-call(bf16[512,1024]{1,0:T(8,128)(2,1)} %q_hbm.3, bf16[768,128]{1,0:T(8,128)(2,1)} %k_hbm.3, bf16[768,128]{1,0:T(8,128)(2,1)} %v_hbm.3), custom_call_target="tpu_custom_call" | custom-call | flops 262144 | bytes 2097152 | tf_op jit(solution)/shard_map/prep/pallas_call | solution.py:291
  5.4 0.0 collective-permute-done.kp_ref
  5.4 0.2 collective-permute-done.1.vp_ref
  5.6 5.2 %query_attention.1.after_ref = bf16[16,192,128]{2,1,0:T(8,128)(2,1)} custom-call(bf16[256,1024]{1,0:T(8,128)(2,1)S(1)} %get-tuple-element.10.q_ref, bf16[768,128]{1,0:T(8,128)(2,1)S(1)} %get-tuple-element.11.k_ref, bf16[768,256]{1,0:T(8,128)(2,1)S(1)} %get-tuple-element.12.values_ref, bf16[768,128]{1,0:T(8,128)(2,1)S(1)} %collective-permute-done.kp_ref, ...), custom_call_target="tpu_custom_call" | custom-call | flops 3221225472 | bytes 3145728 | tf_op jit(solution)/shard_map/query_attention/pallas_call | solution.py:291
  10.8 5.0 %all-to-all-start = ((bf16[16,192,128]{2,1,0:T(8,128)(2,1)}), bf16[16,192,128]{2,1,0:T(8,128)(2,1)S(1)}, u32[]{:S(2)}, u32[]{:S(2)}) async-start(bf16[16,192,128]{2,1,0:T(8,128)(2,1)} %query_attention.1.after_ref), calls=%async_computation | async-start | bytes 1572864 | tf_op jit(solution)/shard_map/all_to_all | solution.py:370
  15.9 9.1 %context_own.1 = (f32[768,1024]{1,0:T(8,128)}, f32[768,128]{1,0:T(8,128)}) custom-call(bf16[768,1024]{1,0:T(8,128)(2,1)} %q_hbm.5, bf16[768,128]{1,0:T(8,128)(2,1)} %k_hbm.3, bf16[768,128]{1,0:T(8,128)(2,1)} %v_hbm.3, bf16[16,192,128]{2,1,0:T(8,128)(2,1)} %query_attention.1.after_ref), custom_call_target="tpu_custom_call" | custom-call | flops 3221225472 | bytes 4194304 | tf_op jit(solution)/shard_map/context_own/pallas_call | solution.py:291
  24.9 4.5 %all-to-all-done.in_ref = bf16[16,192,128]{2,1,0:T(8,128)(2,1)S(1)} async-done(((bf16[16,192,128]{2,1,0:T(8,128)(2,1)}), bf16[16,192,128]{2,1,0:T(8,128)(2,1)S(1)}, u32[]{:S(2)}, u32[]{:S(2)}) %all-to-all-start) | async-done | bytes 786464 | tf_op jit(solution)/shard_map/all_to_all | solution.py:370
  29.5 0.0 copy-start
  29.5 0.5 combine.1
  30.1 15.8 %all_to_all.15.mine_ref = bf16[16,176,128]{2,1,0:T(8,128)(2,1)S(1)} all-to-all(bf16[16,176,128]{2,1,0:T(8,128)(2,1)S(1)} %combine.1), channel_id=1, replica_groups=mesh['y'=4,'x'=4,'c'=2,'z'=8] {'y','x'}, dimensions={0} | all-to-all | bytes 1441792 | tf_op jit(solution)/shard_map/all_to_all | solution.py:370
  45.8 2.3 %collective-permute-start.2 = (bf16[16,176,128]{2,1,0:T(8,128)(2,1)S(1)}, bf16[16,176,128]{2,1,0:T(8,128)(2,1)S(1)}, u32[]{:S(2)}, u32[]{:S(2)}) collective-permute-start(bf16[16,176,128]{2,1,0:T(8,128)(2,1)S(1)} %all_to_all.15.mine_ref), channel_id=1, source_target_pairs={{0,8},{8,0},{1,9},{9,1},{2,10},{10,2},{3,11},{11,3},{4,12},{12,4},... | collective-permute-start | bytes 2162696 | tf_op jit(solution)/shard_map/ppermute | solution.py:366
  48.1 1.8 %collective-permute-done.2.other_ref = bf16[16,176,128]{2,1,0:T(8,128)(2,1)S(1)} collective-permute-done((bf16[16,176,128]{2,1,0:T(8,128)(2,1)S(1)}, bf16[16,176,128]{2,1,0:T(8,128)(2,1)S(1)}, u32[]{:S(2)}, u32[]{:S(2)}) %collective-permute-start.2) | collective-permute-done | bytes 720928 | tf_op jit(solution)/shard_map/ppermute | solution.py:366
  49.9 0.0 copy-done
  49.9 1.9 %project.1 = (bf16[8,64,256]{2,1,0:T(8,128)(2,1)}, bf16[768,128]{1,0:T(8,128)(2,1)}, bf16[768,128]{1,0:T(8,128)(2,1)}) custom-call(bf16[16,176,128]{2,1,0:T(8,128)(2,1)S(1)} %all_to_all.15.mine_ref, bf16[16,176,128]{2,1,0:T(8,128)(2,1)S(1)} %collective-permute-done.2.other_ref, bf16[1024,256]{1,0:T(8,128)(2,1)S(1)} %copy-done), custom_call_target="tpu_custom_call" | custom-call | flops 268435456 | bytes 2097152 | tf_op jit(solution)/shard_map/project/pallas_call | solution.py:291
  51.8 8.2 %all-to-all-start.2 = ((bf16[8,64,256]{2,1,0:T(8,128)(2,1)}), bf16[8,64,256]{2,1,0:T(8,128)(2,1)S(1)}, u32[]{:S(2)}, u32[]{:S(2)}) async-start(bf16[8,64,256]{2,1,0:T(8,128)(2,1)} %get-tuple-element.17), calls=%async_computation.2 | async-start | bytes 524288 | tf_op jit(solution)/shard_map/all_to_all | solution.py:370
  60.0 10.9 %context_anchor.1 = bf16[768,1024]{1,0:T(8,128)(2,1)} custom-call(bf16[768,1024]{1,0:T(8,128)(2,1)} %q_hbm.5, bf16[768,128]{1,0:T(8,128)(2,1)} %get-tuple-element.14.k_hbm, bf16[768,128]{1,0:T(8,128)(2,1)} %get-tuple-element.15.v_hbm, f32[768,1024]{1,0:T(8,128)} %get-tuple-element.16.own_hbm, f32[768,128]{1,0:T(8,128)} %get-tuple-element.13.after_ref.lse_hbm), custom_call_target="tpu_custom_call" | custom-call | flops 4831838208 | bytes 6291456 | tf_op jit(solution)/shard_map/context_anchor/pallas_call | solution.py:291
  70.9 0.2 all-to-all-done.2.in_ref
  71.1 0.7 final_sum.1
Async XLA Ops:
  0.6 4.7 %collective-permute-start = (bf16[768,128]{1,0:T(8,128)(2,1)}, bf16[768,128]{1,0:T(8,128)(2,1)S(1)}, u32[]{:S(2)}, u32[]{:S(2)}) collective-permute-start(bf16[768,128]{1,0:T(8,128)(2,1)} %k_hbm.3), channel_id=1, source_target_pairs={{0,8},{8,0},{1,9},{9,1},{2,10},{10,2},{3,11},{11,3},{4,12},{12,4},... | collective-permute-start | bytes 589832 | tf_op jit(solution)/shard_map/ppermute | solution.py:366
  4.0 1.7 %collective-permute-start.1 = (bf16[768,128]{1,0:T(8,128)(2,1)}, bf16[768,128]{1,0:T(8,128)(2,1)S(1)}, u32[]{:S(2)}, u32[]{:S(2)}) collective-permute-start(bf16[768,128]{1,0:T(8,128)(2,1)} %v_hbm.3), channel_id=1, source_target_pairs={{0,8},{8,0},{1,9},{9,1},{2,10},{10,2},{3,11},{11,3},{4,12},{12,4},... | collective-permute-start | bytes 589832 | tf_op jit(solution)/shard_map/ppermute | solution.py:366
  10.8 18.7 %all-to-all-start = ((bf16[16,192,128]{2,1,0:T(8,128)(2,1)}), bf16[16,192,128]{2,1,0:T(8,128)(2,1)S(1)}, u32[]{:S(2)}, u32[]{:S(2)}) async-start(bf16[16,192,128]{2,1,0:T(8,128)(2,1)} %query_attention.1.after_ref), calls=%async_computation | async-start | bytes 1572864 | tf_op jit(solution)/shard_map/all_to_all | solution.py:370
  29.5 20.4 %copy-start = (bf16[1024,256]{1,0:T(8,128)(2,1)S(1)}, bf16[1024,256]{1,0:T(8,128)(2,1)}, u32[]{:S(2)}) copy-start(bf16[1024,256]{1,0:T(8,128)(2,1)} %w_ref.1) | copy-start | bytes 1572868
  45.8 4.1 %collective-permute-start.2 = (bf16[16,176,128]{2,1,0:T(8,128)(2,1)S(1)}, bf16[16,176,128]{2,1,0:T(8,128)(2,1)S(1)}, u32[]{:S(2)}, u32[]{:S(2)}) collective-permute-start(bf16[16,176,128]{2,1,0:T(8,128)(2,1)S(1)} %all_to_all.15.mine_ref), channel_id=1, source_target_pairs={{0,8},{8,0},{1,9},{9,1},{2,10},{10,2},{3,11},{11,3},{4,12},{12,4},... | collective-permute-start | bytes 2162696 | tf_op jit(solution)/shard_map/ppermute | solution.py:366
  51.8 19.3 %all-to-all-start.2 = ((bf16[8,64,256]{2,1,0:T(8,128)(2,1)}), bf16[8,64,256]{2,1,0:T(8,128)(2,1)S(1)}, u32[]{:S(2)}, u32[]{:S(2)}) async-start(bf16[8,64,256]{2,1,0:T(8,128)(2,1)} %get-tuple-element.17), calls=%async_computation.2 | async-start | bytes 524288 | tf_op jit(solution)/shard_map/all_to_all | solution.py:370

commit v5 on v4

--- a/solution.py
+++ b/solution.py
@@ -144,135 +144,84 @@
     out_ref[...] = total.astype(BF)
 
 
-EARLY = slice(0, 2 * HEAD)
-LATE = slice(2 * HEAD, HEADS * HEAD)
-
-
-def early_and_late(source, target, sems):
-    return [
-        pltpu.make_async_copy(source.at[:, cols], target.at[:, cols], sems.at[n])
-        for n, cols in enumerate((EARLY, LATE))
-    ]
-
-
-def head_columns(j):
-    return pl.ds(pl.multiple_of(HEAD * j, HEAD), HEAD)
-
-
-def head_loop(scores, finish, s_ref, late, write):
-    s_ref[...] = scores(0, 0)
-
-    def body(j, carry):
-        @pl.when(j == 1)
-        def _():
-            for copy in late:
-                copy.wait()
-
-        s0 = s_ref[...]
-        s1 = scores(j, 1)
-        finish(j, 0, s0)
-        s2 = scores(j, 2)
-        finish(j, 1, s1)
-        s_ref[...] = scores(jnp.minimum(j + 1, HEADS - 1), 0)
-        finish(j, 2, s2)
-        write(j).start()
-        return carry
-
-    lax.fori_loop(0, HEADS, body, 0)
-
-
-def own_kernel(
-    q_hbm, k_hbm, v_hbm, after_ref, out_hbm, lse_hbm,
-    q_ref, k_ref, values_ref, out_ref, lse_ref, s_ref, v_ref, sems, out_sems,
-):
-    early, late = early_and_late(q_hbm, q_ref, sems)
-    k_copy = pltpu.make_async_copy(k_hbm, k_ref, sems.at[2])
-    v_copy = pltpu.make_async_copy(v_hbm, v_ref, sems.at[3])
-    for copy in (k_copy, early, v_copy, late):
-        copy.start()
-    values_ref[:, HEAD : 2 * HEAD] = jnp.ones((BLOCK, HEAD), BF)
-    lse_ref[...] = jnp.zeros((BLOCK, HEAD), F32)
+STEP = 2
+STEP_COLUMNS = STEP * HEAD
+
+
+def fill_values(v_ref, values_ref):
+    @pl.when(pl.program_id(0) == 0)
+    def _():
+        values_ref[:, 0:HEAD] = v_ref[...]
+        values_ref[:, HEAD : 2 * HEAD] = jnp.ones((BLOCK, HEAD), BF)
+
+
+def own_kernel(q_ref, k_ref, v_ref, after_ref, out_ref, lse_ref, values_ref):
+    fill_values(v_ref, values_ref)
+
+    @pl.when(pl.program_id(0) == 0)
+    def _():
+        lse_ref[...] = jnp.zeros((BLOCK, HEAD), F32)
+
     lane = lax.broadcasted_iota(jnp.int32, (HALF, HEAD), 1)
     r = lax.broadcasted_iota(jnp.int32, (HALF, HALF), 0)
     c = lax.broadcasted_iota(jnp.int32, (HALF, HALF), 1)
-    for copy in (k_copy, early, v_copy):
-        copy.wait()
-    values_ref[:, 0:HEAD] = v_ref[...]
-
-    def scores(j, i):
-        return scores_of(q_ref[i * HALF : (i + 1) * HALF, head_columns(j)], k_ref[0 : (i + 1) * HALF, :])
-
-    def finish(j, i, s):
-        rows = slice(i * HALF, (i + 1) * HALF)
-        diagonal = jnp.where(c <= r, s[:, i * HALF :], -HIDDEN)
-        s = jnp.concatenate([s[:, 0 : i * HALF], diagonal], axis=1) if i else diagonal
-        peak = jnp.max(s, axis=1, keepdims=True)
-        p = jnp.exp2(s - peak).astype(BF)
-        acc = jnp.dot(p, values_ref[0 : (i + 1) * HALF, :], preferred_element_type=F32)
-        total = acc[:, HEAD : 2 * HEAD]
-        out_ref[rows, head_columns(j)] = acc[:, 0:HEAD] / total
-        lse_ref[rows, :] = jnp.where(lane == j, peak + jnp.log2(total), lse_ref[rows, :])
-
-    def write(j):
-        cols = head_columns(j)
-        return pltpu.make_async_copy(out_ref.at[:, cols], out_hbm.at[:, cols], out_sems.at[j])
-
-    head_loop(scores, finish, s_ref, [late], write)
-    lse_copy = pltpu.make_async_copy(lse_ref, lse_hbm, sems.at[2])
-    lse_copy.start()
-    for j in range(HEADS):
-        write(j).wait()
-    lse_copy.wait()
-
-
-def anchor_kernel(
-    q_hbm, k_hbm, v_hbm, own_hbm, lse_hbm, out_hbm,
-    q_ref, k_ref, values_ref, own_ref, lse_ref, out_ref, s_ref, v_ref, sems, out_sems,
-):
-    early, late = early_and_late(q_hbm, q_ref, sems)
-    k_copy = pltpu.make_async_copy(k_hbm, k_ref, sems.at[2])
-    v_copy = pltpu.make_async_copy(v_hbm, v_ref, sems.at[3])
-    own_early, own_late = early_and_late(own_hbm, own_ref, sems.at[4:6])
-    lse_copy = pltpu.make_async_copy(lse_hbm, lse_ref, sems.at[6])
-    for copy in (k_copy, early, v_copy, lse_copy, own_early, late, own_late):
-        copy.start()
+
+    def scores(h):
+        return [
+            scores_of(q_ref[i * HALF : (i + 1) * HALF, HEAD * h : HEAD * h + HEAD], k_ref[0 : (i + 1) * HALF, :])
+            for i in range(3)
+        ]
+
+    def finish(h, s):
+        head = pl.program_id(0) * STEP + h
+        parts, peaks = [], []
+        for i in range(3):
+            diagonal = jnp.where(c <= r, s[i][:, i * HALF :], -HIDDEN)
+            part = jnp.concatenate([s[i][:, 0 : i * HALF], diagonal], axis=1) if i else diagonal
+            parts.append(part)
+            peaks.append(jnp.max(part, axis=1, keepdims=True))
+        for i in range(3):
+            rows = slice(i * HALF, (i + 1) * HALF)
+            p = jnp.exp2(parts[i] - peaks[i]).astype(BF)
+            acc = jnp.dot(p, values_ref[0 : (i + 1) * HALF, :], preferred_element_type=F32)
+            total = acc[:, HEAD : 2 * HEAD]
+            out_ref[rows, HEAD * h : HEAD * h + HEAD] = (acc[:, 0:HEAD] / total).astype(BF)
+            lse_ref[rows, :] = jnp.where(lane == head, peaks[i] + jnp.log2(total), lse_ref[rows, :])
+
+    pipelined(STEP, scores, finish)
+
+
+def anchor_kernel(q_ref, k_ref, v_ref, own_ref, lse_ref, out_ref, values_ref):
+    fill_values(v_ref, values_ref)
     first = jnp.logical_and(
         lax.axis_index("c") == 0,
         jnp.logical_and(lax.axis_index("x") == 0, lax.axis_index("y") == 0),
     )
-    lane = lax.broadcasted_iota(jnp.int32, (HALF, HEAD), 1)
-    values_ref[:, HEAD : 2 * HEAD] = jnp.ones((BLOCK, HEAD), BF)
-    for copy in (k_copy, early, v_copy, lse_copy, own_early):
-        copy.wait()
-    values_ref[:, 0:HEAD] = v_ref[...]
-
-    def scores(j, i):
-        return scores_of(q_ref[i * HALF : (i + 1) * HALF, head_columns(j)], k_ref[...])
-
-    def finish(j, i, s):
-        rows = slice(i * HALF, (i + 1) * HALF)
-        lse = jnp.sum(jnp.where(lane == j, lse_ref[rows, :], 0.0), axis=1, keepdims=True)
+    lane = lax.broadcasted_iota(jnp.int32, (BLOCK, HEAD), 1)
+
+    def scores(h):
+        return scores_of(q_ref[:, HEAD * h : HEAD * h + HEAD], k_ref[...])
+
+    def finish(h, s):
+        head = pl.program_id(0) * STEP + h
+        lse = jnp.sum(jnp.where(lane == head, lse_ref[...], 0.0), axis=1, keepdims=True)
         peak = jnp.maximum(lse, jnp.max(s, axis=1, keepdims=True))
         peak = jnp.where(first, lse, peak)
         p = jnp.exp2(s - jnp.where(first, HIDDEN, peak)).astype(BF)
         acc = jnp.dot(p, values_ref[...], preferred_element_type=F32)
         weight = jnp.exp2(lse - peak)
-        mixture = acc[:, 0:HEAD] + weight * own_ref[rows, head_columns(j)]
-        out_ref[rows, head_columns(j)] = (mixture / (acc[:, HEAD : 2 * HEAD] + weight)).astype(BF)
-
-    def write(j):
-        cols = head_columns(j)
-        return pltpu.make_async_copy(out_ref.at[:, cols], out_hbm.at[:, cols], out_sems.at[j])
-
-    head_loop(scores, finish, s_ref, [late, own_late], write)
-    for j in range(HEADS):
-        write(j).wait()
+        mixture = acc[:, 0:HEAD] + weight * own_ref[:, HEAD * h : HEAD * h + HEAD].astype(F32)
+        out_ref[:, HEAD * h : HEAD * h + HEAD] = (mixture / (acc[:, HEAD : 2 * HEAD] + weight)).astype(BF)
+
+    pipelined(STEP, scores, finish)
 
 
 VMEM = pl.BlockSpec(memory_space=pltpu.VMEM)
 HBM = pl.BlockSpec(memory_space=pltpu.HBM)
 ANY = pl.BlockSpec(memory_space=pl.ANY)
 WIDE = HEADS * HEAD
+STEP_BLOCK = pl.BlockSpec((BLOCK, STEP_COLUMNS), lambda t: (0, t))
+HEAD_BLOCK = pl.BlockSpec((BLOCK, HEAD), lambda t: (0, 0))
 
 
 def in_hbm(*arrays):
@@ -287,9 +236,10 @@
     return pltpu.VMEM(dims, dtype)
 
 
-def run(kernel, name, operands, in_specs, out_shape, out_specs, scratch, flops, nbytes, exps=0):
+def run(kernel, name, operands, in_specs, out_shape, out_specs, scratch, flops, nbytes, exps=0, grid=()):
     return pl.pallas_call(
         kernel,
+        grid=grid,
         in_specs=in_specs,
         out_specs=out_specs,
         out_shape=out_shape,
@@ -318,27 +268,19 @@
 
 def own_call(ctx_query, k, v, after):
     return run(
-        own_kernel, "context_own", (*in_hbm(ctx_query, k, v), after), [HBM, HBM, HBM, ANY],
-        (pltpu.HBM((BLOCK, WIDE), F32), pltpu.HBM((BLOCK, HEAD), F32)), (HBM, HBM),
-        [
-            buffer((BLOCK, WIDE)), buffer((BLOCK, HEAD)), buffer((BLOCK, 2 * HEAD)), buffer((BLOCK, WIDE), F32),
-            buffer((BLOCK, HEAD), F32), buffer((HALF, HALF), F32), buffer((BLOCK, HEAD)),
-            pltpu.SemaphoreType.DMA((4,)), pltpu.SemaphoreType.DMA((HEADS,)),
-        ],
-        4 * 6144 * 512 * 256, 4 << 20, 6144 * 512,
+        own_kernel, "context_own", (*in_hbm(ctx_query, k, v), after),
+        [STEP_BLOCK, HEAD_BLOCK, HEAD_BLOCK, ANY],
+        (pltpu.HBM((BLOCK, WIDE), BF), pltpu.HBM((BLOCK, HEAD), F32)), (STEP_BLOCK, HEAD_BLOCK),
+        [buffer((BLOCK, 2 * HEAD))], 4 * 6144 * 512 * 256, 4 << 20, 6144 * 512, grid=(HEADS // STEP,),
     )
 
 
 def anchor_call(ctx_query, k, v, own, lse):
     return run(
-        anchor_kernel, "context_anchor", in_hbm(ctx_query, k, v, own, lse), [HBM] * 5,
-        shape((BLOCK, WIDE)), HBM,
-        [
-            buffer((BLOCK, WIDE)), buffer((BLOCK, HEAD)), buffer((BLOCK, 2 * HEAD)), buffer((BLOCK, WIDE), F32),
-            buffer((BLOCK, HEAD), F32), buffer((BLOCK, WIDE)), buffer((HALF, BLOCK), F32), buffer((BLOCK, HEAD)),
-            pltpu.SemaphoreType.DMA((7,)), pltpu.SemaphoreType.DMA((HEADS,)),
-        ],
-        4 * 6144 * 768 * 256, 6 << 20, 6144 * 768,
+        anchor_kernel, "context_anchor", in_hbm(ctx_query, k, v, own, lse),
+        [STEP_BLOCK, HEAD_BLOCK, HEAD_BLOCK, STEP_BLOCK, HEAD_BLOCK],
+        shape((BLOCK, WIDE)), STEP_BLOCK,
+        [buffer((BLOCK, 2 * HEAD))], 4 * 6144 * 768 * 256, 6 << 20, 6144 * 768, grid=(HEADS // STEP,),
     )
 
 

time: 72.1 us -> 72.2 us (level)
  waiting for transfers between devices: 6.77 us -> 9.41 us
  Pallas kernels: 29.6 us -> 27 us
    all_to_all x2, waiting for transfers between devices: 4.73 us -> 7.36 us  [exchange(): return lax.all_to_all(value, axes, 0, 0, tiled=True)]
    pallas_call x7, Pallas kernels: 29.6 us -> 27 us  [run(): pl.pallas_call(kernel, grid=grid, in_specs=in_specs, out_specs=out_specs,...]
  transfers between devices with their start and end apart: 5 -> 5, of which waited for: 4 -> 4; matrix products, arithmetic and copies ran while one was open for 0% -> 0% of each run, Pallas kernels for 30% -> 26%
where the time goes in v5:
time: 72.2 us; the launch traced here: 71.8 us
  Pallas kernels  27 us (37%)
  starting transfers between devices  18.9 us (26%)
  blocking collectives  15.8 us (22%)
  waiting for transfers between devices  9.41 us (13%)
    pallas_call x7, Pallas kernels, run(): pl.pallas_call(kernel, grid=grid, in_specs=in_specs, out_specs=out_specs,...  27 us
    all_to_all x1, blocking collectives, exchange(): return lax.all_to_all(value, axes, 0, 0, tiled=True)  15.8 us
    all_to_all x2, starting transfers between devices, exchange(): return lax.all_to_all(value, axes, 0, 0, tiled=True)  13.2 us
    all_to_all x2, waiting for transfers between devices, exchange(): return lax.all_to_all(value, axes, 0, 0, tiled=True)  7.36 us
    ppermute x3, starting transfers between devices, swap(): return lax.ppermute(value, 'c', [(0, 1), (1, 0)])  5.69 us
    ppermute x3, waiting for transfers between devices, swap(): return lax.ppermute(value, 'c', [(0, 1), (1, 0)])  2.05 us
  transfers between devices with their start and end apart: 5, of which 4 were waited for; matrix products, arithmetic and copies ran while one was open for 0% of the time, Pallas kernels for 26%

profile of v5, /device:TPU:1, one launch (start us, length us, event | category | flops | bytes accessed | tf_op | source)
XLA Modules:
  0.0 71.8 jit_solution(17398739200557484193)
XLA Ops:
  0.6 3.3 %collective-permute-start = (bf16[768,128]{1,0:T(8,128)(2,1)}, bf16[768,128]{1,0:T(8,128)(2,1)S(1)}, u32[]{:S(2)}, u32[]{:S(2)}) collective-permute-start(bf16[768,128]{1,0:T(8,128)(2,1)} %k_ref.1), channel_id=1, source_target_pairs={{0,8},{8,0},{1,9},{9,1},{2,10},{10,2},{3,11},{11,3},{4,12},{12,4},... | collective-permute-start | bytes 589832 | tf_op jit(solution)/shard_map/ppermute | solution.py:308
  4.0 0.1 collective-permute-start.1
  4.1 1.3 %prep.1 = (bf16[256,1024]{1,0:T(8,128)(2,1)S(1)}, bf16[768,128]{1,0:T(8,128)(2,1)S(1)}, bf16[768,256]{1,0:T(8,128)(2,1)S(1)}) custom-call(bf16[512,1024]{1,0:T(8,128)(2,1)} %q_hbm.1, bf16[768,128]{1,0:T(8,128)(2,1)} %k_ref.1, bf16[768,128]{1,0:T(8,128)(2,1)} %v_ref.1), custom_call_target="tpu_custom_call" | custom-call | flops 262144 | bytes 2097152 | tf_op jit(solution)/shard_map/prep/pallas_call | solution.py:240
  5.4 0.0 collective-permute-done.kp_ref
  5.4 0.2 collective-permute-done.1.vp_ref
  5.6 5.2 %query_attention.1.after_ref = bf16[16,192,128]{2,1,0:T(8,128)(2,1)} custom-call(bf16[256,1024]{1,0:T(8,128)(2,1)S(1)} %get-tuple-element.10.q_ref, bf16[768,128]{1,0:T(8,128)(2,1)S(1)} %get-tuple-element.11.k_ref, bf16[768,256]{1,0:T(8,128)(2,1)S(1)} %get-tuple-element.12.values_ref, bf16[768,128]{1,0:T(8,128)(2,1)S(1)} %collective-permute-done.kp_ref, ...), custom_call_target="tpu_custom_call" | custom-call | flops 3221225472 | bytes 3145728 | tf_op jit(solution)/shard_map/query_attention/pallas_call | solution.py:240
  10.8 5.0 %all-to-all-start = ((bf16[16,192,128]{2,1,0:T(8,128)(2,1)}), bf16[16,192,128]{2,1,0:T(8,128)(2,1)S(1)}, u32[]{:S(2)}, u32[]{:S(2)}) async-start(bf16[16,192,128]{2,1,0:T(8,128)(2,1)} %query_attention.1.after_ref), calls=%async_computation | async-start | bytes 1572864 | tf_op jit(solution)/shard_map/all_to_all | solution.py:312
  15.9 7.5 %context_own.1 = (bf16[768,1024]{1,0:T(8,128)(2,1)}, f32[768,128]{1,0:T(8,128)}) custom-call(bf16[768,1024]{1,0:T(8,128)(2,1)} %q_ref.3, bf16[768,128]{1,0:T(8,128)(2,1)} %k_ref.1, bf16[768,128]{1,0:T(8,128)(2,1)} %v_ref.1, bf16[16,192,128]{2,1,0:T(8,128)(2,1)} %query_attention.1.after_ref), custom_call_target="tpu_custom_call" | custom-call | flops 3221225472 | bytes 4194304 | tf_op jit(solution)/shard_map/context_own/pallas_call | solution.py:240
  23.4 6.1 %all-to-all-done.in_ref = bf16[16,192,128]{2,1,0:T(8,128)(2,1)S(1)} async-done(((bf16[16,192,128]{2,1,0:T(8,128)(2,1)}), bf16[16,192,128]{2,1,0:T(8,128)(2,1)S(1)}, u32[]{:S(2)}, u32[]{:S(2)}) %all-to-all-start) | async-done | bytes 786464 | tf_op jit(solution)/shard_map/all_to_all | solution.py:312
  29.5 0.0 copy-start
  29.5 0.5 combine.1
  30.1 15.8 %all_to_all.15.mine_ref = bf16[16,176,128]{2,1,0:T(8,128)(2,1)S(1)} all-to-all(bf16[16,176,128]{2,1,0:T(8,128)(2,1)S(1)} %combine.1), channel_id=1, replica_groups=mesh['y'=4,'x'=4,'c'=2,'z'=8] {'y','x'}, dimensions={0} | all-to-all | bytes 1441792 | tf_op jit(solution)/shard_map/all_to_all | solution.py:312
  45.8 2.3 %collective-permute-start.2 = (bf16[16,176,128]{2,1,0:T(8,128)(2,1)S(1)}, bf16[16,176,128]{2,1,0:T(8,128)(2,1)S(1)}, u32[]{:S(2)}, u32[]{:S(2)}) collective-permute-start(bf16[16,176,128]{2,1,0:T(8,128)(2,1)S(1)} %all_to_all.15.mine_ref), channel_id=1, source_target_pairs={{0,8},{8,0},{1,9},{9,1},{2,10},{10,2},{3,11},{11,3},{4,12},{12,4},... | collective-permute-start | bytes 2162696 | tf_op jit(solution)/shard_map/ppermute | solution.py:308
  48.1 1.8 %collective-permute-done.2.other_ref = bf16[16,176,128]{2,1,0:T(8,128)(2,1)S(1)} collective-permute-done((bf16[16,176,128]{2,1,0:T(8,128)(2,1)S(1)}, bf16[16,176,128]{2,1,0:T(8,128)(2,1)S(1)}, u32[]{:S(2)}, u32[]{:S(2)}) %collective-permute-start.2) | collective-permute-done | bytes 720928 | tf_op jit(solution)/shard_map/ppermute | solution.py:308
  49.9 0.0 copy-done
  49.9 1.9 %project.1 = (bf16[8,64,256]{2,1,0:T(8,128)(2,1)}, bf16[768,128]{1,0:T(8,128)(2,1)}, bf16[768,128]{1,0:T(8,128)(2,1)}) custom-call(bf16[16,176,128]{2,1,0:T(8,128)(2,1)S(1)} %all_to_all.15.mine_ref, bf16[16,176,128]{2,1,0:T(8,128)(2,1)S(1)} %collective-permute-done.2.other_ref, bf16[1024,256]{1,0:T(8,128)(2,1)S(1)} %copy-done), custom_call_target="tpu_custom_call" | custom-call | flops 268435456 | bytes 2097152 | tf_op jit(solution)/shard_map/project/pallas_call | solution.py:240
  51.8 8.2 %all-to-all-start.2 = ((bf16[8,64,256]{2,1,0:T(8,128)(2,1)}), bf16[8,64,256]{2,1,0:T(8,128)(2,1)S(1)}, u32[]{:S(2)}, u32[]{:S(2)}) async-start(bf16[8,64,256]{2,1,0:T(8,128)(2,1)} %get-tuple-element.17), calls=%async_computation.2 | async-start | bytes 524288 | tf_op jit(solution)/shard_map/all_to_all | solution.py:312
  60.0 9.9 %context_anchor.1 = bf16[768,1024]{1,0:T(8,128)(2,1)} custom-call(bf16[768,1024]{1,0:T(8,128)(2,1)} %q_ref.3, bf16[768,128]{1,0:T(8,128)(2,1)} %get-tuple-element.14.k_ref, bf16[768,128]{1,0:T(8,128)(2,1)} %get-tuple-element.15.v_ref, bf16[768,1024]{1,0:T(8,128)(2,1)} %get-tuple-element.16.own_ref, f32[768,128]{1,0:T(8,128)} %get-tuple-element.13.after_ref.lse_ref), custom_call_target="tpu_custom_call" | custom-call | flops 4831838208 | bytes 6291456 | tf_op jit(solution)/shard_map/context_anchor/pallas_call | solution.py:240
  69.9 1.2 %all-to-all-done.2.in_ref = bf16[8,64,256]{2,1,0:T(8,128)(2,1)S(1)} async-done(((bf16[8,64,256]{2,1,0:T(8,128)(2,1)}), bf16[8,64,256]{2,1,0:T(8,128)(2,1)S(1)}, u32[]{:S(2)}, u32[]{:S(2)}) %all-to-all-start.2) | async-done | bytes 262176 | tf_op jit(solution)/shard_map/all_to_all | solution.py:312
  71.1 0.7 final_sum.1
Async XLA Ops:
  0.6 4.7 %collective-permute-start = (bf16[768,128]{1,0:T(8,128)(2,1)}, bf16[768,128]{1,0:T(8,128)(2,1)S(1)}, u32[]{:S(2)}, u32[]{:S(2)}) collective-permute-start(bf16[768,128]{1,0:T(8,128)(2,1)} %k_ref.1), channel_id=1, source_target_pairs={{0,8},{8,0},{1,9},{9,1},{2,10},{10,2},{3,11},{11,3},{4,12},{12,4},... | collective-permute-start | bytes 589832 | tf_op jit(solution)/shard_map/ppermute | solution.py:308
  4.0 1.7 %collective-permute-start.1 = (bf16[768,128]{1,0:T(8,128)(2,1)}, bf16[768,128]{1,0:T(8,128)(2,1)S(1)}, u32[]{:S(2)}, u32[]{:S(2)}) collective-permute-start(bf16[768,128]{1,0:T(8,128)(2,1)} %v_ref.1), channel_id=1, source_target_pairs={{0,8},{8,0},{1,9},{9,1},{2,10},{10,2},{3,11},{11,3},{4,12},{12,4},... | collective-permute-start | bytes 589832 | tf_op jit(solution)/shard_map/ppermute | solution.py:308
  10.8 18.7 %all-to-all-start = ((bf16[16,192,128]{2,1,0:T(8,128)(2,1)}), bf16[16,192,128]{2,1,0:T(8,128)(2,1)S(1)}, u32[]{:S(2)}, u32[]{:S(2)}) async-start(bf16[16,192,128]{2,1,0:T(8,128)(2,1)} %query_attention.1.after_ref), calls=%async_computation | async-start | bytes 1572864 | tf_op jit(solution)/shard_map/all_to_all | solution.py:312
  29.5 20.4 %copy-start = (bf16[1024,256]{1,0:T(8,128)(2,1)S(1)}, bf16[1024,256]{1,0:T(8,128)(2,1)}, u32[]{:S(2)}) copy-start(bf16[1024,256]{1,0:T(8,128)(2,1)} %w_ref.1) | copy-start | bytes 1572868
  45.8 4.1 %collective-permute-start.2 = (bf16[16,176,128]{2,1,0:T(8,128)(2,1)S(1)}, bf16[16,176,128]{2,1,0:T(8,128)(2,1)S(1)}, u32[]{:S(2)}, u32[]{:S(2)}) collective-permute-start(bf16[16,176,128]{2,1,0:T(8,128)(2,1)S(1)} %all_to_all.15.mine_ref), channel_id=1, source_target_pairs={{0,8},{8,0},{1,9},{9,1},{2,10},{10,2},{3,11},{11,3},{4,12},{12,4},... | collective-permute-start | bytes 2162696 | tf_op jit(solution)/shard_map/ppermute | solution.py:308
  51.8 19.3 %all-to-all-start.2 = ((bf16[8,64,256]{2,1,0:T(8,128)(2,1)}), bf16[8,64,256]{2,1,0:T(8,128)(2,1)S(1)}, u32[]{:S(2)}, u32[]{:S(2)}) async-start(bf16[8,64,256]{2,1,0:T(8,128)(2,1)} %get-tuple-element.17), calls=%async_computation.2 | async-start | bytes 524288 | tf_op jit(solution)/shard_map/all_to_all | solution.py:312

commit v6 on v5

--- a/solution.py
+++ b/solution.py
@@ -155,7 +155,7 @@
         values_ref[:, HEAD : 2 * HEAD] = jnp.ones((BLOCK, HEAD), BF)
 
 
-def own_kernel(q_ref, k_ref, v_ref, after_ref, out_ref, lse_ref, values_ref):
+def own_kernel(q_ref, k_ref, v_ref, after_ref, x_ref, y_ref, z_ref, out_ref, lse_ref, values_ref):
     fill_values(v_ref, values_ref)
 
     @pl.when(pl.program_id(0) == 0)
@@ -266,10 +266,10 @@
     )
 
 
-def own_call(ctx_query, k, v, after):
-    return run(
-        own_kernel, "context_own", (*in_hbm(ctx_query, k, v), after),
-        [STEP_BLOCK, HEAD_BLOCK, HEAD_BLOCK, ANY],
+def own_call(ctx_query, k, v, after, greetings):
+    return run(
+        own_kernel, "context_own", (*in_hbm(ctx_query, k, v), after, *greetings),
+        [STEP_BLOCK, HEAD_BLOCK, HEAD_BLOCK] + [ANY] * 4,
         (pltpu.HBM((BLOCK, WIDE), BF), pltpu.HBM((BLOCK, HEAD), F32)), (STEP_BLOCK, HEAD_BLOCK),
         [buffer((BLOCK, 2 * HEAD))], 4 * 6144 * 512 * 256, 4 << 20, 6144 * 512, grid=(HEADS // STEP,),
     )
@@ -308,16 +308,22 @@
     return lax.ppermute(value, "c", [(0, 1), (1, 0)])
 
 
+def greet(value, axis, size):
+    return lax.ppermute(value, axis, [(i, (i + 1) % size) for i in range(size)])
+
+
 def exchange(value, axes):
     return lax.all_to_all(value, axes, 0, 0, tiled=True)
 
 
 def per_device(ctx_query, context_key, context_value, query, out_weight):
     key_p, value_p = swap(context_key), swap(context_value)
+    few = context_key[0:16]
+    greetings = [greet(few, axis, size) for axis, size in (("x", 4), ("y", 4), ("z", 8))]
     q, k, values = prep_call(query, context_key, context_value)
     sent = query_call(q, k, values, key_p, value_p)
     received = exchange(sent, ("y", "x"))
-    own, lse = own_call(ctx_query, context_key, context_value, sent)
+    own, lse = own_call(ctx_query, context_key, context_value, sent, greetings)
     gathered = exchange(combine_call(received, lse), ("y", "x"))
     shares, key_a, value_a = project_call(gathered, swap(gathered), out_weight)
     ctx_out = anchor_call(ctx_query, key_a, value_a, own, lse)

time: 72.2 us -> 79.4 us (1.100)
  starting transfers between devices: 18.9 us -> 23 us
  blocking collectives: 15.8 us -> 17.8 us
    ppermute x0 -> x3, waiting for transfers between devices: none -> 6.56 us  [greet(): return lax.ppermute(value, axis, [(i, (i + 1) % size) for i in range(size)])]
    all_to_all x2, waiting for transfers between devices: 7.36 us -> 1.23 us  [exchange(): return lax.all_to_all(value, axes, 0, 0, tiled=True)]
    ppermute x0 -> x3, starting transfers between devices: none -> 4.19 us  [greet(): return lax.ppermute(value, axis, [(i, (i + 1) % size) for i in range(size)])]
    all_to_all x1, blocking collectives: 15.8 us -> 17.8 us  [exchange(): return lax.all_to_all(value, axes, 0, 0, tiled=True)]
  transfers between devices with their start and end apart: 5 -> 8, of which waited for: 4 -> 5; matrix products, arithmetic and copies ran while one was open for 0% -> 1% of each run, Pallas kernels for 26% -> 24%
where the time goes in v6:
time: 79.4 us; the launch traced here: 79 us
  Pallas kernels  27 us (34%)
  starting transfers between devices  23 us (29%)
  blocking collectives  17.8 us (22%)
  waiting for transfers between devices  9.84 us (12%)
    pallas_call x7, Pallas kernels, run(): pl.pallas_call(kernel, grid=grid, in_specs=in_specs, out_specs=out_specs,...  27 us
    all_to_all x1, blocking collectives, exchange(): return lax.all_to_all(value, axes, 0, 0, tiled=True)  17.8 us
    all_to_all x2, starting transfers between devices, exchange(): return lax.all_to_all(value, axes, 0, 0, tiled=True)  13.2 us
    ppermute x3, waiting for transfers between devices, greet(): return lax.ppermute(value, axis, [(i, (i + 1) % size) for i in range(size)])  6.56 us
    ppermute x3, starting transfers between devices, swap(): return lax.ppermute(value, 'c', [(0, 1), (1, 0)])  5.58 us
    ppermute x3, starting transfers between devices, greet(): return lax.ppermute(value, axis, [(i, (i + 1) % size) for i in range(size)])  4.19 us
    ppermute x3, waiting for transfers between devices, swap(): return lax.ppermute(value, 'c', [(0, 1), (1, 0)])  2.05 us
  transfers between devices with their start and end apart: 8, of which 5 were waited for; matrix products, arithmetic and copies ran while one was open for 1% of the time, Pallas kernels for 24%

profile of v6, /device:TPU:1, one launch (start us, length us, event | category | flops | bytes accessed | tf_op | source)
XLA Modules:
  0.0 79.0 jit_solution(9801191823666891268)
XLA Ops:
  0.6 3.3 %collective-permute-start.1 = (bf16[768,128]{1,0:T(8,128)(2,1)}, bf16[768,128]{1,0:T(8,128)(2,1)S(1)}, u32[]{:S(2)}, u32[]{:S(2)}) collective-permute-start(bf16[768,128]{1,0:T(8,128)(2,1)} %v_ref.1), channel_id=1, source_target_pairs={{0,8},{8,0},{1,9},{9,1},{2,10},{10,2},{3,11},{11,3},{4,12},{12,4},... | collective-permute-start | bytes 589832 | tf_op jit(solution)/shard_map/ppermute | solution.py:308
  4.0 0.1 collective-permute-start
  4.1 1.3 %prep.1 = (bf16[256,1024]{1,0:T(8,128)(2,1)S(1)}, bf16[768,128]{1,0:T(8,128)(2,1)S(1)}, bf16[768,256]{1,0:T(8,128)(2,1)S(1)}) custom-call(bf16[512,1024]{1,0:T(8,128)(2,1)} %q_hbm.1, bf16[768,128]{1,0:T(8,128)(2,1)} %k_ref.1, bf16[768,128]{1,0:T(8,128)(2,1)} %v_ref.1), custom_call_target="tpu_custom_call" | custom-call | flops 262144 | bytes 2097152 | tf_op jit(solution)/shard_map/prep/pallas_call | solution.py:240
  5.4 0.0 collective-permute-done.1.vp_ref
  5.4 0.2 collective-permute-done.kp_ref
  5.6 5.2 %query_attention.1.after_ref = bf16[16,192,128]{2,1,0:T(8,128)(2,1)} custom-call(bf16[256,1024]{1,0:T(8,128)(2,1)S(1)} %get-tuple-element.10.q_ref, bf16[768,128]{1,0:T(8,128)(2,1)S(1)} %get-tuple-element.11.k_ref, bf16[768,256]{1,0:T(8,128)(2,1)S(1)} %get-tuple-element.12.values_ref, bf16[768,128]{1,0:T(8,128)(2,1)S(1)} %collective-permute-done.kp_ref, ...), custom_call_target="tpu_custom_call" | custom-call | flops 3221225472 | bytes 3145728 | tf_op jit(solution)/shard_map/query_attention/pallas_call | solution.py:240
  10.8 5.0 %all-to-all-start = ((bf16[16,192,128]{2,1,0:T(8,128)(2,1)}), bf16[16,192,128]{2,1,0:T(8,128)(2,1)S(1)}, u32[]{:S(2)}, u32[]{:S(2)}) async-start(bf16[16,192,128]{2,1,0:T(8,128)(2,1)} %query_attention.1.after_ref), calls=%async_computation | async-start | bytes 1572864 | tf_op jit(solution)/shard_map/all_to_all | solution.py:316
  15.9 0.7 slice.3
  16.6 1.6 %collective-permute-start.4 = (bf16[16,128]{1,0:T(8,128)(2,1)S(1)}, bf16[16,128]{1,0:T(8,128)(2,1)S(1)}, u32[]{:S(2)}, u32[]{:S(2)}) collective-permute-start(bf16[16,128]{1,0:T(8,128)(2,1)S(1)} %slice.3), channel_id=1, source_target_pairs={{0,1},{1,2},{2,3},{3,4},{4,5},{5,6},{6,7},{7,0},{8,9},{9,10},{10,1... | collective-permute-start | bytes 12296 | tf_op jit(solution)/shard_map/ppermute | solution.py:312
  18.2 1.4 %collective-permute-start.3 = (bf16[16,128]{1,0:T(8,128)(2,1)S(1)}, bf16[16,128]{1,0:T(8,128)(2,1)S(1)}, u32[]{:S(2)}, u32[]{:S(2)}) collective-permute-start(bf16[16,128]{1,0:T(8,128)(2,1)S(1)} %slice.3), channel_id=1, source_target_pairs={{0,64},{64,128},{128,192},{192,0},{1,65},{65,129},{129,193},{193,1... | collective-permute-start | bytes 12296 | tf_op jit(solution)/shard_map/ppermute | solution.py:312
  19.6 1.2 %collective-permute-start.2 = (bf16[16,128]{1,0:T(8,128)(2,1)S(1)}, bf16[16,128]{1,0:T(8,128)(2,1)S(1)}, u32[]{:S(2)}, u32[]{:S(2)}) collective-permute-start(bf16[16,128]{1,0:T(8,128)(2,1)S(1)} %slice.3), channel_id=1, source_target_pairs={{0,16},{16,32},{32,48},{48,0},{1,17},{17,33},{33,49},{49,1},{2,18}... | collective-permute-start | bytes 12296 | tf_op jit(solution)/shard_map/ppermute | solution.py:312
  20.7 2.7 %collective-permute-done.4.z_ref = bf16[16,128]{1,0:T(8,128)(2,1)S(1)} collective-permute-done((bf16[16,128]{1,0:T(8,128)(2,1)S(1)}, bf16[16,128]{1,0:T(8,128)(2,1)S(1)}, u32[]{:S(2)}, u32[]{:S(2)}) %collective-permute-start.4) | collective-permute-done | bytes 4128 | tf_op jit(solution)/shard_map/ppermute | solution.py:312
  23.4 0.0 collective-permute-done.3.y_ref
  23.4 3.9 %collective-permute-done.2.x_ref = bf16[16,128]{1,0:T(8,128)(2,1)S(1)} collective-permute-done((bf16[16,128]{1,0:T(8,128)(2,1)S(1)}, bf16[16,128]{1,0:T(8,128)(2,1)S(1)}, u32[]{:S(2)}, u32[]{:S(2)}) %collective-permute-start.2) | collective-permute-done | bytes 4128 | tf_op jit(solution)/shard_map/ppermute | solution.py:312
  27.3 7.5 %context_own.1 = (bf16[768,1024]{1,0:T(8,128)(2,1)}, f32[768,128]{1,0:T(8,128)}) custom-call(bf16[768,1024]{1,0:T(8,128)(2,1)} %q_ref.3, bf16[768,128]{1,0:T(8,128)(2,1)} %k_ref.1, bf16[768,128]{1,0:T(8,128)(2,1)} %v_ref.1, bf16[16,192,128]{2,1,0:T(8,128)(2,1)} %query_attention.1.after_ref, bf16[16,128]{1,0:T(8,128)(2,1)S(1)} %collective-permute-done.2.x_ref, ...), custom_call_target="tpu_custom_call" | custom-call | flops 3221225472 | bytes 4194304 | tf_op jit(solution)/shard_map/context_own/pallas_call | solution.py:240
  34.8 0.0 all-to-all-done.in_ref
  34.8 0.0 copy-start
  34.8 0.5 combine.1
  35.4 17.8 %all_to_all.15.mine_ref = bf16[16,176,128]{2,1,0:T(8,128)(2,1)S(1)} all-to-all(bf16[16,176,128]{2,1,0:T(8,128)(2,1)S(1)} %combine.1), channel_id=1, replica_groups=mesh['y'=4,'x'=4,'c'=2,'z'=8] {'y','x'}, dimensions={0} | all-to-all | bytes 1441792 | tf_op jit(solution)/shard_map/all_to_all | solution.py:316
  53.2 2.1 %collective-permute-start.5 = (bf16[16,176,128]{2,1,0:T(8,128)(2,1)S(1)}, bf16[16,176,128]{2,1,0:T(8,128)(2,1)S(1)}, u32[]{:S(2)}, u32[]{:S(2)}) collective-permute-start(bf16[16,176,128]{2,1,0:T(8,128)(2,1)S(1)} %all_to_all.15.mine_ref), channel_id=1, source_target_pairs={{0,8},{8,0},{1,9},{9,1},{2,10},{10,2},{3,11},{11,3},{4,12},{12,4},... | collective-permute-start | bytes 2162696 | tf_op jit(solution)/shard_map/ppermute | solution.py:308
  55.3 1.8 %collective-permute-done.5.other_ref = bf16[16,176,128]{2,1,0:T(8,128)(2,1)S(1)} collective-permute-done((bf16[16,176,128]{2,1,0:T(8,128)(2,1)S(1)}, bf16[16,176,128]{2,1,0:T(8,128)(2,1)S(1)}, u32[]{:S(2)}, u32[]{:S(2)}) %collective-permute-start.5) | collective-permute-done | bytes 720928 | tf_op jit(solution)/shard_map/ppermute | solution.py:308
  57.1 0.0 copy-done
  57.1 1.9 %project.1 = (bf16[8,64,256]{2,1,0:T(8,128)(2,1)}, bf16[768,128]{1,0:T(8,128)(2,1)}, bf16[768,128]{1,0:T(8,128)(2,1)}) custom-call(bf16[16,176,128]{2,1,0:T(8,128)(2,1)S(1)} %all_to_all.15.mine_ref, bf16[16,176,128]{2,1,0:T(8,128)(2,1)S(1)} %collective-permute-done.5.other_ref, bf16[1024,256]{1,0:T(8,128)(2,1)S(1)} %copy-done), custom_call_target="tpu_custom_call" | custom-call | flops 268435456 | bytes 2097152 | tf_op jit(solution)/shard_map/project/pallas_call | solution.py:240
  59.0 8.2 %all-to-all-start.2 = ((bf16[8,64,256]{2,1,0:T(8,128)(2,1)}), bf16[8,64,256]{2,1,0:T(8,128)(2,1)S(1)}, u32[]{:S(2)}, u32[]{:S(2)}) async-start(bf16[8,64,256]{2,1,0:T(8,128)(2,1)} %get-tuple-element.17), calls=%async_computation.2 | async-start | bytes 524288 | tf_op jit(solution)/shard_map/all_to_all | solution.py:316
  67.2 9.9 %context_anchor.1 = bf16[768,1024]{1,0:T(8,128)(2,1)} custom-call(bf16[768,1024]{1,0:T(8,128)(2,1)} %q_ref.3, bf16[768,128]{1,0:T(8,128)(2,1)} %get-tuple-element.14.k_ref, bf16[768,128]{1,0:T(8,128)(2,1)} %get-tuple-element.15.v_ref, bf16[768,1024]{1,0:T(8,128)(2,1)} %get-tuple-element.16.own_ref, f32[768,128]{1,0:T(8,128)} %get-tuple-element.13.after_ref.lse_ref), custom_call_target="tpu_custom_call" | custom-call | flops 4831838208 | bytes 6291456 | tf_op jit(solution)/shard_map/context_anchor/pallas_call | solution.py:240
  77.1 1.2 %all-to-all-done.2.in_ref = bf16[8,64,256]{2,1,0:T(8,128)(2,1)S(1)} async-done(((bf16[8,64,256]{2,1,0:T(8,128)(2,1)}), bf16[8,64,256]{2,1,0:T(8,128)(2,1)S(1)}, u32[]{:S(2)}, u32[]{:S(2)}) %all-to-all-start.2) | async-done | bytes 262176 | tf_op jit(solution)/shard_map/all_to_all | solution.py:316
  78.3 0.7 final_sum.1
Async XLA Ops:
  0.6 4.7 %collective-permute-start.1 = (bf16[768,128]{1,0:T(8,128)(2,1)}, bf16[768,128]{1,0:T(8,128)(2,1)S(1)}, u32[]{:S(2)}, u32[]{:S(2)}) collective-permute-start(bf16[768,128]{1,0:T(8,128)(2,1)} %v_ref.1), channel_id=1, source_target_pairs={{0,8},{8,0},{1,9},{9,1},{2,10},{10,2},{3,11},{11,3},{4,12},{12,4},... | collective-permute-start | bytes 589832 | tf_op jit(solution)/shard_map/ppermute | solution.py:308
  4.0 1.7 %collective-permute-start = (bf16[768,128]{1,0:T(8,128)(2,1)}, bf16[768,128]{1,0:T(8,128)(2,1)S(1)}, u32[]{:S(2)}, u32[]{:S(2)}) collective-permute-start(bf16[768,128]{1,0:T(8,128)(2,1)} %k_ref.1), channel_id=1, source_target_pairs={{0,8},{8,0},{1,9},{9,1},{2,10},{10,2},{3,11},{11,3},{4,12},{12,4},... | collective-permute-start | bytes 589832 | tf_op jit(solution)/shard_map/ppermute | solution.py:308
  10.8 23.9 %all-to-all-start = ((bf16[16,192,128]{2,1,0:T(8,128)(2,1)}), bf16[16,192,128]{2,1,0:T(8,128)(2,1)S(1)}, u32[]{:S(2)}, u32[]{:S(2)}) async-start(bf16[16,192,128]{2,1,0:T(8,128)(2,1)} %query_attention.1.after_ref), calls=%async_computation | async-start | bytes 1572864 | tf_op jit(solution)/shard_map/all_to_all | solution.py:316
  16.6 6.9 %collective-permute-start.4 = (bf16[16,128]{1,0:T(8,128)(2,1)S(1)}, bf16[16,128]{1,0:T(8,128)(2,1)S(1)}, u32[]{:S(2)}, u32[]{:S(2)}) collective-permute-start(bf16[16,128]{1,0:T(8,128)(2,1)S(1)} %slice.3), channel_id=1, source_target_pairs={{0,1},{1,2},{2,3},{3,4},{4,5},{5,6},{6,7},{7,0},{8,9},{9,10},{10,1... | collective-permute-start | bytes 12296 | tf_op jit(solution)/shard_map/ppermute | solution.py:312
  18.2 5.2 %collective-permute-start.3 = (bf16[16,128]{1,0:T(8,128)(2,1)S(1)}, bf16[16,128]{1,0:T(8,128)(2,1)S(1)}, u32[]{:S(2)}, u32[]{:S(2)}) collective-permute-start(bf16[16,128]{1,0:T(8,128)(2,1)S(1)} %slice.3), channel_id=1, source_target_pairs={{0,64},{64,128},{128,192},{192,0},{1,65},{65,129},{129,193},{193,1... | collective-permute-start | bytes 12296 | tf_op jit(solution)/shard_map/ppermute | solution.py:312
  19.6 7.7 %collective-permute-start.2 = (bf16[16,128]{1,0:T(8,128)(2,1)S(1)}, bf16[16,128]{1,0:T(8,128)(2,1)S(1)}, u32[]{:S(2)}, u32[]{:S(2)}) collective-permute-start(bf16[16,128]{1,0:T(8,128)(2,1)S(1)} %slice.3), channel_id=1, source_target_pairs={{0,16},{16,32},{32,48},{48,0},{1,17},{17,33},{33,49},{49,1},{2,18}... | collective-permute-start | bytes 12296 | tf_op jit(solution)/shard_map/ppermute | solution.py:312
  34.8 22.3 %copy-start = (bf16[1024,256]{1,0:T(8,128)(2,1)S(1)}, bf16[1024,256]{1,0:T(8,128)(2,1)}, u32[]{:S(2)}) copy-start(bf16[1024,256]{1,0:T(8,128)(2,1)} %w_ref.1) | copy-start | bytes 1572868
  53.2 4.0 %collective-permute-start.5 = (bf16[16,176,128]{2,1,0:T(8,128)(2,1)S(1)}, bf16[16,176,128]{2,1,0:T(8,128)(2,1)S(1)}, u32[]{:S(2)}, u32[]{:S(2)}) collective-permute-start(bf16[16,176,128]{2,1,0:T(8,128)(2,1)S(1)} %all_to_all.15.mine_ref), channel_id=1, source_target_pairs={{0,8},{8,0},{1,9},{9,1},{2,10},{10,2},{3,11},{11,3},{4,12},{12,4},... | collective-permute-start | bytes 2162696 | tf_op jit(solution)/shard_map/ppermute | solution.py:308
  59.0 19.3 %all-to-all-start.2 = ((bf16[8,64,256]{2,1,0:T(8,128)(2,1)}), bf16[8,64,256]{2,1,0:T(8,128)(2,1)S(1)}, u32[]{:S(2)}, u32[]{:S(2)}) async-start(bf16[8,64,256]{2,1,0:T(8,128)(2,1)} %get-tuple-element.17), calls=%async_computation.2 | async-start | bytes 524288 | tf_op jit(solution)/shard_map/all_to_all | solution.py:316

commit v7 on v5

--- a/solution.py
+++ b/solution.py
@@ -54,7 +54,7 @@
     values_ref[:, 0:HEAD] = v_buf[...]
 
 
-def query_kernel(q_ref, k_ref, values_ref, kp_ref, vp_ref, out_ref, values_p):
+def query_kernel(q_ref, k_ref, values_ref, kp_ref, vp_ref, out_hbm, values_p, out_ref, sems):
     core = lax.axis_index("c")
     values_p[:, 0:HEAD] = vp_ref[...]
     values_p[:, HEAD : 2 * HEAD] = jnp.ones((BLOCK, HEAD), BF)
@@ -88,7 +88,17 @@
                 core == 0, k_ref[at : at + ANCHOR_ROWS, :], vp_ref[at : at + ANCHOR_ROWS, :]
             )
 
-    pipelined(HEADS, scores, finish)
+    def write(j):
+        rows = slice(2 * j, 2 * j + 2)
+        return pltpu.make_async_copy(out_ref.at[rows], out_hbm.at[rows], sems.at[j])
+
+    def finish_and_write(j, s):
+        finish(j, s)
+        write(j).start()
+
+    pipelined(HEADS, scores, finish_and_write)
+    for j in range(HEADS):
+        write(j).wait()
 
 
 def combine_kernel(in_ref, after_ref, out_ref):
@@ -109,17 +119,17 @@
         out_ref[g, HEAD:SEND2, :] = anchor
 
 
-def project_kernel(mine_ref, other_ref, w_ref, out_ref, k_hbm, v_hbm, k_ref, v_ref, sems):
+def project_kernel(mine_ref, other_ref, w_ref, out_hbm, k_hbm, v_hbm, out_ref, k_ref, v_ref, sems):
     core = lax.axis_index("c")
     for g in range(16):
         rows = slice(g * ANCHOR_ROWS, (g + 1) * ANCHOR_ROWS)
         one, two = mine_ref[g, HEAD:SEND2, :], other_ref[g, HEAD:SEND2, :]
         k_ref[rows, :] = jnp.where(core == 0, one, two)
         v_ref[rows, :] = jnp.where(core == 0, two, one)
-    copies = (
+    copies = [
         pltpu.make_async_copy(k_ref, k_hbm, sems.at[0]),
         pltpu.make_async_copy(v_ref, v_hbm, sems.at[1]),
-    )
+    ]
     for copy in copies:
         copy.start()
     for ref, owner in ((mine_ref, core), (other_ref, 1 - core)):
@@ -133,6 +143,9 @@
         y = jnp.dot(a, w_ref[...], preferred_element_type=F32).astype(BF)
         for z in range(4):
             out_ref[4 * owner + z] = y[64 * z : 64 * z + 64, :]
+        half = pl.ds(4 * owner, 4)
+        copies.append(pltpu.make_async_copy(out_ref.at[half], out_hbm.at[half], sems.at[len(copies)]))
+        copies[-1].start()
     for copy in copies:
         copy.wait()
 
@@ -191,8 +204,16 @@
     pipelined(STEP, scores, finish)
 
 
-def anchor_kernel(q_ref, k_ref, v_ref, own_ref, lse_ref, out_ref, values_ref):
+def anchor_kernel(q_ref, k_ref, v_ref, own_ref, lse_ref, out_ref, values_ref, keys_ref):
     fill_values(v_ref, values_ref)
+
+    @pl.when(pl.program_id(0) == 0)
+    def _():
+        k = k_ref[...].astype(F32) * LOG2_SCALE
+        high = k.astype(BF)
+        keys_ref[:, 0:HEAD] = high
+        keys_ref[:, HEAD : 2 * HEAD] = (k - high.astype(F32)).astype(BF)
+
     first = jnp.logical_and(
         lax.axis_index("c") == 0,
         jnp.logical_and(lax.axis_index("x") == 0, lax.axis_index("y") == 0),
@@ -200,20 +221,28 @@
     lane = lax.broadcasted_iota(jnp.int32, (BLOCK, HEAD), 1)
 
     def scores(h):
-        return scores_of(q_ref[:, HEAD * h : HEAD * h + HEAD], k_ref[...])
+        q = q_ref[:, HEAD * h : HEAD * h + HEAD]
+        return lax.dot_general(
+            jnp.concatenate([q, q], axis=1), keys_ref[...], (((1,), (1,)), ((), ())), preferred_element_type=F32
+        )
 
     def finish(h, s):
         head = pl.program_id(0) * STEP + h
         lse = jnp.sum(jnp.where(lane == head, lse_ref[...], 0.0), axis=1, keepdims=True)
         peak = jnp.maximum(lse, jnp.max(s, axis=1, keepdims=True))
-        peak = jnp.where(first, lse, peak)
-        p = jnp.exp2(s - jnp.where(first, HIDDEN, peak)).astype(BF)
+        p = jnp.exp2(s - peak).astype(BF)
         acc = jnp.dot(p, values_ref[...], preferred_element_type=F32)
         weight = jnp.exp2(lse - peak)
         mixture = acc[:, 0:HEAD] + weight * own_ref[:, HEAD * h : HEAD * h + HEAD].astype(F32)
         out_ref[:, HEAD * h : HEAD * h + HEAD] = (mixture / (acc[:, HEAD : 2 * HEAD] + weight)).astype(BF)
 
-    pipelined(STEP, scores, finish)
+    @pl.when(first)
+    def _():
+        out_ref[...] = own_ref[...]
+
+    @pl.when(jnp.logical_not(first))
+    def _():
+        pipelined(STEP, scores, finish)
 
 
 VMEM = pl.BlockSpec(memory_space=pltpu.VMEM)
@@ -261,7 +290,8 @@
 def query_call(q, k, values, kp, vp):
     return run(
         query_kernel, "query_attention", (q, k, values, kp, vp), [VMEM] * 5,
-        shape((16, SEND1, HEAD)), VMEM, [buffer((BLOCK, 2 * HEAD))],
+        pltpu.HBM((16, SEND1, HEAD), BF), HBM,
+        [buffer((BLOCK, 2 * HEAD)), buffer((16, SEND1, HEAD)), pltpu.SemaphoreType.DMA((HEADS,))],
         4 * 2048 * 1536 * 256, 3 << 20, 2048 * 1536,
     )
 
@@ -280,7 +310,7 @@
         anchor_kernel, "context_anchor", in_hbm(ctx_query, k, v, own, lse),
         [STEP_BLOCK, HEAD_BLOCK, HEAD_BLOCK, STEP_BLOCK, HEAD_BLOCK],
         shape((BLOCK, WIDE)), STEP_BLOCK,
-        [buffer((BLOCK, 2 * HEAD))], 4 * 6144 * 768 * 256, 6 << 20, 6144 * 768, grid=(HEADS // STEP,),
+        [buffer((BLOCK, 2 * HEAD))] * 2, 4 * 6144 * 768 * 256, 6 << 20, 6144 * 768, grid=(HEADS // STEP,),
     )
 
 
@@ -294,8 +324,8 @@
 def project_call(mine, other, w):
     return run(
         project_kernel, "project", (mine, other, w), [VMEM] * 3,
-        (shape((8, 64, 256)), pltpu.HBM((BLOCK, HEAD), BF), pltpu.HBM((BLOCK, HEAD), BF)), (VMEM, HBM, HBM),
-        [buffer((BLOCK, HEAD)), buffer((BLOCK, HEAD)), pltpu.SemaphoreType.DMA((2,))],
+        (pltpu.HBM((8, 64, 256), BF), pltpu.HBM((BLOCK, HEAD), BF), pltpu.HBM((BLOCK, HEAD), BF)), (HBM,) * 3,
+        [buffer((8, 64, 256)), buffer((BLOCK, HEAD)), buffer((BLOCK, HEAD)), pltpu.SemaphoreType.DMA((4,))],
         2 * 512 * 1024 * 256, 2 << 20,
     )
 

time: 72.2 us -> 71.5 us (level)
  Pallas kernels: 27 us -> 25.1 us
  local copies, waits for them, and re-layouts: 0.01 us -> 1.16 us
    pallas_call x7, Pallas kernels: 27 us -> 25.1 us  [run(): pl.pallas_call(kernel, grid=grid, in_specs=in_specs, out_specs=out_specs,...]
    unnamed x2 -> x4, local copies, waits for them, and re-layouts: 0.01 us -> 1.16 us
  transfers between devices with their start and end apart: 5 -> 5, of which waited for: 4 -> 4; matrix products, arithmetic and copies ran while one was open for 0% -> 0% of each run, Pallas kernels for 26% -> 25%
where the time goes in v7:
time: 71.5 us; the launch traced here: 71 us
  Pallas kernels  25.1 us (35%)
  starting transfers between devices  18.9 us (26%)
  blocking collectives  15.8 us (22%)
  waiting for transfers between devices  9.4 us (13%)
  local copies, waits for them, and re-layouts  1.16 us (2%)
    pallas_call x7, Pallas kernels, run(): pl.pallas_call(kernel, grid=grid, in_specs=in_specs, out_specs=out_specs,...  25.1 us
    all_to_all x1, blocking collectives, exchange(): return lax.all_to_all(value, axes, 0, 0, tiled=True)  15.8 us
    all_to_all x2, starting transfers between devices, exchange(): return lax.all_to_all(value, axes, 0, 0, tiled=True)  13.2 us
    all_to_all x2, waiting for transfers between devices, exchange(): return lax.all_to_all(value, axes, 0, 0, tiled=True)  7.35 us
    ppermute x3, starting transfers between devices, swap(): return lax.ppermute(value, 'c', [(0, 1), (1, 0)])  5.69 us
    ppermute x3, waiting for transfers between devices, swap(): return lax.ppermute(value, 'c', [(0, 1), (1, 0)])  2.05 us
  transfers between devices with their start and end apart: 5, of which 4 were waited for; matrix products, arithmetic and copies ran while one was open for 0% of the time, Pallas kernels for 25%

profile of v7, /device:TPU:1, one launch (start us, length us, event | category | flops | bytes accessed | tf_op | source)
XLA Modules:
  0.0 71.0 jit_solution(11001380680813804344)
XLA Ops:
  0.6 3.3 %collective-permute-start = (bf16[768,128]{1,0:T(8,128)(2,1)}, bf16[768,128]{1,0:T(8,128)(2,1)S(1)}, u32[]{:S(2)}, u32[]{:S(2)}) collective-permute-start(bf16[768,128]{1,0:T(8,128)(2,1)} %k_ref.1), channel_id=1, source_target_pairs={{0,8},{8,0},{1,9},{9,1},{2,10},{10,2},{3,11},{11,3},{4,12},{12,4},... | collective-permute-start | bytes 589832 | tf_op jit(solution)/shard_map/ppermute | solution.py:338
  4.0 0.1 collective-permute-start.1
  4.1 1.3 %prep.1 = (bf16[256,1024]{1,0:T(8,128)(2,1)S(1)}, bf16[768,128]{1,0:T(8,128)(2,1)S(1)}, bf16[768,256]{1,0:T(8,128)(2,1)S(1)}) custom-call(bf16[512,1024]{1,0:T(8,128)(2,1)} %q_hbm.1, bf16[768,128]{1,0:T(8,128)(2,1)} %k_ref.1, bf16[768,128]{1,0:T(8,128)(2,1)} %v_ref.1), custom_call_target="tpu_custom_call" | custom-call | flops 262144 | bytes 2097152 | tf_op jit(solution)/shard_map/prep/pallas_call | solution.py:269
  5.4 0.0 collective-permute-done.kp_ref
  5.4 0.2 collective-permute-done.1.vp_ref
  5.6 5.1 %query_attention.1.after_ref = bf16[16,192,128]{2,1,0:T(8,128)(2,1)} custom-call(bf16[256,1024]{1,0:T(8,128)(2,1)S(1)} %get-tuple-element.10.q_ref, bf16[768,128]{1,0:T(8,128)(2,1)S(1)} %get-tuple-element.11.k_ref, bf16[768,256]{1,0:T(8,128)(2,1)S(1)} %get-tuple-element.12.values_ref, bf16[768,128]{1,0:T(8,128)(2,1)S(1)} %collective-permute-done.kp_ref, ...), custom_call_target="tpu_custom_call" | custom-call | flops 3221225472 | bytes 3145728 | tf_op jit(solution)/shard_map/query_attention/pallas_call | solution.py:269
  10.7 5.0 %all-to-all-start = ((bf16[16,192,128]{2,1,0:T(8,128)(2,1)}), bf16[16,192,128]{2,1,0:T(8,128)(2,1)S(1)}, u32[]{:S(2)}, u32[]{:S(2)}) async-start(bf16[16,192,128]{2,1,0:T(8,128)(2,1)} %query_attention.1.after_ref), calls=%async_computation | async-start | bytes 1572864 | tf_op jit(solution)/shard_map/all_to_all | solution.py:342
  15.7 0.0 copy-start
  15.7 1.2 %copy-done = bf16[16,192,128]{2,1,0:T(8,128)(2,1)S(1)} copy-done((bf16[16,192,128]{2,1,0:T(8,128)(2,1)S(1)}, bf16[16,192,128]{2,1,0:T(8,128)(2,1)}, u32[]{:S(2)}) %copy-start) | copy-done | bytes 786456
  16.9 7.5 %context_own.1 = (bf16[768,1024]{1,0:T(8,128)(2,1)}, f32[768,128]{1,0:T(8,128)}) custom-call(bf16[768,1024]{1,0:T(8,128)(2,1)} %q_ref.3, bf16[768,128]{1,0:T(8,128)(2,1)} %k_ref.1, bf16[768,128]{1,0:T(8,128)(2,1)} %v_ref.1, bf16[16,192,128]{2,1,0:T(8,128)(2,1)S(1)} %copy-done), custom_call_target="tpu_custom_call" | custom-call | flops 3221225472 | bytes 4194304 | tf_op jit(solution)/shard_map/context_own/pallas_call | solution.py:269
  24.4 5.0 %all-to-all-done.in_ref = bf16[16,192,128]{2,1,0:T(8,128)(2,1)S(1)} async-done(((bf16[16,192,128]{2,1,0:T(8,128)(2,1)}), bf16[16,192,128]{2,1,0:T(8,128)(2,1)S(1)}, u32[]{:S(2)}, u32[]{:S(2)}) %all-to-all-start) | async-done | bytes 786464 | tf_op jit(solution)/shard_map/all_to_all | solution.py:342
  29.4 0.0 copy-start.1
  29.4 0.5 combine.1
  29.9 15.8 %all_to_all.15.mine_ref = bf16[16,176,128]{2,1,0:T(8,128)(2,1)S(1)} all-to-all(bf16[16,176,128]{2,1,0:T(8,128)(2,1)S(1)} %combine.1), channel_id=1, replica_groups=mesh['y'=4,'x'=4,'c'=2,'z'=8] {'y','x'}, dimensions={0} | all-to-all | bytes 1441792 | tf_op jit(solution)/shard_map/all_to_all | solution.py:342
  45.7 2.3 %collective-permute-start.2 = (bf16[16,176,128]{2,1,0:T(8,128)(2,1)S(1)}, bf16[16,176,128]{2,1,0:T(8,128)(2,1)S(1)}, u32[]{:S(2)}, u32[]{:S(2)}) collective-permute-start(bf16[16,176,128]{2,1,0:T(8,128)(2,1)S(1)} %all_to_all.15.mine_ref), channel_id=1, source_target_pairs={{0,8},{8,0},{1,9},{9,1},{2,10},{10,2},{3,11},{11,3},{4,12},{12,4},... | collective-permute-start | bytes 2162696 | tf_op jit(solution)/shard_map/ppermute | solution.py:338
  48.0 1.8 %collective-permute-done.2.other_ref = bf16[16,176,128]{2,1,0:T(8,128)(2,1)S(1)} collective-permute-done((bf16[16,176,128]{2,1,0:T(8,128)(2,1)S(1)}, bf16[16,176,128]{2,1,0:T(8,128)(2,1)S(1)}, u32[]{:S(2)}, u32[]{:S(2)}) %collective-permute-start.2) | collective-permute-done | bytes 720928 | tf_op jit(solution)/shard_map/ppermute | solution.py:338
  49.8 0.0 copy-done.1
  49.8 1.3 %project.1 = (bf16[8,64,256]{2,1,0:T(8,128)(2,1)}, bf16[768,128]{1,0:T(8,128)(2,1)}, bf16[768,128]{1,0:T(8,128)(2,1)}) custom-call(bf16[16,176,128]{2,1,0:T(8,128)(2,1)S(1)} %all_to_all.15.mine_ref, bf16[16,176,128]{2,1,0:T(8,128)(2,1)S(1)} %collective-permute-done.2.other_ref, bf16[1024,256]{1,0:T(8,128)(2,1)S(1)} %copy-done.1), custom_call_target="tpu_custom_call" | custom-call | flops 268435456 | bytes 2097152 | tf_op jit(solution)/shard_map/project/pallas_call | solution.py:269
  51.1 8.2 %all-to-all-start.2 = ((bf16[8,64,256]{2,1,0:T(8,128)(2,1)}), bf16[8,64,256]{2,1,0:T(8,128)(2,1)S(1)}, u32[]{:S(2)}, u32[]{:S(2)}) async-start(bf16[8,64,256]{2,1,0:T(8,128)(2,1)} %get-tuple-element.17), calls=%async_computation.2 | async-start | bytes 524288 | tf_op jit(solution)/shard_map/all_to_all | solution.py:342
  59.3 8.7 %context_anchor.1 = bf16[768,1024]{1,0:T(8,128)(2,1)} custom-call(bf16[768,1024]{1,0:T(8,128)(2,1)} %q_ref.3, bf16[768,128]{1,0:T(8,128)(2,1)} %get-tuple-element.14.k_ref, bf16[768,128]{1,0:T(8,128)(2,1)} %get-tuple-element.15.v_ref, bf16[768,1024]{1,0:T(8,128)(2,1)} %get-tuple-element.16.own_ref, f32[768,128]{1,0:T(8,128)} %get-tuple-element.13.after_ref.lse_ref), custom_call_target="tpu_custom_call" | custom-call | flops 4831838208 | bytes 6291456 | tf_op jit(solution)/shard_map/context_anchor/pallas_call | solution.py:269
  68.0 2.3 %all-to-all-done.2.in_ref = bf16[8,64,256]{2,1,0:T(8,128)(2,1)S(1)} async-done(((bf16[8,64,256]{2,1,0:T(8,128)(2,1)}), bf16[8,64,256]{2,1,0:T(8,128)(2,1)S(1)}, u32[]{:S(2)}, u32[]{:S(2)}) %all-to-all-start.2) | async-done | bytes 262176 | tf_op jit(solution)/shard_map/all_to_all | solution.py:342
  70.4 0.7 final_sum.1
Async XLA Ops:
  0.6 4.7 %collective-permute-start = (bf16[768,128]{1,0:T(8,128)(2,1)}, bf16[768,128]{1,0:T(8,128)(2,1)S(1)}, u32[]{:S(2)}, u32[]{:S(2)}) collective-permute-start(bf16[768,128]{1,0:T(8,128)(2,1)} %k_ref.1), channel_id=1, source_target_pairs={{0,8},{8,0},{1,9},{9,1},{2,10},{10,2},{3,11},{11,3},{4,12},{12,4},... | collective-permute-start | bytes 589832 | tf_op jit(solution)/shard_map/ppermute | solution.py:338
  4.0 1.7 %collective-permute-start.1 = (bf16[768,128]{1,0:T(8,128)(2,1)}, bf16[768,128]{1,0:T(8,128)(2,1)S(1)}, u32[]{:S(2)}, u32[]{:S(2)}) collective-permute-start(bf16[768,128]{1,0:T(8,128)(2,1)} %v_ref.1), channel_id=1, source_target_pairs={{0,8},{8,0},{1,9},{9,1},{2,10},{10,2},{3,11},{11,3},{4,12},{12,4},... | collective-permute-start | bytes 589832 | tf_op jit(solution)/shard_map/ppermute | solution.py:338
  10.7 18.7 %all-to-all-start = ((bf16[16,192,128]{2,1,0:T(8,128)(2,1)}), bf16[16,192,128]{2,1,0:T(8,128)(2,1)S(1)}, u32[]{:S(2)}, u32[]{:S(2)}) async-start(bf16[16,192,128]{2,1,0:T(8,128)(2,1)} %query_attention.1.after_ref), calls=%async_computation | async-start | bytes 1572864 | tf_op jit(solution)/shard_map/all_to_all | solution.py:342
  15.7 1.2 %copy-start = (bf16[16,192,128]{2,1,0:T(8,128)(2,1)S(1)}, bf16[16,192,128]{2,1,0:T(8,128)(2,1)}, u32[]{:S(2)}) copy-start(bf16[16,192,128]{2,1,0:T(8,128)(2,1)} %query_attention.1.after_ref) | copy-start | bytes 2359300
  29.4 20.4 %copy-start.1 = (bf16[1024,256]{1,0:T(8,128)(2,1)S(1)}, bf16[1024,256]{1,0:T(8,128)(2,1)}, u32[]{:S(2)}) copy-start(bf16[1024,256]{1,0:T(8,128)(2,1)} %w_ref.1) | copy-start | bytes 1572868
  45.7 4.1 %collective-permute-start.2 = (bf16[16,176,128]{2,1,0:T(8,128)(2,1)S(1)}, bf16[16,176,128]{2,1,0:T(8,128)(2,1)S(1)}, u32[]{:S(2)}, u32[]{:S(2)}) collective-permute-start(bf16[16,176,128]{2,1,0:T(8,128)(2,1)S(1)} %all_to_all.15.mine_ref), channel_id=1, source_target_pairs={{0,8},{8,0},{1,9},{9,1},{2,10},{10,2},{3,11},{11,3},{4,12},{12,4},... | collective-permute-start | bytes 2162696 | tf_op jit(solution)/shard_map/ppermute | solution.py:338
  51.1 19.3 %all-to-all-start.2 = ((bf16[8,64,256]{2,1,0:T(8,128)(2,1)}), bf16[8,64,256]{2,1,0:T(8,128)(2,1)S(1)}, u32[]{:S(2)}, u32[]{:S(2)}) async-start(bf16[8,64,256]{2,1,0:T(8,128)(2,1)} %get-tuple-element.17), calls=%async_computation.2 | async-start | bytes 524288 | tf_op jit(solution)/shard_map/all_to_all | solution.py:342

commit v8 on v7

--- a/solution.py
+++ b/solution.py
@@ -247,7 +247,6 @@
 
 VMEM = pl.BlockSpec(memory_space=pltpu.VMEM)
 HBM = pl.BlockSpec(memory_space=pltpu.HBM)
-ANY = pl.BlockSpec(memory_space=pl.ANY)
 WIDE = HEADS * HEAD
 STEP_BLOCK = pl.BlockSpec((BLOCK, STEP_COLUMNS), lambda t: (0, t))
 HEAD_BLOCK = pl.BlockSpec((BLOCK, HEAD), lambda t: (0, 0))
@@ -298,8 +297,8 @@
 
 def own_call(ctx_query, k, v, after):
     return run(
-        own_kernel, "context_own", (*in_hbm(ctx_query, k, v), after),
-        [STEP_BLOCK, HEAD_BLOCK, HEAD_BLOCK, ANY],
+        own_kernel, "context_own", in_hbm(ctx_query, k, v, after),
+        [STEP_BLOCK, HEAD_BLOCK, HEAD_BLOCK, HBM],
         (pltpu.HBM((BLOCK, WIDE), BF), pltpu.HBM((BLOCK, HEAD), F32)), (STEP_BLOCK, HEAD_BLOCK),
         [buffer((BLOCK, 2 * HEAD))], 4 * 6144 * 512 * 256, 4 << 20, 6144 * 512, grid=(HEADS // STEP,),
     )
@@ -346,9 +345,9 @@
     key_p, value_p = swap(context_key), swap(context_value)
     q, k, values = prep_call(query, context_key, context_value)
     sent = query_call(q, k, values, key_p, value_p)
-    received = exchange(sent, ("y", "x"))
+    received = exchange(sent, ("x", "y"))
     own, lse = own_call(ctx_query, context_key, context_value, sent)
-    gathered = exchange(combine_call(received, lse), ("y", "x"))
+    gathered = exchange(combine_call(received, lse), ("x", "y"))
     shares, key_a, value_a = project_call(gathered, swap(gathered), out_weight)
     ctx_out = anchor_call(ctx_query, key_a, value_a, own, lse)
     answer = final_call(exchange(shares, "z"))

time: 71.5 us -> 71.1 us (level)
  local copies, waits for them, and re-layouts: 1.16 us -> 0.01 us
    unnamed x4 -> x2, local copies, waits for them, and re-layouts: 1.16 us -> 0.01 us
    ppermute x3, starting transfers between devices: 5.69 us -> 6.41 us  [swap(): return lax.ppermute(value, 'c', [(0, 1), (1, 0)])]
where the time goes in v8:
time: 71.1 us; the launch traced here: 70.7 us
  Pallas kernels  25.1 us (35%)
  starting transfers between devices  19.6 us (28%)
  blocking collectives  15.7 us (22%)
  waiting for transfers between devices  9.53 us (13%)
    pallas_call x7, Pallas kernels, run(): pl.pallas_call(kernel, grid=grid, in_specs=in_specs, out_specs=out_specs,...  25.1 us
    all_to_all x1, blocking collectives, exchange(): return lax.all_to_all(value, axes, 0, 0, tiled=True)  15.7 us
    all_to_all x2, starting transfers between devices, exchange(): return lax.all_to_all(value, axes, 0, 0, tiled=True)  13.2 us
    all_to_all x2, waiting for transfers between devices, exchange(): return lax.all_to_all(value, axes, 0, 0, tiled=True)  7.49 us
    ppermute x3, starting transfers between devices, swap(): return lax.ppermute(value, 'c', [(0, 1), (1, 0)])  6.41 us
    ppermute x3, waiting for transfers between devices, swap(): return lax.ppermute(value, 'c', [(0, 1), (1, 0)])  2.05 us
  transfers between devices with their start and end apart: 5, of which 4 were waited for; matrix products, arithmetic and copies ran while one was open for 0% of the time, Pallas kernels for 25%

profile of v8, /device:TPU:1, one launch (start us, length us, event | category | flops | bytes accessed | tf_op | source)
XLA Modules:
  0.0 70.7 jit_solution(6917227915444040785)
XLA Ops:
  0.6 3.3 %collective-permute-start = (bf16[768,128]{1,0:T(8,128)(2,1)}, bf16[768,128]{1,0:T(8,128)(2,1)S(1)}, u32[]{:S(2)}, u32[]{:S(2)}) collective-permute-start(bf16[768,128]{1,0:T(8,128)(2,1)} %k_ref.1), channel_id=1, source_target_pairs={{0,8},{8,0},{1,9},{9,1},{2,10},{10,2},{3,11},{11,3},{4,12},{12,4},... | collective-permute-start | bytes 589832 | tf_op jit(solution)/shard_map/ppermute | solution.py:337
  4.0 0.1 collective-permute-start.1
  4.1 1.3 %prep.1 = (bf16[256,1024]{1,0:T(8,128)(2,1)S(1)}, bf16[768,128]{1,0:T(8,128)(2,1)S(1)}, bf16[768,256]{1,0:T(8,128)(2,1)S(1)}) custom-call(bf16[512,1024]{1,0:T(8,128)(2,1)} %q_hbm.1, bf16[768,128]{1,0:T(8,128)(2,1)} %k_ref.1, bf16[768,128]{1,0:T(8,128)(2,1)} %v_ref.1), custom_call_target="tpu_custom_call" | custom-call | flops 262144 | bytes 2097152 | tf_op jit(solution)/shard_map/prep/pallas_call | solution.py:268
  5.4 0.0 collective-permute-done.kp_ref
  5.4 0.2 collective-permute-done.1.vp_ref
  5.6 5.1 %query_attention.1.after_ref = bf16[16,192,128]{2,1,0:T(8,128)(2,1)} custom-call(bf16[256,1024]{1,0:T(8,128)(2,1)S(1)} %get-tuple-element.10.q_ref, bf16[768,128]{1,0:T(8,128)(2,1)S(1)} %get-tuple-element.11.k_ref, bf16[768,256]{1,0:T(8,128)(2,1)S(1)} %get-tuple-element.12.values_ref, bf16[768,128]{1,0:T(8,128)(2,1)S(1)} %collective-permute-done.kp_ref, ...), custom_call_target="tpu_custom_call" | custom-call | flops 3221225472 | bytes 3145728 | tf_op jit(solution)/shard_map/query_attention/pallas_call | solution.py:268
  10.7 5.0 %all-to-all-start = ((bf16[16,192,128]{2,1,0:T(8,128)(2,1)}), bf16[16,192,128]{2,1,0:T(8,128)(2,1)S(1)}, u32[]{:S(2)}, u32[]{:S(2)}) async-start(bf16[16,192,128]{2,1,0:T(8,128)(2,1)} %query_attention.1.after_ref), calls=%async_computation | async-start | bytes 1572864 | tf_op jit(solution)/shard_map/all_to_all | solution.py:341
  15.7 7.5 %context_own.1 = (bf16[768,1024]{1,0:T(8,128)(2,1)}, f32[768,128]{1,0:T(8,128)}) custom-call(bf16[768,1024]{1,0:T(8,128)(2,1)} %q_ref.3, bf16[768,128]{1,0:T(8,128)(2,1)} %k_ref.1, bf16[768,128]{1,0:T(8,128)(2,1)} %v_ref.1, bf16[16,192,128]{2,1,0:T(8,128)(2,1)} %query_attention.1.after_ref), custom_call_target="tpu_custom_call" | custom-call | flops 3221225472 | bytes 4194304 | tf_op jit(solution)/shard_map/context_own/pallas_call | solution.py:268
  23.2 5.2 %all-to-all-done.in_ref = bf16[16,192,128]{2,1,0:T(8,128)(2,1)S(1)} async-done(((bf16[16,192,128]{2,1,0:T(8,128)(2,1)}), bf16[16,192,128]{2,1,0:T(8,128)(2,1)S(1)}, u32[]{:S(2)}, u32[]{:S(2)}) %all-to-all-start) | async-done | bytes 786464 | tf_op jit(solution)/shard_map/all_to_all | solution.py:341
  28.4 0.0 copy-start
  28.4 0.5 combine.1
  29.0 15.7 %all_to_all.15.mine_ref = bf16[16,176,128]{2,1,0:T(8,128)(2,1)S(1)} all-to-all(bf16[16,176,128]{2,1,0:T(8,128)(2,1)S(1)} %combine.1), channel_id=1, replica_groups=mesh['y'=4,'x'=4,'c'=2,'z'=8] {'x','y'}, dimensions={0} | all-to-all | bytes 1441792 | tf_op jit(solution)/shard_map/all_to_all | solution.py:341
  44.7 3.0 %collective-permute-start.2 = (bf16[16,176,128]{2,1,0:T(8,128)(2,1)S(1)}, bf16[16,176,128]{2,1,0:T(8,128)(2,1)S(1)}, u32[]{:S(2)}, u32[]{:S(2)}) collective-permute-start(bf16[16,176,128]{2,1,0:T(8,128)(2,1)S(1)} %all_to_all.15.mine_ref), channel_id=1, source_target_pairs={{0,8},{8,0},{1,9},{9,1},{2,10},{10,2},{3,11},{11,3},{4,12},{12,4},... | collective-permute-start | bytes 2162696 | tf_op jit(solution)/shard_map/ppermute | solution.py:337
  47.7 1.8 %collective-permute-done.2.other_ref = bf16[16,176,128]{2,1,0:T(8,128)(2,1)S(1)} collective-permute-done((bf16[16,176,128]{2,1,0:T(8,128)(2,1)S(1)}, bf16[16,176,128]{2,1,0:T(8,128)(2,1)S(1)}, u32[]{:S(2)}, u32[]{:S(2)}) %collective-permute-start.2) | collective-permute-done | bytes 720928 | tf_op jit(solution)/shard_map/ppermute | solution.py:337
  49.5 0.0 copy-done
  49.5 1.3 %project.1 = (bf16[8,64,256]{2,1,0:T(8,128)(2,1)}, bf16[768,128]{1,0:T(8,128)(2,1)}, bf16[768,128]{1,0:T(8,128)(2,1)}) custom-call(bf16[16,176,128]{2,1,0:T(8,128)(2,1)S(1)} %all_to_all.15.mine_ref, bf16[16,176,128]{2,1,0:T(8,128)(2,1)S(1)} %collective-permute-done.2.other_ref, bf16[1024,256]{1,0:T(8,128)(2,1)S(1)} %copy-done), custom_call_target="tpu_custom_call" | custom-call | flops 268435456 | bytes 2097152 | tf_op jit(solution)/shard_map/project/pallas_call | solution.py:268
  50.8 8.2 %all-to-all-start.2 = ((bf16[8,64,256]{2,1,0:T(8,128)(2,1)}), bf16[8,64,256]{2,1,0:T(8,128)(2,1)S(1)}, u32[]{:S(2)}, u32[]{:S(2)}) async-start(bf16[8,64,256]{2,1,0:T(8,128)(2,1)} %get-tuple-element.17), calls=%async_computation.2 | async-start | bytes 524288 | tf_op jit(solution)/shard_map/all_to_all | solution.py:341
  59.0 8.7 %context_anchor.1 = bf16[768,1024]{1,0:T(8,128)(2,1)} custom-call(bf16[768,1024]{1,0:T(8,128)(2,1)} %q_ref.3, bf16[768,128]{1,0:T(8,128)(2,1)} %get-tuple-element.14.k_ref, bf16[768,128]{1,0:T(8,128)(2,1)} %get-tuple-element.15.v_ref, bf16[768,1024]{1,0:T(8,128)(2,1)} %get-tuple-element.16.own_ref, f32[768,128]{1,0:T(8,128)} %get-tuple-element.13.after_ref.lse_ref), custom_call_target="tpu_custom_call" | custom-call | flops 4831838208 | bytes 6291456 | tf_op jit(solution)/shard_map/context_anchor/pallas_call | solution.py:268
  67.7 2.3 %all-to-all-done.2.in_ref = bf16[8,64,256]{2,1,0:T(8,128)(2,1)S(1)} async-done(((bf16[8,64,256]{2,1,0:T(8,128)(2,1)}), bf16[8,64,256]{2,1,0:T(8,128)(2,1)S(1)}, u32[]{:S(2)}, u32[]{:S(2)}) %all-to-all-start.2) | async-done | bytes 262176 | tf_op jit(solution)/shard_map/all_to_all | solution.py:341
  70.0 0.7 final_sum.1
Async XLA Ops:
  0.6 4.7 %collective-permute-start = (bf16[768,128]{1,0:T(8,128)(2,1)}, bf16[768,128]{1,0:T(8,128)(2,1)S(1)}, u32[]{:S(2)}, u32[]{:S(2)}) collective-permute-start(bf16[768,128]{1,0:T(8,128)(2,1)} %k_ref.1), channel_id=1, source_target_pairs={{0,8},{8,0},{1,9},{9,1},{2,10},{10,2},{3,11},{11,3},{4,12},{12,4},... | collective-permute-start | bytes 589832 | tf_op jit(solution)/shard_map/ppermute | solution.py:337
  4.0 1.7 %collective-permute-start.1 = (bf16[768,128]{1,0:T(8,128)(2,1)}, bf16[768,128]{1,0:T(8,128)(2,1)S(1)}, u32[]{:S(2)}, u32[]{:S(2)}) collective-permute-start(bf16[768,128]{1,0:T(8,128)(2,1)} %v_ref.1), channel_id=1, source_target_pairs={{0,8},{8,0},{1,9},{9,1},{2,10},{10,2},{3,11},{11,3},{4,12},{12,4},... | collective-permute-start | bytes 589832 | tf_op jit(solution)/shard_map/ppermute | solution.py:337
  10.7 17.7 %all-to-all-start = ((bf16[16,192,128]{2,1,0:T(8,128)(2,1)}), bf16[16,192,128]{2,1,0:T(8,128)(2,1)S(1)}, u32[]{:S(2)}, u32[]{:S(2)}) async-start(bf16[16,192,128]{2,1,0:T(8,128)(2,1)} %query_attention.1.after_ref), calls=%async_computation | async-start | bytes 1572864 | tf_op jit(solution)/shard_map/all_to_all | solution.py:341
  28.4 21.1 %copy-start = (bf16[1024,256]{1,0:T(8,128)(2,1)S(1)}, bf16[1024,256]{1,0:T(8,128)(2,1)}, u32[]{:S(2)}) copy-start(bf16[1024,256]{1,0:T(8,128)(2,1)} %w_ref.1) | copy-start | bytes 1572868
  44.7 4.8 %collective-permute-start.2 = (bf16[16,176,128]{2,1,0:T(8,128)(2,1)S(1)}, bf16[16,176,128]{2,1,0:T(8,128)(2,1)S(1)}, u32[]{:S(2)}, u32[]{:S(2)}) collective-permute-start(bf16[16,176,128]{2,1,0:T(8,128)(2,1)S(1)} %all_to_all.15.mine_ref), channel_id=1, source_target_pairs={{0,8},{8,0},{1,9},{9,1},{2,10},{10,2},{3,11},{11,3},{4,12},{12,4},... | collective-permute-start | bytes 2162696 | tf_op jit(solution)/shard_map/ppermute | solution.py:337
  50.8 19.2 %all-to-all-start.2 = ((bf16[8,64,256]{2,1,0:T(8,128)(2,1)}), bf16[8,64,256]{2,1,0:T(8,128)(2,1)S(1)}, u32[]{:S(2)}, u32[]{:S(2)}) async-start(bf16[8,64,256]{2,1,0:T(8,128)(2,1)} %get-tuple-element.17), calls=%async_computation.2 | async-start | bytes 524288 | tf_op jit(solution)/shard_map/all_to_all | solution.py:341

commit v9 on v8

--- a/solution.py
+++ b/solution.py
@@ -119,7 +119,29 @@
         out_ref[g, HEAD:SEND2, :] = anchor
 
 
-def project_kernel(mine_ref, other_ref, w_ref, out_hbm, k_hbm, v_hbm, out_ref, k_ref, v_ref, sems):
+def project_rows(ref, w_ref, owner, out_hbm, out_ref, sem):
+    a = jnp.concatenate(
+        [
+            jnp.concatenate([ref[2 * j + half, 0:HEAD, :] for j in range(HEADS)], axis=1)
+            for half in range(2)
+        ],
+        axis=0,
+    )
+    y = jnp.dot(a, w_ref[...], preferred_element_type=F32).astype(BF)
+    for z in range(4):
+        out_ref[z] = y[64 * z : 64 * z + 64, :]
+    copy = pltpu.make_async_copy(out_ref, out_hbm.at[pl.ds(4 * owner, 4)], sem)
+    copy.start()
+    return copy
+
+
+def project_mine_kernel(mine_ref, w_ref, out_hbm, out_ref, sem):
+    project_rows(mine_ref, w_ref, lax.axis_index("c"), out_hbm, out_ref, sem).wait()
+
+
+def project_other_kernel(
+    half_done_hbm, mine_ref, other_ref, w_ref, out_hbm, k_hbm, v_hbm, out_ref, k_ref, v_ref, sem, sems
+):
     core = lax.axis_index("c")
     for g in range(16):
         rows = slice(g * ANCHOR_ROWS, (g + 1) * ANCHOR_ROWS)
@@ -132,29 +154,9 @@
     ]
     for copy in copies:
         copy.start()
-    for ref, owner in ((mine_ref, core), (other_ref, 1 - core)):
-        a = jnp.concatenate(
-            [
-                jnp.concatenate([ref[2 * j + half, 0:HEAD, :] for j in range(HEADS)], axis=1)
-                for half in range(2)
-            ],
-            axis=0,
-        )
-        y = jnp.dot(a, w_ref[...], preferred_element_type=F32).astype(BF)
-        for z in range(4):
-            out_ref[4 * owner + z] = y[64 * z : 64 * z + 64, :]
-        half = pl.ds(4 * owner, 4)
-        copies.append(pltpu.make_async_copy(out_ref.at[half], out_hbm.at[half], sems.at[len(copies)]))
-        copies[-1].start()
+    copies.append(project_rows(other_ref, w_ref, 1 - core, out_hbm, out_ref, sem))
     for copy in copies:
         copy.wait()
-
-
-def final_kernel(in_ref, out_ref):
-    total = in_ref[0].astype(F32)
-    for z in range(1, 8):
-        total = total + in_ref[z].astype(F32)
-    out_ref[...] = total.astype(BF)
 
 
 STEP = 2
@@ -264,7 +266,7 @@
     return pltpu.VMEM(dims, dtype)
 
 
-def run(kernel, name, operands, in_specs, out_shape, out_specs, scratch, flops, nbytes, exps=0, grid=()):
+def run(kernel, name, operands, in_specs, out_shape, out_specs, scratch, flops, nbytes, exps=0, grid=(), aliases=None):
     return pl.pallas_call(
         kernel,
         grid=grid,
@@ -272,6 +274,7 @@
         out_specs=out_specs,
         out_shape=out_shape,
         scratch_shapes=scratch,
+        input_output_aliases=aliases or {},
         compiler_params=pltpu.CompilerParams(vmem_limit_bytes=24 * 1024 * 1024),
         cost_estimate=pl.CostEstimate(flops=flops, bytes_accessed=nbytes, transcendentals=exps),
         name=name,
@@ -320,17 +323,28 @@
     )
 
 
-def project_call(mine, other, w):
-    return run(
-        project_kernel, "project", (mine, other, w), [VMEM] * 3,
+def project_mine_call(mine, w):
+    return run(
+        project_mine_kernel, "project_mine", (mine, w), [VMEM] * 2,
+        pltpu.HBM((8, 64, 256), BF), HBM,
+        [buffer((4, 64, 256)), pltpu.SemaphoreType.DMA], 2 * 256 * 1024 * 256, 1 << 20,
+    )
+
+
+def project_other_call(half_done, mine, other, w):
+    return run(
+        project_other_kernel, "project_other", (*in_hbm(half_done), mine, other, w), [HBM] + [VMEM] * 3,
         (pltpu.HBM((8, 64, 256), BF), pltpu.HBM((BLOCK, HEAD), BF), pltpu.HBM((BLOCK, HEAD), BF)), (HBM,) * 3,
-        [buffer((8, 64, 256)), buffer((BLOCK, HEAD)), buffer((BLOCK, HEAD)), pltpu.SemaphoreType.DMA((4,))],
-        2 * 512 * 1024 * 256, 2 << 20,
-    )
-
-
-def final_call(received):
-    return run(final_kernel, "final_sum", (received,), [VMEM], shape((64, 256)), VMEM, [], 1 << 17, 1 << 18)
+        [
+            buffer((4, 64, 256)), buffer((BLOCK, HEAD)), buffer((BLOCK, HEAD)),
+            pltpu.SemaphoreType.DMA, pltpu.SemaphoreType.DMA((2,)),
+        ],
+        2 * 256 * 1024 * 256, 1 << 20, aliases={0: 0},
+    )
+
+
+def final_sum(received):
+    return jnp.sum(received.astype(F32), axis=0).astype(BF)
 
 
 def swap(value):
@@ -348,9 +362,11 @@
     received = exchange(sent, ("x", "y"))
     own, lse = own_call(ctx_query, context_key, context_value, sent)
     gathered = exchange(combine_call(received, lse), ("x", "y"))
-    shares, key_a, value_a = project_call(gathered, swap(gathered), out_weight)
+    other = swap(gathered)
+    half_done = project_mine_call(gathered, out_weight)
+    shares, key_a, value_a = project_other_call(half_done, gathered, other, out_weight)
     ctx_out = anchor_call(ctx_query, key_a, value_a, own, lse)
-    answer = final_call(exchange(shares, "z"))
+    answer = final_sum(exchange(shares, "z"))
     return ctx_out, answer
 
 

time: 71.1 us -> 71 us (level)
  waiting for transfers between devices: 9.53 us -> 8.65 us
    ppermute x3, waiting for transfers between devices: 2.05 us -> 1.07 us  [swap(): return lax.ppermute(value, 'c', [(0, 1), (1, 0)])]
  transfers between devices with their start and end apart: 5 -> 5, of which waited for: 4 -> 4; matrix products, arithmetic and copies ran while one was open for 0% -> 0% of each run, Pallas kernels for 25% -> 26%
where the time goes in v9:
time: 71 us; the launch traced here: 70.6 us
  Pallas kernels  25.2 us (35%)
  starting transfers between devices  19.6 us (28%)
  blocking collectives  15.7 us (22%)
  waiting for transfers between devices  8.65 us (12%)
    pallas_call x7, Pallas kernels, run(): pl.pallas_call(kernel, grid=grid, in_specs=in_specs, out_specs=out_specs,...  25.2 us
    all_to_all x1, blocking collectives, exchange(): return lax.all_to_all(value, axes, 0, 0, tiled=True)  15.7 us
    all_to_all x2, starting transfers between devices, exchange(): return lax.all_to_all(value, axes, 0, 0, tiled=True)  13.2 us
    all_to_all x2, waiting for transfers between devices, exchange(): return lax.all_to_all(value, axes, 0, 0, tiled=True)  7.58 us
    ppermute x3, starting transfers between devices, swap(): return lax.ppermute(value, 'c', [(0, 1), (1, 0)])  6.41 us
  transfers between devices with their start and end apart: 5, of which 4 were waited for; matrix products, arithmetic and copies ran while one was open for 0% of the time, Pallas kernels for 26%

profile of v9, /device:TPU:1, one launch (start us, length us, event | category | flops | bytes accessed | tf_op | source)
XLA Modules:
  0.0 70.6 jit_solution(1632602598440435318)
XLA Ops:
  0.6 3.3 %collective-permute-start = (bf16[768,128]{1,0:T(8,128)(2,1)}, bf16[768,128]{1,0:T(8,128)(2,1)S(1)}, u32[]{:S(2)}, u32[]{:S(2)}) collective-permute-start(bf16[768,128]{1,0:T(8,128)(2,1)} %k_ref.1), channel_id=1, source_target_pairs={{0,8},{8,0},{1,9},{9,1},{2,10},{10,2},{3,11},{11,3},{4,12},{12,4},... | collective-permute-start | bytes 589832 | tf_op jit(solution)/shard_map/ppermute | solution.py:351
  4.0 0.1 collective-permute-start.1
  4.1 1.3 %prep.1 = (bf16[256,1024]{1,0:T(8,128)(2,1)S(1)}, bf16[768,128]{1,0:T(8,128)(2,1)S(1)}, bf16[768,256]{1,0:T(8,128)(2,1)S(1)}) custom-call(bf16[512,1024]{1,0:T(8,128)(2,1)} %q_hbm.1, bf16[768,128]{1,0:T(8,128)(2,1)} %k_ref.1, bf16[768,128]{1,0:T(8,128)(2,1)} %v_ref.1), custom_call_target="tpu_custom_call" | custom-call | flops 262144 | bytes 2097152 | tf_op jit(solution)/shard_map/prep/pallas_call | solution.py:270
  5.4 0.0 collective-permute-done.kp_ref
  5.4 0.2 collective-permute-done.1.vp_ref
  5.6 5.1 %query_attention.1.after_ref = bf16[16,192,128]{2,1,0:T(8,128)(2,1)} custom-call(bf16[256,1024]{1,0:T(8,128)(2,1)S(1)} %get-tuple-element.10.q_ref, bf16[768,128]{1,0:T(8,128)(2,1)S(1)} %get-tuple-element.11.k_ref, bf16[768,256]{1,0:T(8,128)(2,1)S(1)} %get-tuple-element.12.values_ref, bf16[768,128]{1,0:T(8,128)(2,1)S(1)} %collective-permute-done.kp_ref, ...), custom_call_target="tpu_custom_call" | custom-call | flops 3221225472 | bytes 3145728 | tf_op jit(solution)/shard_map/query_attention/pallas_call | solution.py:270
  10.7 5.0 %all-to-all-start = ((bf16[16,192,128]{2,1,0:T(8,128)(2,1)}), bf16[16,192,128]{2,1,0:T(8,128)(2,1)S(1)}, u32[]{:S(2)}, u32[]{:S(2)}) async-start(bf16[16,192,128]{2,1,0:T(8,128)(2,1)} %query_attention.1.after_ref), calls=%async_computation | async-start | bytes 1572864 | tf_op jit(solution)/shard_map/all_to_all | solution.py:355
  15.7 7.5 %context_own.1 = (bf16[768,1024]{1,0:T(8,128)(2,1)}, f32[768,128]{1,0:T(8,128)}) custom-call(bf16[768,1024]{1,0:T(8,128)(2,1)} %q_ref.3, bf16[768,128]{1,0:T(8,128)(2,1)} %k_ref.1, bf16[768,128]{1,0:T(8,128)(2,1)} %v_ref.1, bf16[16,192,128]{2,1,0:T(8,128)(2,1)} %query_attention.1.after_ref), custom_call_target="tpu_custom_call" | custom-call | flops 3221225472 | bytes 4194304 | tf_op jit(solution)/shard_map/context_own/pallas_call | solution.py:270
  23.2 5.2 %all-to-all-done.in_ref = bf16[16,192,128]{2,1,0:T(8,128)(2,1)S(1)} async-done(((bf16[16,192,128]{2,1,0:T(8,128)(2,1)}), bf16[16,192,128]{2,1,0:T(8,128)(2,1)S(1)}, u32[]{:S(2)}, u32[]{:S(2)}) %all-to-all-start) | async-done | bytes 786464 | tf_op jit(solution)/shard_map/all_to_all | solution.py:355
  28.4 0.0 copy-start
  28.4 0.5 combine.1
  29.0 15.7 %all_to_all.15.mine_ref = bf16[16,176,128]{2,1,0:T(8,128)(2,1)S(1)} all-to-all(bf16[16,176,128]{2,1,0:T(8,128)(2,1)S(1)} %combine.1), channel_id=1, replica_groups=mesh['y'=4,'x'=4,'c'=2,'z'=8] {'x','y'}, dimensions={0} | all-to-all | bytes 1441792 | tf_op jit(solution)/shard_map/all_to_all | solution.py:355
  44.7 3.0 %collective-permute-start.2 = (bf16[16,176,128]{2,1,0:T(8,128)(2,1)S(1)}, bf16[16,176,128]{2,1,0:T(8,128)(2,1)S(1)}, u32[]{:S(2)}, u32[]{:S(2)}) collective-permute-start(bf16[16,176,128]{2,1,0:T(8,128)(2,1)S(1)} %all_to_all.15.mine_ref), channel_id=1, source_target_pairs={{0,8},{8,0},{1,9},{9,1},{2,10},{10,2},{3,11},{11,3},{4,12},{12,4},... | collective-permute-start | bytes 2162696 | tf_op jit(solution)/shard_map/ppermute | solution.py:351
  47.7 0.0 copy-done
  47.7 1.0 %project_mine.1.half_done_hbm = bf16[8,64,256]{2,1,0:T(8,128)(2,1)} custom-call(bf16[16,176,128]{2,1,0:T(8,128)(2,1)S(1)} %all_to_all.15.mine_ref, bf16[1024,256]{1,0:T(8,128)(2,1)S(1)} %copy-done), custom_call_target="tpu_custom_call" | custom-call | flops 134217728 | bytes 1048576 | tf_op jit(solution)/shard_map/project_mine/pallas_call | solution.py:270
  48.6 0.8 %collective-permute-done.2.other_ref = bf16[16,176,128]{2,1,0:T(8,128)(2,1)S(1)} collective-permute-done((bf16[16,176,128]{2,1,0:T(8,128)(2,1)S(1)}, bf16[16,176,128]{2,1,0:T(8,128)(2,1)S(1)}, u32[]{:S(2)}, u32[]{:S(2)}) %collective-permute-start.2) | collective-permute-done | bytes 720928 | tf_op jit(solution)/shard_map/ppermute | solution.py:351
  49.5 1.1 %project_other.1 = (bf16[8,64,256]{2,1,0:T(8,128)(2,1)}, bf16[768,128]{1,0:T(8,128)(2,1)}, bf16[768,128]{1,0:T(8,128)(2,1)}) custom-call(bf16[8,64,256]{2,1,0:T(8,128)(2,1)} %project_mine.1.half_done_hbm, bf16[16,176,128]{2,1,0:T(8,128)(2,1)S(1)} %all_to_all.15.mine_ref, ...), custom_call_target="tpu_custom_call", output_to_operand_aliasing={{0}: (0, {})} | custom-call | flops 134217728 | bytes 1048576 | tf_op jit(solution)/shard_map/project_other/pallas_call | solution.py:270
  50.6 8.2 %all-to-all-start.2 = ((bf16[8,64,256]{2,1,0:T(8,128)(2,1)}), bf16[8,64,256]{2,1,0:T(8,128)(2,1)S(1)}, u32[]{:S(2)}, u32[]{:S(2)}) async-start(bf16[8,64,256]{2,1,0:T(8,128)(2,1)} %get-tuple-element.17), calls=%async_computation.2 | async-start | bytes 524288 | tf_op jit(solution)/shard_map/all_to_all | solution.py:355
  58.8 8.7 %context_anchor.1 = bf16[768,1024]{1,0:T(8,128)(2,1)} custom-call(bf16[768,1024]{1,0:T(8,128)(2,1)} %q_ref.3, bf16[768,128]{1,0:T(8,128)(2,1)} %get-tuple-element.14.k_ref, bf16[768,128]{1,0:T(8,128)(2,1)} %get-tuple-element.15.v_ref, bf16[768,1024]{1,0:T(8,128)(2,1)} %get-tuple-element.16.own_ref, f32[768,128]{1,0:T(8,128)} %get-tuple-element.13.after_ref.lse_ref), custom_call_target="tpu_custom_call" | custom-call | flops 4831838208 | bytes 6291456 | tf_op jit(solution)/shard_map/context_anchor/pallas_call | solution.py:270
  67.5 2.4 %all-to-all-done.2 = bf16[8,64,256]{2,1,0:T(8,128)(2,1)S(1)} async-done(((bf16[8,64,256]{2,1,0:T(8,128)(2,1)}), bf16[8,64,256]{2,1,0:T(8,128)(2,1)S(1)}, u32[]{:S(2)}, u32[]{:S(2)}) %all-to-all-start.2) | async-done | bytes 262176 | tf_op jit(solution)/shard_map/all_to_all | solution.py:355
  69.9 0.7 reduce_sum.12
Async XLA Ops:
  0.6 4.7 %collective-permute-start = (bf16[768,128]{1,0:T(8,128)(2,1)}, bf16[768,128]{1,0:T(8,128)(2,1)S(1)}, u32[]{:S(2)}, u32[]{:S(2)}) collective-permute-start(bf16[768,128]{1,0:T(8,128)(2,1)} %k_ref.1), channel_id=1, source_target_pairs={{0,8},{8,0},{1,9},{9,1},{2,10},{10,2},{3,11},{11,3},{4,12},{12,4},... | collective-permute-start | bytes 589832 | tf_op jit(solution)/shard_map/ppermute | solution.py:351
  4.0 1.7 %collective-permute-start.1 = (bf16[768,128]{1,0:T(8,128)(2,1)}, bf16[768,128]{1,0:T(8,128)(2,1)S(1)}, u32[]{:S(2)}, u32[]{:S(2)}) collective-permute-start(bf16[768,128]{1,0:T(8,128)(2,1)} %v_ref.1), channel_id=1, source_target_pairs={{0,8},{8,0},{1,9},{9,1},{2,10},{10,2},{3,11},{11,3},{4,12},{12,4},... | collective-permute-start | bytes 589832 | tf_op jit(solution)/shard_map/ppermute | solution.py:351
  10.7 17.7 %all-to-all-start = ((bf16[16,192,128]{2,1,0:T(8,128)(2,1)}), bf16[16,192,128]{2,1,0:T(8,128)(2,1)S(1)}, u32[]{:S(2)}, u32[]{:S(2)}) async-start(bf16[16,192,128]{2,1,0:T(8,128)(2,1)} %query_attention.1.after_ref), calls=%async_computation | async-start | bytes 1572864 | tf_op jit(solution)/shard_map/all_to_all | solution.py:355
  28.4 19.3 %copy-start = (bf16[1024,256]{1,0:T(8,128)(2,1)S(1)}, bf16[1024,256]{1,0:T(8,128)(2,1)}, u32[]{:S(2)}) copy-start(bf16[1024,256]{1,0:T(8,128)(2,1)} %w_ref.3) | copy-start | bytes 1572868
  44.7 4.8 %collective-permute-start.2 = (bf16[16,176,128]{2,1,0:T(8,128)(2,1)S(1)}, bf16[16,176,128]{2,1,0:T(8,128)(2,1)S(1)}, u32[]{:S(2)}, u32[]{:S(2)}) collective-permute-start(bf16[16,176,128]{2,1,0:T(8,128)(2,1)S(1)} %all_to_all.15.mine_ref), channel_id=1, source_target_pairs={{0,8},{8,0},{1,9},{9,1},{2,10},{10,2},{3,11},{11,3},{4,12},{12,4},... | collective-permute-start | bytes 2162696 | tf_op jit(solution)/shard_map/ppermute | solution.py:351
  50.6 19.3 %all-to-all-start.2 = ((bf16[8,64,256]{2,1,0:T(8,128)(2,1)}), bf16[8,64,256]{2,1,0:T(8,128)(2,1)S(1)}, u32[]{:S(2)}, u32[]{:S(2)}) async-start(bf16[8,64,256]{2,1,0:T(8,128)(2,1)} %get-tuple-element.17), calls=%async_computation.2 | async-start | bytes 524288 | tf_op jit(solution)/shard_map/all_to_all | solution.py:355

commit v10 on v8

--- a/solution.py
+++ b/solution.py
@@ -54,14 +54,16 @@
     values_ref[:, 0:HEAD] = v_buf[...]
 
 
-def query_kernel(q_ref, k_ref, values_ref, kp_ref, vp_ref, out_hbm, values_p, out_ref, sems):
+def query_kernel(first_head, q_ref, k_ref, values_ref, kp_ref, vp_ref, *refs):
+    out_hbm, values_p, out_ref, sems = refs[-4:]
     core = lax.axis_index("c")
     values_p[:, 0:HEAD] = vp_ref[...]
     values_p[:, HEAD : 2 * HEAD] = jnp.ones((BLOCK, HEAD), BF)
     row_id = lax.broadcasted_iota(jnp.int32, (16, HEAD), 0)
 
     def scores(j):
-        q = q_ref[:, HEAD * j : HEAD * j + HEAD]
+        at = HEAD * (first_head + j)
+        q = q_ref[:, at : at + HEAD]
         return scores_of(q, k_ref[...]), scores_of(q, kp_ref[...])
 
     def finish(j, s):
@@ -83,21 +85,21 @@
             stats = jnp.where(row_id == 1, high, stats)
             stats = jnp.where(row_id == 2, total_l - high, stats)
             out_ref[2 * j + half, HEAD:STATS, :] = stats.astype(BF)
-            at = (2 * j + half) * ANCHOR_ROWS
+            at = (2 * (first_head + j) + half) * ANCHOR_ROWS
             out_ref[2 * j + half, STATS:SEND1, :] = jnp.where(
                 core == 0, k_ref[at : at + ANCHOR_ROWS, :], vp_ref[at : at + ANCHOR_ROWS, :]
             )
 
     def write(j):
-        rows = slice(2 * j, 2 * j + 2)
-        return pltpu.make_async_copy(out_ref.at[rows], out_hbm.at[rows], sems.at[j])
+        rows = slice(2 * (first_head + j), 2 * (first_head + j) + 2)
+        return pltpu.make_async_copy(out_ref.at[2 * j : 2 * j + 2], out_hbm.at[rows], sems.at[j])
 
     def finish_and_write(j, s):
         finish(j, s)
         write(j).start()
 
-    pipelined(HEADS, scores, finish_and_write)
-    for j in range(HEADS):
+    pipelined(HEADS // 2, scores, finish_and_write)
+    for j in range(HEADS // 2):
         write(j).wait()
 
 
@@ -247,6 +249,7 @@
 
 VMEM = pl.BlockSpec(memory_space=pltpu.VMEM)
 HBM = pl.BlockSpec(memory_space=pltpu.HBM)
+ANY = pl.BlockSpec(memory_space=pl.ANY)
 WIDE = HEADS * HEAD
 STEP_BLOCK = pl.BlockSpec((BLOCK, STEP_COLUMNS), lambda t: (0, t))
 HEAD_BLOCK = pl.BlockSpec((BLOCK, HEAD), lambda t: (0, 0))
@@ -264,7 +267,7 @@
     return pltpu.VMEM(dims, dtype)
 
 
-def run(kernel, name, operands, in_specs, out_shape, out_specs, scratch, flops, nbytes, exps=0, grid=()):
+def run(kernel, name, operands, in_specs, out_shape, out_specs, scratch, flops, nbytes, exps=0, grid=(), aliases=None):
     return pl.pallas_call(
         kernel,
         grid=grid,
@@ -272,6 +275,7 @@
         out_specs=out_specs,
         out_shape=out_shape,
         scratch_shapes=scratch,
+        input_output_aliases=aliases or {},
         compiler_params=pltpu.CompilerParams(vmem_limit_bytes=24 * 1024 * 1024),
         cost_estimate=pl.CostEstimate(flops=flops, bytes_accessed=nbytes, transcendentals=exps),
         name=name,
@@ -286,12 +290,14 @@
     )
 
 
-def query_call(q, k, values, kp, vp):
-    return run(
-        query_kernel, "query_attention", (q, k, values, kp, vp), [VMEM] * 5,
+def query_call(first_head, q, k, values, kp, vp, *more, anywhere=()):
+    return run(
+        functools.partial(query_kernel, first_head), f"query_attention_{first_head}",
+        (q, k, values, kp, vp, *in_hbm(*more), *anywhere),
+        [VMEM] * 5 + [HBM] * len(more) + [ANY] * len(anywhere),
         pltpu.HBM((16, SEND1, HEAD), BF), HBM,
-        [buffer((BLOCK, 2 * HEAD)), buffer((16, SEND1, HEAD)), pltpu.SemaphoreType.DMA((HEADS,))],
-        4 * 2048 * 1536 * 256, 3 << 20, 2048 * 1536,
+        [buffer((BLOCK, 2 * HEAD)), buffer((HEADS, SEND1, HEAD)), pltpu.SemaphoreType.DMA((HEADS // 2,))],
+        2 * 2048 * 1536 * 256, 3 << 20, 1024 * 1536, aliases={5: 0} if more else None,
     )
 
 
@@ -337,6 +343,11 @@
     return lax.ppermute(value, "c", [(0, 1), (1, 0)])
 
 
+def greet(axis, size):
+    few = jnp.ones((16, HEAD), BF)
+    return lax.ppermute(few, axis, [(i, (i + 1) % size) for i in range(size)])
+
+
 def exchange(value, axes):
     return lax.all_to_all(value, axes, 0, 0, tiled=True)
 
@@ -344,7 +355,9 @@
 def per_device(ctx_query, context_key, context_value, query, out_weight):
     key_p, value_p = swap(context_key), swap(context_value)
     q, k, values = prep_call(query, context_key, context_value)
-    sent = query_call(q, k, values, key_p, value_p)
+    greetings = (greet("x", 4), greet("y", 4))
+    half_sent = query_call(0, q, k, values, key_p, value_p)
+    sent = query_call(HEADS // 2, q, k, values, key_p, value_p, half_sent, anywhere=greetings)
     received = exchange(sent, ("x", "y"))
     own, lse = own_call(ctx_query, context_key, context_value, sent)
     gathered = exchange(combine_call(received, lse), ("x", "y"))

time: 71.1 us -> 73.3 us (1.031)
  starting transfers between devices: 19.6 us -> 22.3 us
  blocking collectives: 15.7 us -> 14.1 us
  Pallas kernels: 25.1 us -> 26.2 us
    all_to_all x1, blocking collectives: 15.7 us -> 14.1 us  [exchange(): return lax.all_to_all(value, axes, 0, 0, tiled=True)]
    all_to_all x2, starting transfers between devices: 13.2 us -> 14.4 us  [exchange(): return lax.all_to_all(value, axes, 0, 0, tiled=True)]
    pallas_call x7 -> x8, Pallas kernels: 25.1 us -> 26.2 us  [run(): pl.pallas_call(kernel, grid=grid, in_specs=in_specs, out_specs=out_specs,...]
    ppermute x0 -> x2, starting transfers between devices: none -> 0.77 us  [greet(): return lax.ppermute(few, axis, [(i, (i + 1) % size) for i in range(size)])]
  transfers between devices with their start and end apart: 5 -> 7, of which waited for: 4 -> 3; matrix products, arithmetic and copies ran while one was open for 0% -> 0% of each run, Pallas kernels for 25% -> 28%
where the time goes in v10:
time: 73.3 us; the launch traced here: 72.8 us
  Pallas kernels  26.2 us (36%)
  starting transfers between devices  22.3 us (30%)
  blocking collectives  14.1 us (19%)
  waiting for transfers between devices  9.45 us (13%)
    pallas_call x8, Pallas kernels, run(): pl.pallas_call(kernel, grid=grid, in_specs=in_specs, out_specs=out_specs,...  26.2 us
    all_to_all x2, starting transfers between devices, exchange(): return lax.all_to_all(value, axes, 0, 0, tiled=True)  14.4 us
    all_to_all x1, blocking collectives, exchange(): return lax.all_to_all(value, axes, 0, 0, tiled=True)  14.1 us
    all_to_all x2, waiting for transfers between devices, exchange(): return lax.all_to_all(value, axes, 0, 0, tiled=True)  7.62 us
    ppermute x3, starting transfers between devices, swap(): return lax.ppermute(value, 'c', [(0, 1), (1, 0)])  7.12 us
    ppermute x3, waiting for transfers between devices, swap(): return lax.ppermute(value, 'c', [(0, 1), (1, 0)])  1.82 us
  transfers between devices with their start and end apart: 7, of which 3 were waited for; matrix products, arithmetic and copies ran while one was open for 0% of the time, Pallas kernels for 28%

profile of v10, /device:TPU:1, one launch (start us, length us, event | category | flops | bytes accessed | tf_op | source)
XLA Modules:
  0.0 72.8 jit_solution(9514880069210949993)
XLA Ops:
  0.6 3.3 %collective-permute-start = (bf16[768,128]{1,0:T(8,128)(2,1)}, bf16[768,128]{1,0:T(8,128)(2,1)S(1)}, u32[]{:S(2)}, u32[]{:S(2)}) collective-permute-start(bf16[768,128]{1,0:T(8,128)(2,1)} %k_ref.1), channel_id=1, source_target_pairs={{0,8},{8,0},{1,9},{9,1},{2,10},{10,2},{3,11},{11,3},{4,12},{12,4},... | collective-permute-start | bytes 589832 | tf_op jit(solution)/shard_map/ppermute | solution.py:343
  4.0 0.1 collective-permute-start.1
  4.1 0.0 collective-permute-start.3
  4.1 0.8 %collective-permute-start.2 = (bf16[16,128]{1,0:T(8,128)(2,1)S(1)}, bf16[16,128]{1,0:T(8,128)(2,1)S(1)}, u32[]{:S(2)}, u32[]{:S(2)}) collective-permute-start(bf16[16,128]{1,0:T(8,128)(2,1)S(1)} %broadcast.3), channel_id=1, source_target_pairs={{0,16},{16,32},{32,48},{48,0},{1,17},{17,33},{33,49},{49,1},{2,18}... | collective-permute-start | bytes 12296 | tf_op jit(solution)/shard_map/ppermute | solution.py:348
  4.8 1.3 %prep.1 = (bf16[256,1024]{1,0:T(8,128)(2,1)S(1)}, bf16[768,128]{1,0:T(8,128)(2,1)S(1)}, bf16[768,256]{1,0:T(8,128)(2,1)S(1)}) custom-call(bf16[512,1024]{1,0:T(8,128)(2,1)} %q_hbm.1, bf16[768,128]{1,0:T(8,128)(2,1)} %k_ref.1, bf16[768,128]{1,0:T(8,128)(2,1)} %v_ref.1), custom_call_target="tpu_custom_call" | custom-call | flops 262144 | bytes 2097152 | tf_op jit(solution)/shard_map/prep/pallas_call | solution.py:271
  6.1 0.0 collective-permute-done.kp_ref
  6.2 0.0 collective-permute-done.1.vp_ref
  6.2 3.1 %query_attention_0.1.refs_0_ = bf16[16,192,128]{2,1,0:T(8,128)(2,1)} custom-call(bf16[256,1024]{1,0:T(8,128)(2,1)S(1)} %get-tuple-element.10.q_ref, bf16[768,128]{1,0:T(8,128)(2,1)S(1)} %get-tuple-element.11.k_ref, bf16[768,256]{1,0:T(8,128)(2,1)S(1)} %get-tuple-element.12.values_ref, bf16[768,128]{1,0:T(8,128)(2,1)S(1)} %collective-permute-done.kp_ref, ...), custom_call_target="tpu_custom_call" | custom-call | flops 1610612736 | bytes 3145728 | tf_op jit(solution)/shard_map/query_attention_0/pallas_call | solution.py:271
  9.3 0.0 collective-permute-done.3.refs_2_
  9.3 0.0 collective-permute-done.2.refs_1_
  9.3 3.1 %query_attention_4.1.after_ref = bf16[16,192,128]{2,1,0:T(8,128)(2,1)} custom-call(bf16[256,1024]{1,0:T(8,128)(2,1)S(1)} %get-tuple-element.10.q_ref, bf16[768,128]{1,0:T(8,128)(2,1)S(1)} %get-tuple-element.11.k_ref, bf16[768,256]{1,0:T(8,128)(2,1)S(1)} %get-tuple-element.12.values_ref, ...), custom_call_target="tpu_custom_call", output_to_operand_aliasing={{}: (5, {})} | custom-call | flops 1610612736 | bytes 3145728 | tf_op jit(solution)/shard_map/query_attention_4/pallas_call | solution.py:271
  12.4 6.2 %all-to-all-start = ((bf16[16,192,128]{2,1,0:T(8,128)(2,1)}), bf16[16,192,128]{2,1,0:T(8,128)(2,1)S(1)}, u32[]{:S(2)}, u32[]{:S(2)}) async-start(bf16[16,192,128]{2,1,0:T(8,128)(2,1)} %query_attention_4.1.after_ref), calls=%async_computation | async-start | bytes 1572864 | tf_op jit(solution)/shard_map/all_to_all | solution.py:352
  18.6 7.5 %context_own.1 = (bf16[768,1024]{1,0:T(8,128)(2,1)}, f32[768,128]{1,0:T(8,128)}) custom-call(bf16[768,1024]{1,0:T(8,128)(2,1)} %q_ref.3, bf16[768,128]{1,0:T(8,128)(2,1)} %k_ref.1, bf16[768,128]{1,0:T(8,128)(2,1)} %v_ref.1, bf16[16,192,128]{2,1,0:T(8,128)(2,1)} %query_attention_4.1.after_ref), custom_call_target="tpu_custom_call" | custom-call | flops 3221225472 | bytes 4194304 | tf_op jit(solution)/shard_map/context_own/pallas_call | solution.py:271
  26.1 5.3 %all-to-all-done.in_ref = bf16[16,192,128]{2,1,0:T(8,128)(2,1)S(1)} async-done(((bf16[16,192,128]{2,1,0:T(8,128)(2,1)}), bf16[16,192,128]{2,1,0:T(8,128)(2,1)S(1)}, u32[]{:S(2)}, u32[]{:S(2)}) %all-to-all-start) | async-done | bytes 786464 | tf_op jit(solution)/shard_map/all_to_all | solution.py:352
  31.4 0.0 copy-start
  31.4 0.5 combine.1
  31.9 14.1 %all_to_all.15.mine_ref = bf16[16,176,128]{2,1,0:T(8,128)(2,1)S(1)} all-to-all(bf16[16,176,128]{2,1,0:T(8,128)(2,1)S(1)} %combine.1), channel_id=1, replica_groups=mesh['y'=4,'x'=4,'c'=2,'z'=8] {'x','y'}, dimensions={0} | all-to-all | bytes 1441792 | tf_op jit(solution)/shard_map/all_to_all | solution.py:352
  46.0 3.7 %collective-permute-start.4 = (bf16[16,176,128]{2,1,0:T(8,128)(2,1)S(1)}, bf16[16,176,128]{2,1,0:T(8,128)(2,1)S(1)}, u32[]{:S(2)}, u32[]{:S(2)}) collective-permute-start(bf16[16,176,128]{2,1,0:T(8,128)(2,1)S(1)} %all_to_all.15.mine_ref), channel_id=1, source_target_pairs={{0,8},{8,0},{1,9},{9,1},{2,10},{10,2},{3,11},{11,3},{4,12},{12,4},... | collective-permute-start | bytes 2162696 | tf_op jit(solution)/shard_map/ppermute | solution.py:343
  49.7 1.8 %collective-permute-done.4.other_ref = bf16[16,176,128]{2,1,0:T(8,128)(2,1)S(1)} collective-permute-done((bf16[16,176,128]{2,1,0:T(8,128)(2,1)S(1)}, bf16[16,176,128]{2,1,0:T(8,128)(2,1)S(1)}, u32[]{:S(2)}, u32[]{:S(2)}) %collective-permute-start.4) | collective-permute-done | bytes 720928 | tf_op jit(solution)/shard_map/ppermute | solution.py:343
  51.6 0.0 copy-done
  51.6 1.3 %project.1 = (bf16[8,64,256]{2,1,0:T(8,128)(2,1)}, bf16[768,128]{1,0:T(8,128)(2,1)}, bf16[768,128]{1,0:T(8,128)(2,1)}) custom-call(bf16[16,176,128]{2,1,0:T(8,128)(2,1)S(1)} %all_to_all.15.mine_ref, bf16[16,176,128]{2,1,0:T(8,128)(2,1)S(1)} %collective-permute-done.4.other_ref, bf16[1024,256]{1,0:T(8,128)(2,1)S(1)} %copy-done), custom_call_target="tpu_custom_call" | custom-call | flops 268435456 | bytes 2097152 | tf_op jit(solution)/shard_map/project/pallas_call | solution.py:271
  52.9 8.2 %all-to-all-start.2 = ((bf16[8,64,256]{2,1,0:T(8,128)(2,1)}), bf16[8,64,256]{2,1,0:T(8,128)(2,1)S(1)}, u32[]{:S(2)}, u32[]{:S(2)}) async-start(bf16[8,64,256]{2,1,0:T(8,128)(2,1)} %get-tuple-element.17), calls=%async_computation.2 | async-start | bytes 524288 | tf_op jit(solution)/shard_map/all_to_all | solution.py:352
  61.1 8.7 %context_anchor.1 = bf16[768,1024]{1,0:T(8,128)(2,1)} custom-call(bf16[768,1024]{1,0:T(8,128)(2,1)} %q_ref.3, bf16[768,128]{1,0:T(8,128)(2,1)} %get-tuple-element.14.k_ref, bf16[768,128]{1,0:T(8,128)(2,1)} %get-tuple-element.15.v_ref, bf16[768,1024]{1,0:T(8,128)(2,1)} %get-tuple-element.16.own_ref, f32[768,128]{1,0:T(8,128)} %get-tuple-element.13.after_ref.lse_ref), custom_call_target="tpu_custom_call" | custom-call | flops 4831838208 | bytes 6291456 | tf_op jit(solution)/shard_map/context_anchor/pallas_call | solution.py:271
  69.8 2.3 %all-to-all-done.2.in_ref = bf16[8,64,256]{2,1,0:T(8,128)(2,1)S(1)} async-done(((bf16[8,64,256]{2,1,0:T(8,128)(2,1)}), bf16[8,64,256]{2,1,0:T(8,128)(2,1)S(1)}, u32[]{:S(2)}, u32[]{:S(2)}) %all-to-all-start.2) | async-done | bytes 262176 | tf_op jit(solution)/shard_map/all_to_all | solution.py:352
  72.2 0.7 final_sum.1
  (1 shorter events, 0.0 us)
Async XLA Ops:
  0.6 5.5 %collective-permute-start = (bf16[768,128]{1,0:T(8,128)(2,1)}, bf16[768,128]{1,0:T(8,128)(2,1)S(1)}, u32[]{:S(2)}, u32[]{:S(2)}) collective-permute-start(bf16[768,128]{1,0:T(8,128)(2,1)} %k_ref.1), channel_id=1, source_target_pairs={{0,8},{8,0},{1,9},{9,1},{2,10},{10,2},{3,11},{11,3},{4,12},{12,4},... | collective-permute-start | bytes 589832 | tf_op jit(solution)/shard_map/ppermute | solution.py:343
  4.0 2.2 %collective-permute-start.1 = (bf16[768,128]{1,0:T(8,128)(2,1)}, bf16[768,128]{1,0:T(8,128)(2,1)S(1)}, u32[]{:S(2)}, u32[]{:S(2)}) collective-permute-start(bf16[768,128]{1,0:T(8,128)(2,1)} %v_ref.1), channel_id=1, source_target_pairs={{0,8},{8,0},{1,9},{9,1},{2,10},{10,2},{3,11},{11,3},{4,12},{12,4},... | collective-permute-start | bytes 589832 | tf_op jit(solution)/shard_map/ppermute | solution.py:343
  4.1 5.2 %collective-permute-start.3 = (bf16[16,128]{1,0:T(8,128)(2,1)S(1)}, bf16[16,128]{1,0:T(8,128)(2,1)S(1)}, u32[]{:S(2)}, u32[]{:S(2)}) collective-permute-start(bf16[16,128]{1,0:T(8,128)(2,1)S(1)} %broadcast.3), channel_id=1, source_target_pairs={{0,64},{64,128},{128,192},{192,0},{1,65},{65,129},{129,193},{193,1... | collective-permute-start | bytes 12296 | tf_op jit(solution)/shard_map/ppermute | solution.py:348
  4.1 5.2 %collective-permute-start.2 = (bf16[16,128]{1,0:T(8,128)(2,1)S(1)}, bf16[16,128]{1,0:T(8,128)(2,1)S(1)}, u32[]{:S(2)}, u32[]{:S(2)}) collective-permute-start(bf16[16,128]{1,0:T(8,128)(2,1)S(1)} %broadcast.3), channel_id=1, source_target_pairs={{0,16},{16,32},{32,48},{48,0},{1,17},{17,33},{33,49},{49,1},{2,18}... | collective-permute-start | bytes 12296 | tf_op jit(solution)/shard_map/ppermute | solution.py:348
  12.4 18.9 %all-to-all-start = ((bf16[16,192,128]{2,1,0:T(8,128)(2,1)}), bf16[16,192,128]{2,1,0:T(8,128)(2,1)S(1)}, u32[]{:S(2)}, u32[]{:S(2)}) async-start(bf16[16,192,128]{2,1,0:T(8,128)(2,1)} %query_attention_4.1.after_ref), calls=%async_computation | async-start | bytes 1572864 | tf_op jit(solution)/shard_map/all_to_all | solution.py:352
  31.4 20.2 %copy-start = (bf16[1024,256]{1,0:T(8,128)(2,1)S(1)}, bf16[1024,256]{1,0:T(8,128)(2,1)}, u32[]{:S(2)}) copy-start(bf16[1024,256]{1,0:T(8,128)(2,1)} %w_ref.1) | copy-start | bytes 1572868
  46.0 5.5 %collective-permute-start.4 = (bf16[16,176,128]{2,1,0:T(8,128)(2,1)S(1)}, bf16[16,176,128]{2,1,0:T(8,128)(2,1)S(1)}, u32[]{:S(2)}, u32[]{:S(2)}) collective-permute-start(bf16[16,176,128]{2,1,0:T(8,128)(2,1)S(1)} %all_to_all.15.mine_ref), channel_id=1, source_target_pairs={{0,8},{8,0},{1,9},{9,1},{2,10},{10,2},{3,11},{11,3},{4,12},{12,4},... | collective-permute-start | bytes 2162696 | tf_op jit(solution)/shard_map/ppermute | solution.py:343
  52.9 19.3 %all-to-all-start.2 = ((bf16[8,64,256]{2,1,0:T(8,128)(2,1)}), bf16[8,64,256]{2,1,0:T(8,128)(2,1)S(1)}, u32[]{:S(2)}, u32[]{:S(2)}) async-start(bf16[8,64,256]{2,1,0:T(8,128)(2,1)} %get-tuple-element.17), calls=%async_computation.2 | async-start | bytes 524288 | tf_op jit(solution)/shard_map/all_to_all | solution.py:352

commit v11 on v8

--- a/solution.py
+++ b/solution.py
@@ -16,6 +16,7 @@
 SEND1 = STATS + ANCHOR_ROWS
 SEND2 = HEAD + ANCHOR_ROWS
 HIDDEN = 1e30
+Z_ORDER = [[4, 5, 6, 7, 0, 1, 2, 3]]
 LOG2_SCALE = 1.4426950408889634 * HEAD ** (-0.5)
 BF = jnp.bfloat16
 F32 = jnp.float32
@@ -132,7 +133,7 @@
     ]
     for copy in copies:
         copy.start()
-    for ref, owner in ((mine_ref, core), (other_ref, 1 - core)):
+    for ref, place in ((mine_ref, 1 - core), (other_ref, core)):
         a = jnp.concatenate(
             [
                 jnp.concatenate([ref[2 * j + half, 0:HEAD, :] for j in range(HEADS)], axis=1)
@@ -142,8 +143,8 @@
         )
         y = jnp.dot(a, w_ref[...], preferred_element_type=F32).astype(BF)
         for z in range(4):
-            out_ref[4 * owner + z] = y[64 * z : 64 * z + 64, :]
-        half = pl.ds(4 * owner, 4)
+            out_ref[4 * place + z] = y[64 * z : 64 * z + 64, :]
+        half = pl.ds(4 * place, 4)
         copies.append(pltpu.make_async_copy(out_ref.at[half], out_hbm.at[half], sems.at[len(copies)]))
         copies[-1].start()
     for copy in copies:
@@ -337,8 +338,8 @@
     return lax.ppermute(value, "c", [(0, 1), (1, 0)])
 
 
-def exchange(value, axes):
-    return lax.all_to_all(value, axes, 0, 0, tiled=True)
+def exchange(value, axes, order=None):
+    return lax.all_to_all(value, axes, 0, 0, axis_index_groups=order, tiled=True)
 
 
 def per_device(ctx_query, context_key, context_value, query, out_weight):
@@ -350,7 +351,7 @@
     gathered = exchange(combine_call(received, lse), ("x", "y"))
     shares, key_a, value_a = project_call(gathered, swap(gathered), out_weight)
     ctx_out = anchor_call(ctx_query, key_a, value_a, own, lse)
-    answer = final_call(exchange(shares, "z"))
+    answer = final_call(exchange(shares, "z", Z_ORDER))
     return ctx_out, answer
 
 

time: 71.1 us -> 70.9 us (level)
  waiting for transfers between devices: 9.53 us -> 7.24 us
  starting transfers between devices: 19.6 us -> 21.7 us
    all_to_all x2, waiting for transfers between devices: 7.49 us -> 5.19 us  [exchange(): lax.all_to_all(value, axes, 0, 0, axis_index_groups=order, tiled=True)]
    all_to_all x2, starting transfers between devices: 13.2 us -> 15.3 us  [exchange(): lax.all_to_all(value, axes, 0, 0, axis_index_groups=order, tiled=True)]
  transfers between devices with their start and end apart: 5 -> 5, of which waited for: 4 -> 3; matrix products, arithmetic and copies ran while one was open for 0% -> 0% of each run, Pallas kernels for 25% -> 25%
where the time goes in v11:
time: 70.9 us; the launch traced here: 70.4 us
  Pallas kernels  25.1 us (35%)
  starting transfers between devices  21.7 us (31%)
  blocking collectives  15.7 us (22%)
  waiting for transfers between devices  7.24 us (10%)
    pallas_call x7, Pallas kernels, run(): pl.pallas_call(kernel, grid=grid, in_specs=in_specs, out_specs=out_specs,...  25.1 us
    all_to_all x1, blocking collectives, exchange(): lax.all_to_all(value, axes, 0, 0, axis_index_groups=order, tiled=True)  15.7 us
    all_to_all x2, starting transfers between devices, exchange(): lax.all_to_all(value, axes, 0, 0, axis_index_groups=order, tiled=True)  15.3 us
    ppermute x3, starting transfers between devices, swap(): return lax.ppermute(value, 'c', [(0, 1), (1, 0)])  6.41 us
    all_to_all x2, waiting for transfers between devices, exchange(): lax.all_to_all(value, axes, 0, 0, axis_index_groups=order, tiled=True)  5.19 us
    ppermute x3, waiting for transfers between devices, swap(): return lax.ppermute(value, 'c', [(0, 1), (1, 0)])  2.05 us
  transfers between devices with their start and end apart: 5, of which 3 were waited for; matrix products, arithmetic and copies ran while one was open for 0% of the time, Pallas kernels for 25%

profile of v11, /device:TPU:1, one launch (start us, length us, event | category | flops | bytes accessed | tf_op | source)
XLA Modules:
  0.0 70.4 jit_solution(12451541926736071222)
XLA Ops:
  0.6 3.3 %collective-permute-start = (bf16[768,128]{1,0:T(8,128)(2,1)}, bf16[768,128]{1,0:T(8,128)(2,1)S(1)}, u32[]{:S(2)}, u32[]{:S(2)}) collective-permute-start(bf16[768,128]{1,0:T(8,128)(2,1)} %k_ref.1), channel_id=1, source_target_pairs={{0,8},{8,0},{1,9},{9,1},{2,10},{10,2},{3,11},{11,3},{4,12},{12,4},... | collective-permute-start | bytes 589832 | tf_op jit(solution)/shard_map/ppermute | solution.py:338
  4.0 0.1 collective-permute-start.1
  4.1 1.3 %prep.1 = (bf16[256,1024]{1,0:T(8,128)(2,1)S(1)}, bf16[768,128]{1,0:T(8,128)(2,1)S(1)}, bf16[768,256]{1,0:T(8,128)(2,1)S(1)}) custom-call(bf16[512,1024]{1,0:T(8,128)(2,1)} %q_hbm.1, bf16[768,128]{1,0:T(8,128)(2,1)} %k_ref.1, bf16[768,128]{1,0:T(8,128)(2,1)} %v_ref.1), custom_call_target="tpu_custom_call" | custom-call | flops 262144 | bytes 2097152 | tf_op jit(solution)/shard_map/prep/pallas_call | solution.py:269
  5.4 0.0 collective-permute-done.kp_ref
  5.4 0.2 collective-permute-done.1.vp_ref
  5.6 5.1 %query_attention.1.after_ref = bf16[16,192,128]{2,1,0:T(8,128)(2,1)} custom-call(bf16[256,1024]{1,0:T(8,128)(2,1)S(1)} %get-tuple-element.10.q_ref, bf16[768,128]{1,0:T(8,128)(2,1)S(1)} %get-tuple-element.11.k_ref, bf16[768,256]{1,0:T(8,128)(2,1)S(1)} %get-tuple-element.12.values_ref, bf16[768,128]{1,0:T(8,128)(2,1)S(1)} %collective-permute-done.kp_ref, ...), custom_call_target="tpu_custom_call" | custom-call | flops 3221225472 | bytes 3145728 | tf_op jit(solution)/shard_map/query_attention/pallas_call | solution.py:269
  10.7 5.0 %all-to-all-start = ((bf16[16,192,128]{2,1,0:T(8,128)(2,1)}), bf16[16,192,128]{2,1,0:T(8,128)(2,1)S(1)}, u32[]{:S(2)}, u32[]{:S(2)}) async-start(bf16[16,192,128]{2,1,0:T(8,128)(2,1)} %query_attention.1.after_ref), calls=%async_computation | async-start | bytes 1572864 | tf_op jit(solution)/shard_map/all_to_all | solution.py:342
  15.7 7.5 %context_own.1 = (bf16[768,1024]{1,0:T(8,128)(2,1)}, f32[768,128]{1,0:T(8,128)}) custom-call(bf16[768,1024]{1,0:T(8,128)(2,1)} %q_ref.3, bf16[768,128]{1,0:T(8,128)(2,1)} %k_ref.1, bf16[768,128]{1,0:T(8,128)(2,1)} %v_ref.1, bf16[16,192,128]{2,1,0:T(8,128)(2,1)} %query_attention.1.after_ref), custom_call_target="tpu_custom_call" | custom-call | flops 3221225472 | bytes 4194304 | tf_op jit(solution)/shard_map/context_own/pallas_call | solution.py:269
  23.2 5.2 %all-to-all-done.in_ref = bf16[16,192,128]{2,1,0:T(8,128)(2,1)S(1)} async-done(((bf16[16,192,128]{2,1,0:T(8,128)(2,1)}), bf16[16,192,128]{2,1,0:T(8,128)(2,1)S(1)}, u32[]{:S(2)}, u32[]{:S(2)}) %all-to-all-start) | async-done | bytes 786464 | tf_op jit(solution)/shard_map/all_to_all | solution.py:342
  28.4 0.0 copy-start
  28.4 0.5 combine.1
  29.0 15.7 %all_to_all.15.mine_ref = bf16[16,176,128]{2,1,0:T(8,128)(2,1)S(1)} all-to-all(bf16[16,176,128]{2,1,0:T(8,128)(2,1)S(1)} %combine.1), channel_id=1, replica_groups=mesh['y'=4,'x'=4,'c'=2,'z'=8] {'x','y'}, dimensions={0} | all-to-all | bytes 1441792 | tf_op jit(solution)/shard_map/all_to_all | solution.py:342
  44.7 3.0 %collective-permute-start.2 = (bf16[16,176,128]{2,1,0:T(8,128)(2,1)S(1)}, bf16[16,176,128]{2,1,0:T(8,128)(2,1)S(1)}, u32[]{:S(2)}, u32[]{:S(2)}) collective-permute-start(bf16[16,176,128]{2,1,0:T(8,128)(2,1)S(1)} %all_to_all.15.mine_ref), channel_id=1, source_target_pairs={{0,8},{8,0},{1,9},{9,1},{2,10},{10,2},{3,11},{11,3},{4,12},{12,4},... | collective-permute-start | bytes 2162696 | tf_op jit(solution)/shard_map/ppermute | solution.py:338
  47.7 1.8 %collective-permute-done.2.other_ref = bf16[16,176,128]{2,1,0:T(8,128)(2,1)S(1)} collective-permute-done((bf16[16,176,128]{2,1,0:T(8,128)(2,1)S(1)}, bf16[16,176,128]{2,1,0:T(8,128)(2,1)S(1)}, u32[]{:S(2)}, u32[]{:S(2)}) %collective-permute-start.2) | collective-permute-done | bytes 720928 | tf_op jit(solution)/shard_map/ppermute | solution.py:338
  49.5 0.0 copy-done
  49.5 1.3 %project.1 = (bf16[8,64,256]{2,1,0:T(8,128)(2,1)}, bf16[768,128]{1,0:T(8,128)(2,1)}, bf16[768,128]{1,0:T(8,128)(2,1)}) custom-call(bf16[16,176,128]{2,1,0:T(8,128)(2,1)S(1)} %all_to_all.15.mine_ref, bf16[16,176,128]{2,1,0:T(8,128)(2,1)S(1)} %collective-permute-done.2.other_ref, bf16[1024,256]{1,0:T(8,128)(2,1)S(1)} %copy-done), custom_call_target="tpu_custom_call" | custom-call | flops 268435456 | bytes 2097152 | tf_op jit(solution)/shard_map/project/pallas_call | solution.py:269
  50.8 10.2 %all-to-all-start.2 = ((bf16[8,64,256]{2,1,0:T(8,128)(2,1)}), bf16[8,64,256]{2,1,0:T(8,128)(2,1)S(1)}, u32[]{:S(2)}, u32[]{:S(2)}) async-start(bf16[8,64,256]{2,1,0:T(8,128)(2,1)} %get-tuple-element.17), calls=%async_computation.2 | async-start | bytes 524288 | tf_op jit(solution)/shard_map/all_to_all | solution.py:342
  61.1 8.7 %context_anchor.1 = bf16[768,1024]{1,0:T(8,128)(2,1)} custom-call(bf16[768,1024]{1,0:T(8,128)(2,1)} %q_ref.3, bf16[768,128]{1,0:T(8,128)(2,1)} %get-tuple-element.14.k_ref, bf16[768,128]{1,0:T(8,128)(2,1)} %get-tuple-element.15.v_ref, bf16[768,1024]{1,0:T(8,128)(2,1)} %get-tuple-element.16.own_ref, f32[768,128]{1,0:T(8,128)} %get-tuple-element.13.after_ref.lse_ref), custom_call_target="tpu_custom_call" | custom-call | flops 4831838208 | bytes 6291456 | tf_op jit(solution)/shard_map/context_anchor/pallas_call | solution.py:269
  69.8 0.0 all-to-all-done.2.in_ref
  69.8 0.7 final_sum.1
Async XLA Ops:
  0.6 4.7 %collective-permute-start = (bf16[768,128]{1,0:T(8,128)(2,1)}, bf16[768,128]{1,0:T(8,128)(2,1)S(1)}, u32[]{:S(2)}, u32[]{:S(2)}) collective-permute-start(bf16[768,128]{1,0:T(8,128)(2,1)} %k_ref.1), channel_id=1, source_target_pairs={{0,8},{8,0},{1,9},{9,1},{2,10},{10,2},{3,11},{11,3},{4,12},{12,4},... | collective-permute-start | bytes 589832 | tf_op jit(solution)/shard_map/ppermute | solution.py:338
  4.0 1.7 %collective-permute-start.1 = (bf16[768,128]{1,0:T(8,128)(2,1)}, bf16[768,128]{1,0:T(8,128)(2,1)S(1)}, u32[]{:S(2)}, u32[]{:S(2)}) collective-permute-start(bf16[768,128]{1,0:T(8,128)(2,1)} %v_ref.1), channel_id=1, source_target_pairs={{0,8},{8,0},{1,9},{9,1},{2,10},{10,2},{3,11},{11,3},{4,12},{12,4},... | collective-permute-start | bytes 589832 | tf_op jit(solution)/shard_map/ppermute | solution.py:338
  10.7 17.7 %all-to-all-start = ((bf16[16,192,128]{2,1,0:T(8,128)(2,1)}), bf16[16,192,128]{2,1,0:T(8,128)(2,1)S(1)}, u32[]{:S(2)}, u32[]{:S(2)}) async-start(bf16[16,192,128]{2,1,0:T(8,128)(2,1)} %query_attention.1.after_ref), calls=%async_computation | async-start | bytes 1572864 | tf_op jit(solution)/shard_map/all_to_all | solution.py:342
  28.4 21.1 %copy-start = (bf16[1024,256]{1,0:T(8,128)(2,1)S(1)}, bf16[1024,256]{1,0:T(8,128)(2,1)}, u32[]{:S(2)}) copy-start(bf16[1024,256]{1,0:T(8,128)(2,1)} %w_ref.1) | copy-start | bytes 1572868
  44.7 4.8 %collective-permute-start.2 = (bf16[16,176,128]{2,1,0:T(8,128)(2,1)S(1)}, bf16[16,176,128]{2,1,0:T(8,128)(2,1)S(1)}, u32[]{:S(2)}, u32[]{:S(2)}) collective-permute-start(bf16[16,176,128]{2,1,0:T(8,128)(2,1)S(1)} %all_to_all.15.mine_ref), channel_id=1, source_target_pairs={{0,8},{8,0},{1,9},{9,1},{2,10},{10,2},{3,11},{11,3},{4,12},{12,4},... | collective-permute-start | bytes 2162696 | tf_op jit(solution)/shard_map/ppermute | solution.py:338
  50.8 19.0 %all-to-all-start.2 = ((bf16[8,64,256]{2,1,0:T(8,128)(2,1)}), bf16[8,64,256]{2,1,0:T(8,128)(2,1)S(1)}, u32[]{:S(2)}, u32[]{:S(2)}) async-start(bf16[8,64,256]{2,1,0:T(8,128)(2,1)} %get-tuple-element.17), calls=%async_computation.2 | async-start | bytes 524288 | tf_op jit(solution)/shard_map/all_to_all | solution.py:342

commit v12 on v11

--- a/solution.py
+++ b/solution.py
@@ -16,7 +16,9 @@
 SEND1 = STATS + ANCHOR_ROWS
 SEND2 = HEAD + ANCHOR_ROWS
 HIDDEN = 1e30
-Z_ORDER = [[4, 5, 6, 7, 0, 1, 2, 3]]
+Z_ORDER = [[6, 7, 0, 1, 2, 3, 4, 5]]
+PLANE_ORDER = [[8, 9, 10, 11, 12, 13, 14, 15, 0, 1, 2, 3, 4, 5, 6, 7]]
+ROOT = 8
 LOG2_SCALE = 1.4426950408889634 * HEAD ** (-0.5)
 BF = jnp.bfloat16
 F32 = jnp.float32
@@ -114,7 +116,7 @@
     for g in range(16):
         out = out + weight_t[:, g : g + 1] * in_ref[g, 0:HEAD, :].astype(F32)
     out = out.astype(BF)
-    anchor = in_ref[0, STATS:SEND1, :]
+    anchor = in_ref[ROOT, STATS:SEND1, :]
     for g in range(16):
         out_ref[g, 0:HEAD, :] = out
         out_ref[g, HEAD:SEND2, :] = anchor
@@ -133,7 +135,7 @@
     ]
     for copy in copies:
         copy.start()
-    for ref, place in ((mine_ref, 1 - core), (other_ref, core)):
+    for ref, owner in ((mine_ref, core), (other_ref, 1 - core)):
         a = jnp.concatenate(
             [
                 jnp.concatenate([ref[2 * j + half, 0:HEAD, :] for j in range(HEADS)], axis=1)
@@ -142,11 +144,14 @@
             axis=0,
         )
         y = jnp.dot(a, w_ref[...], preferred_element_type=F32).astype(BF)
-        for z in range(4):
-            out_ref[4 * place + z] = y[64 * z : 64 * z + 64, :]
-        half = pl.ds(4 * place, 4)
-        copies.append(pltpu.make_async_copy(out_ref.at[half], out_hbm.at[half], sems.at[len(copies)]))
-        copies[-1].start()
+        for t in range(2):
+            place = lax.rem(2 * owner + t + 1, 4)
+            for z in range(2):
+                at = 64 * (2 * t + z)
+                out_ref[2 * place + z] = y[at : at + 64, :]
+            pair = pl.ds(2 * place, 2)
+            copies.append(pltpu.make_async_copy(out_ref.at[pair], out_hbm.at[pair], sems.at[len(copies)]))
+            copies[-1].start()
     for copy in copies:
         copy.wait()
 
@@ -325,7 +330,7 @@
     return run(
         project_kernel, "project", (mine, other, w), [VMEM] * 3,
         (pltpu.HBM((8, 64, 256), BF), pltpu.HBM((BLOCK, HEAD), BF), pltpu.HBM((BLOCK, HEAD), BF)), (HBM,) * 3,
-        [buffer((8, 64, 256)), buffer((BLOCK, HEAD)), buffer((BLOCK, HEAD)), pltpu.SemaphoreType.DMA((4,))],
+        [buffer((8, 64, 256)), buffer((BLOCK, HEAD)), buffer((BLOCK, HEAD)), pltpu.SemaphoreType.DMA((6,))],
         2 * 512 * 1024 * 256, 2 << 20,
     )
 
@@ -346,9 +351,9 @@
     key_p, value_p = swap(context_key), swap(context_value)
     q, k, values = prep_call(query, context_key, context_value)
     sent = query_call(q, k, values, key_p, value_p)
-    received = exchange(sent, ("x", "y"))
+    received = exchange(sent, ("x", "y"), PLANE_ORDER)
     own, lse = own_call(ctx_query, context_key, context_value, sent)
-    gathered = exchange(combine_call(received, lse), ("x", "y"))
+    gathered = exchange(combine_call(received, lse), ("x", "y"), PLANE_ORDER)
     shares, key_a, value_a = project_call(gathered, swap(gathered), out_weight)
     ctx_out = anchor_call(ctx_query, key_a, value_a, own, lse)
     answer = final_call(exchange(shares, "z", Z_ORDER))

time: 70.9 us -> 68.6 us (0.968)
  waiting for transfers between devices: 7.24 us -> 5.93 us
    all_to_all x2, waiting for transfers between devices: 5.19 us -> 3.88 us  [exchange(): lax.all_to_all(value, axes, 0, 0, axis_index_groups=order, tiled=True)]
  transfers between devices with their start and end apart: 5 -> 5, of which waited for: 3 -> 3; matrix products, arithmetic and copies ran while one was open for 0% -> 0% of each run, Pallas kernels for 25% -> 26%
where the time goes in v12:
time: 68.6 us; the launch traced here: 68.2 us
  Pallas kernels  25 us (36%)
  starting transfers between devices  21.1 us (31%)
  blocking collectives  15.5 us (23%)
  waiting for transfers between devices  5.93 us (9%)
    pallas_call x7, Pallas kernels, run(): pl.pallas_call(kernel, grid=grid, in_specs=in_specs, out_specs=out_specs,...  25 us
    all_to_all x1, blocking collectives, exchange(): lax.all_to_all(value, axes, 0, 0, axis_index_groups=order, tiled=True)  15.5 us
    all_to_all x2, starting transfers between devices, exchange(): lax.all_to_all(value, axes, 0, 0, axis_index_groups=order, tiled=True)  15.2 us
    ppermute x3, starting transfers between devices, swap(): return lax.ppermute(value, 'c', [(0, 1), (1, 0)])  5.84 us
    all_to_all x2, waiting for transfers between devices, exchange(): lax.all_to_all(value, axes, 0, 0, axis_index_groups=order, tiled=True)  3.88 us
    ppermute x3, waiting for transfers between devices, swap(): return lax.ppermute(value, 'c', [(0, 1), (1, 0)])  2.05 us
  transfers between devices with their start and end apart: 5, of which 3 were waited for; matrix products, arithmetic and copies ran while one was open for 0% of the time, Pallas kernels for 26%

profile of v12, /device:TPU:1, one launch (start us, length us, event | category | flops | bytes accessed | tf_op | source)
XLA Modules:
  0.0 68.2 jit_solution(17418613652439662109)
XLA Ops:
  0.6 3.3 %collective-permute-start = (bf16[768,128]{1,0:T(8,128)(2,1)}, bf16[768,128]{1,0:T(8,128)(2,1)S(1)}, u32[]{:S(2)}, u32[]{:S(2)}) collective-permute-start(bf16[768,128]{1,0:T(8,128)(2,1)} %k_ref.1), channel_id=1, source_target_pairs={{0,8},{8,0},{1,9},{9,1},{2,10},{10,2},{3,11},{11,3},{4,12},{12,4},... | collective-permute-start | bytes 589832 | tf_op jit(solution)/shard_map/ppermute | solution.py:343
  4.0 0.1 collective-permute-start.1
  4.1 1.3 %prep.1 = (bf16[256,1024]{1,0:T(8,128)(2,1)S(1)}, bf16[768,128]{1,0:T(8,128)(2,1)S(1)}, bf16[768,256]{1,0:T(8,128)(2,1)S(1)}) custom-call(bf16[512,1024]{1,0:T(8,128)(2,1)} %q_hbm.1, bf16[768,128]{1,0:T(8,128)(2,1)} %k_ref.1, bf16[768,128]{1,0:T(8,128)(2,1)} %v_ref.1), custom_call_target="tpu_custom_call" | custom-call | flops 262144 | bytes 2097152 | tf_op jit(solution)/shard_map/prep/pallas_call | solution.py:274
  5.4 0.0 collective-permute-done.kp_ref
  5.4 0.2 collective-permute-done.1.vp_ref
  5.6 5.1 %query_attention.1.after_ref = bf16[16,192,128]{2,1,0:T(8,128)(2,1)} custom-call(bf16[256,1024]{1,0:T(8,128)(2,1)S(1)} %get-tuple-element.10.q_ref, bf16[768,128]{1,0:T(8,128)(2,1)S(1)} %get-tuple-element.11.k_ref, bf16[768,256]{1,0:T(8,128)(2,1)S(1)} %get-tuple-element.12.values_ref, bf16[768,128]{1,0:T(8,128)(2,1)S(1)} %collective-permute-done.kp_ref, ...), custom_call_target="tpu_custom_call" | custom-call | flops 3221225472 | bytes 3145728 | tf_op jit(solution)/shard_map/query_attention/pallas_call | solution.py:274
  10.7 5.9 %all-to-all-start = ((bf16[16,192,128]{2,1,0:T(8,128)(2,1)}), bf16[16,192,128]{2,1,0:T(8,128)(2,1)S(1)}, u32[]{:S(2)}, u32[]{:S(2)}) async-start(bf16[16,192,128]{2,1,0:T(8,128)(2,1)} %query_attention.1.after_ref), calls=%async_computation | async-start | bytes 1572864 | tf_op jit(solution)/shard_map/all_to_all | solution.py:347
  16.5 7.5 %context_own.1 = (bf16[768,1024]{1,0:T(8,128)(2,1)}, f32[768,128]{1,0:T(8,128)}) custom-call(bf16[768,1024]{1,0:T(8,128)(2,1)} %q_ref.3, bf16[768,128]{1,0:T(8,128)(2,1)} %k_ref.1, bf16[768,128]{1,0:T(8,128)(2,1)} %v_ref.1, bf16[16,192,128]{2,1,0:T(8,128)(2,1)} %query_attention.1.after_ref), custom_call_target="tpu_custom_call" | custom-call | flops 3221225472 | bytes 4194304 | tf_op jit(solution)/shard_map/context_own/pallas_call | solution.py:274
  24.0 3.9 %all-to-all-done.in_ref = bf16[16,192,128]{2,1,0:T(8,128)(2,1)S(1)} async-done(((bf16[16,192,128]{2,1,0:T(8,128)(2,1)}), bf16[16,192,128]{2,1,0:T(8,128)(2,1)S(1)}, u32[]{:S(2)}, u32[]{:S(2)}) %all-to-all-start) | async-done | bytes 786464 | tf_op jit(solution)/shard_map/all_to_all | solution.py:347
  27.9 0.0 copy-start
  27.9 0.5 combine.1
  28.5 15.5 %all_to_all.15.mine_ref = bf16[16,176,128]{2,1,0:T(8,128)(2,1)S(1)} all-to-all(bf16[16,176,128]{2,1,0:T(8,128)(2,1)S(1)} %combine.1), channel_id=1, replica_groups={{32,96,160,224,48,112,176,240,0,64,128,192,16,80,144,208},{33,97,161,22..., dimensions={0} | all-to-all | bytes 1441792 | tf_op jit(solution)/shard_map/all_to_all | solution.py:347
  43.9 2.4 %collective-permute-start.2 = (bf16[16,176,128]{2,1,0:T(8,128)(2,1)S(1)}, bf16[16,176,128]{2,1,0:T(8,128)(2,1)S(1)}, u32[]{:S(2)}, u32[]{:S(2)}) collective-permute-start(bf16[16,176,128]{2,1,0:T(8,128)(2,1)S(1)} %all_to_all.15.mine_ref), channel_id=1, source_target_pairs={{0,8},{8,0},{1,9},{9,1},{2,10},{10,2},{3,11},{11,3},{4,12},{12,4},... | collective-permute-start | bytes 2162696 | tf_op jit(solution)/shard_map/ppermute | solution.py:343
  46.3 1.8 %collective-permute-done.2.other_ref = bf16[16,176,128]{2,1,0:T(8,128)(2,1)S(1)} collective-permute-done((bf16[16,176,128]{2,1,0:T(8,128)(2,1)S(1)}, bf16[16,176,128]{2,1,0:T(8,128)(2,1)S(1)}, u32[]{:S(2)}, u32[]{:S(2)}) %collective-permute-start.2) | collective-permute-done | bytes 720928 | tf_op jit(solution)/shard_map/ppermute | solution.py:343
  48.2 0.0 copy-done
  48.2 1.3 %project.1 = (bf16[8,64,256]{2,1,0:T(8,128)(2,1)}, bf16[768,128]{1,0:T(8,128)(2,1)}, bf16[768,128]{1,0:T(8,128)(2,1)}) custom-call(bf16[16,176,128]{2,1,0:T(8,128)(2,1)S(1)} %all_to_all.15.mine_ref, bf16[16,176,128]{2,1,0:T(8,128)(2,1)S(1)} %collective-permute-done.2.other_ref, bf16[1024,256]{1,0:T(8,128)(2,1)S(1)} %copy-done), custom_call_target="tpu_custom_call" | custom-call | flops 268435456 | bytes 2097152 | tf_op jit(solution)/shard_map/project/pallas_call | solution.py:274
  49.4 9.4 %all-to-all-start.2 = ((bf16[8,64,256]{2,1,0:T(8,128)(2,1)}), bf16[8,64,256]{2,1,0:T(8,128)(2,1)S(1)}, u32[]{:S(2)}, u32[]{:S(2)}) async-start(bf16[8,64,256]{2,1,0:T(8,128)(2,1)} %get-tuple-element.17), calls=%async_computation.2 | async-start | bytes 524288 | tf_op jit(solution)/shard_map/all_to_all | solution.py:347
  58.8 8.7 %context_anchor.1 = bf16[768,1024]{1,0:T(8,128)(2,1)} custom-call(bf16[768,1024]{1,0:T(8,128)(2,1)} %q_ref.3, bf16[768,128]{1,0:T(8,128)(2,1)} %get-tuple-element.14.k_ref, bf16[768,128]{1,0:T(8,128)(2,1)} %get-tuple-element.15.v_ref, bf16[768,1024]{1,0:T(8,128)(2,1)} %get-tuple-element.16.own_ref, f32[768,128]{1,0:T(8,128)} %get-tuple-element.13.after_ref.lse_ref), custom_call_target="tpu_custom_call" | custom-call | flops 4831838208 | bytes 6291456 | tf_op jit(solution)/shard_map/context_anchor/pallas_call | solution.py:274
  67.5 0.0 all-to-all-done.2.in_ref
  67.5 0.7 final_sum.1
Async XLA Ops:
  0.6 4.7 %collective-permute-start = (bf16[768,128]{1,0:T(8,128)(2,1)}, bf16[768,128]{1,0:T(8,128)(2,1)S(1)}, u32[]{:S(2)}, u32[]{:S(2)}) collective-permute-start(bf16[768,128]{1,0:T(8,128)(2,1)} %k_ref.1), channel_id=1, source_target_pairs={{0,8},{8,0},{1,9},{9,1},{2,10},{10,2},{3,11},{11,3},{4,12},{12,4},... | collective-permute-start | bytes 589832 | tf_op jit(solution)/shard_map/ppermute | solution.py:343
  4.0 1.7 %collective-permute-start.1 = (bf16[768,128]{1,0:T(8,128)(2,1)}, bf16[768,128]{1,0:T(8,128)(2,1)S(1)}, u32[]{:S(2)}, u32[]{:S(2)}) collective-permute-start(bf16[768,128]{1,0:T(8,128)(2,1)} %v_ref.1), channel_id=1, source_target_pairs={{0,8},{8,0},{1,9},{9,1},{2,10},{10,2},{3,11},{11,3},{4,12},{12,4},... | collective-permute-start | bytes 589832 | tf_op jit(solution)/shard_map/ppermute | solution.py:343
  10.7 17.2 %all-to-all-start = ((bf16[16,192,128]{2,1,0:T(8,128)(2,1)}), bf16[16,192,128]{2,1,0:T(8,128)(2,1)S(1)}, u32[]{:S(2)}, u32[]{:S(2)}) async-start(bf16[16,192,128]{2,1,0:T(8,128)(2,1)} %query_attention.1.after_ref), calls=%async_computation | async-start | bytes 1572864 | tf_op jit(solution)/shard_map/all_to_all | solution.py:347
  27.9 20.3 %copy-start = (bf16[1024,256]{1,0:T(8,128)(2,1)S(1)}, bf16[1024,256]{1,0:T(8,128)(2,1)}, u32[]{:S(2)}) copy-start(bf16[1024,256]{1,0:T(8,128)(2,1)} %w_ref.1) | copy-start | bytes 1572868
  43.9 4.2 %collective-permute-start.2 = (bf16[16,176,128]{2,1,0:T(8,128)(2,1)S(1)}, bf16[16,176,128]{2,1,0:T(8,128)(2,1)S(1)}, u32[]{:S(2)}, u32[]{:S(2)}) collective-permute-start(bf16[16,176,128]{2,1,0:T(8,128)(2,1)S(1)} %all_to_all.15.mine_ref), channel_id=1, source_target_pairs={{0,8},{8,0},{1,9},{9,1},{2,10},{10,2},{3,11},{11,3},{4,12},{12,4},... | collective-permute-start | bytes 2162696 | tf_op jit(solution)/shard_map/ppermute | solution.py:343
  49.4 18.1 %all-to-all-start.2 = ((bf16[8,64,256]{2,1,0:T(8,128)(2,1)}), bf16[8,64,256]{2,1,0:T(8,128)(2,1)S(1)}, u32[]{:S(2)}, u32[]{:S(2)}) async-start(bf16[8,64,256]{2,1,0:T(8,128)(2,1)} %get-tuple-element.17), calls=%async_computation.2 | async-start | bytes 524288 | tf_op jit(solution)/shard_map/all_to_all | solution.py:347

commit v13 on v12

--- a/solution.py
+++ b/solution.py
@@ -16,7 +16,7 @@
 SEND1 = STATS + ANCHOR_ROWS
 SEND2 = HEAD + ANCHOR_ROWS
 HIDDEN = 1e30
-Z_ORDER = [[6, 7, 0, 1, 2, 3, 4, 5]]
+Z_ORDER = [[7, 0, 1, 2, 3, 4, 5, 6]]
 PLANE_ORDER = [[8, 9, 10, 11, 12, 13, 14, 15, 0, 1, 2, 3, 4, 5, 6, 7]]
 ROOT = 8
 LOG2_SCALE = 1.4426950408889634 * HEAD ** (-0.5)
@@ -144,13 +144,10 @@
             axis=0,
         )
         y = jnp.dot(a, w_ref[...], preferred_element_type=F32).astype(BF)
-        for t in range(2):
-            place = lax.rem(2 * owner + t + 1, 4)
-            for z in range(2):
-                at = 64 * (2 * t + z)
-                out_ref[2 * place + z] = y[at : at + 64, :]
-            pair = pl.ds(2 * place, 2)
-            copies.append(pltpu.make_async_copy(out_ref.at[pair], out_hbm.at[pair], sems.at[len(copies)]))
+        for z in range(4):
+            place = lax.rem(4 * owner + z + 1, 8)
+            out_ref[place] = y[64 * z : 64 * z + 64, :]
+            copies.append(pltpu.make_async_copy(out_ref.at[place], out_hbm.at[place], sems.at[len(copies)]))
             copies[-1].start()
     for copy in copies:
         copy.wait()
@@ -330,7 +327,7 @@
     return run(
         project_kernel, "project", (mine, other, w), [VMEM] * 3,
         (pltpu.HBM((8, 64, 256), BF), pltpu.HBM((BLOCK, HEAD), BF), pltpu.HBM((BLOCK, HEAD), BF)), (HBM,) * 3,
-        [buffer((8, 64, 256)), buffer((BLOCK, HEAD)), buffer((BLOCK, HEAD)), pltpu.SemaphoreType.DMA((6,))],
+        [buffer((8, 64, 256)), buffer((BLOCK, HEAD)), buffer((BLOCK, HEAD)), pltpu.SemaphoreType.DMA((10,))],
         2 * 512 * 1024 * 256, 2 << 20,
     )
 

time: 68.6 us -> 68.2 us (level)
  no operation moved by 1% of the time
where the time goes in v13:
time: 68.2 us; the launch traced here: 67.8 us
  Pallas kernels  25.1 us (37%)
  starting transfers between devices  20.6 us (30%)
  blocking collectives  15.5 us (23%)
  waiting for transfers between devices  5.93 us (9%)
    pallas_call x7, Pallas kernels, run(): pl.pallas_call(kernel, grid=grid, in_specs=in_specs, out_specs=out_specs,...  25.1 us
    all_to_all x1, blocking collectives, exchange(): lax.all_to_all(value, axes, 0, 0, axis_index_groups=order, tiled=True)  15.5 us
    all_to_all x2, starting transfers between devices, exchange(): lax.all_to_all(value, axes, 0, 0, axis_index_groups=order, tiled=True)  14.8 us
    ppermute x3, starting transfers between devices, swap(): return lax.ppermute(value, 'c', [(0, 1), (1, 0)])  5.84 us
    all_to_all x2, waiting for transfers between devices, exchange(): lax.all_to_all(value, axes, 0, 0, axis_index_groups=order, tiled=True)  3.88 us
    ppermute x3, waiting for transfers between devices, swap(): return lax.ppermute(value, 'c', [(0, 1), (1, 0)])  2.05 us
  transfers between devices with their start and end apart: 5, of which 3 were waited for; matrix products, arithmetic and copies ran while one was open for 0% of the time, Pallas kernels for 26%

profile of v13, /device:TPU:1, one launch (start us, length us, event | category | flops | bytes accessed | tf_op | source)
XLA Modules:
  0.0 67.8 jit_solution(503389978508968540)
XLA Ops:
  0.6 3.3 %collective-permute-start = (bf16[768,128]{1,0:T(8,128)(2,1)}, bf16[768,128]{1,0:T(8,128)(2,1)S(1)}, u32[]{:S(2)}, u32[]{:S(2)}) collective-permute-start(bf16[768,128]{1,0:T(8,128)(2,1)} %k_ref.1), channel_id=1, source_target_pairs={{0,8},{8,0},{1,9},{9,1},{2,10},{10,2},{3,11},{11,3},{4,12},{12,4},... | collective-permute-start | bytes 589832 | tf_op jit(solution)/shard_map/ppermute | solution.py:340
  4.0 0.1 collective-permute-start.1
  4.1 1.3 %prep.1 = (bf16[256,1024]{1,0:T(8,128)(2,1)S(1)}, bf16[768,128]{1,0:T(8,128)(2,1)S(1)}, bf16[768,256]{1,0:T(8,128)(2,1)S(1)}) custom-call(bf16[512,1024]{1,0:T(8,128)(2,1)} %q_hbm.1, bf16[768,128]{1,0:T(8,128)(2,1)} %k_ref.1, bf16[768,128]{1,0:T(8,128)(2,1)} %v_ref.1), custom_call_target="tpu_custom_call" | custom-call | flops 262144 | bytes 2097152 | tf_op jit(solution)/shard_map/prep/pallas_call | solution.py:271
  5.4 0.0 collective-permute-done.kp_ref
  5.4 0.2 collective-permute-done.1.vp_ref
  5.6 5.1 %query_attention.1.after_ref = bf16[16,192,128]{2,1,0:T(8,128)(2,1)} custom-call(bf16[256,1024]{1,0:T(8,128)(2,1)S(1)} %get-tuple-element.10.q_ref, bf16[768,128]{1,0:T(8,128)(2,1)S(1)} %get-tuple-element.11.k_ref, bf16[768,256]{1,0:T(8,128)(2,1)S(1)} %get-tuple-element.12.values_ref, bf16[768,128]{1,0:T(8,128)(2,1)S(1)} %collective-permute-done.kp_ref, ...), custom_call_target="tpu_custom_call" | custom-call | flops 3221225472 | bytes 3145728 | tf_op jit(solution)/shard_map/query_attention/pallas_call | solution.py:271
  10.7 5.9 %all-to-all-start = ((bf16[16,192,128]{2,1,0:T(8,128)(2,1)}), bf16[16,192,128]{2,1,0:T(8,128)(2,1)S(1)}, u32[]{:S(2)}, u32[]{:S(2)}) async-start(bf16[16,192,128]{2,1,0:T(8,128)(2,1)} %query_attention.1.after_ref), calls=%async_computation | async-start | bytes 1572864 | tf_op jit(solution)/shard_map/all_to_all | solution.py:344
  16.5 7.5 %context_own.1 = (bf16[768,1024]{1,0:T(8,128)(2,1)}, f32[768,128]{1,0:T(8,128)}) custom-call(bf16[768,1024]{1,0:T(8,128)(2,1)} %q_ref.3, bf16[768,128]{1,0:T(8,128)(2,1)} %k_ref.1, bf16[768,128]{1,0:T(8,128)(2,1)} %v_ref.1, bf16[16,192,128]{2,1,0:T(8,128)(2,1)} %query_attention.1.after_ref), custom_call_target="tpu_custom_call" | custom-call | flops 3221225472 | bytes 4194304 | tf_op jit(solution)/shard_map/context_own/pallas_call | solution.py:271
  24.0 3.9 %all-to-all-done.in_ref = bf16[16,192,128]{2,1,0:T(8,128)(2,1)S(1)} async-done(((bf16[16,192,128]{2,1,0:T(8,128)(2,1)}), bf16[16,192,128]{2,1,0:T(8,128)(2,1)S(1)}, u32[]{:S(2)}, u32[]{:S(2)}) %all-to-all-start) | async-done | bytes 786464 | tf_op jit(solution)/shard_map/all_to_all | solution.py:344
  27.9 0.0 copy-start
  27.9 0.5 combine.1
  28.5 15.5 %all_to_all.15.mine_ref = bf16[16,176,128]{2,1,0:T(8,128)(2,1)S(1)} all-to-all(bf16[16,176,128]{2,1,0:T(8,128)(2,1)S(1)} %combine.1), channel_id=1, replica_groups={{32,96,160,224,48,112,176,240,0,64,128,192,16,80,144,208},{33,97,161,22..., dimensions={0} | all-to-all | bytes 1441792 | tf_op jit(solution)/shard_map/all_to_all | solution.py:344
  43.9 2.4 %collective-permute-start.2 = (bf16[16,176,128]{2,1,0:T(8,128)(2,1)S(1)}, bf16[16,176,128]{2,1,0:T(8,128)(2,1)S(1)}, u32[]{:S(2)}, u32[]{:S(2)}) collective-permute-start(bf16[16,176,128]{2,1,0:T(8,128)(2,1)S(1)} %all_to_all.15.mine_ref), channel_id=1, source_target_pairs={{0,8},{8,0},{1,9},{9,1},{2,10},{10,2},{3,11},{11,3},{4,12},{12,4},... | collective-permute-start | bytes 2162696 | tf_op jit(solution)/shard_map/ppermute | solution.py:340
  46.3 1.8 %collective-permute-done.2.other_ref = bf16[16,176,128]{2,1,0:T(8,128)(2,1)S(1)} collective-permute-done((bf16[16,176,128]{2,1,0:T(8,128)(2,1)S(1)}, bf16[16,176,128]{2,1,0:T(8,128)(2,1)S(1)}, u32[]{:S(2)}, u32[]{:S(2)}) %collective-permute-start.2) | collective-permute-done | bytes 720928 | tf_op jit(solution)/shard_map/ppermute | solution.py:340
  48.2 0.0 copy-done
  48.2 1.3 %project.1 = (bf16[8,64,256]{2,1,0:T(8,128)(2,1)}, bf16[768,128]{1,0:T(8,128)(2,1)}, bf16[768,128]{1,0:T(8,128)(2,1)}) custom-call(bf16[16,176,128]{2,1,0:T(8,128)(2,1)S(1)} %all_to_all.15.mine_ref, bf16[16,176,128]{2,1,0:T(8,128)(2,1)S(1)} %collective-permute-done.2.other_ref, bf16[1024,256]{1,0:T(8,128)(2,1)S(1)} %copy-done), custom_call_target="tpu_custom_call" | custom-call | flops 268435456 | bytes 2097152 | tf_op jit(solution)/shard_map/project/pallas_call | solution.py:271
  49.5 8.9 %all-to-all-start.2 = ((bf16[8,64,256]{2,1,0:T(8,128)(2,1)}), bf16[8,64,256]{2,1,0:T(8,128)(2,1)S(1)}, u32[]{:S(2)}, u32[]{:S(2)}) async-start(bf16[8,64,256]{2,1,0:T(8,128)(2,1)} %get-tuple-element.17), calls=%async_computation.2 | async-start | bytes 524288 | tf_op jit(solution)/shard_map/all_to_all | solution.py:344
  58.4 8.7 %context_anchor.1 = bf16[768,1024]{1,0:T(8,128)(2,1)} custom-call(bf16[768,1024]{1,0:T(8,128)(2,1)} %q_ref.3, bf16[768,128]{1,0:T(8,128)(2,1)} %get-tuple-element.14.k_ref, bf16[768,128]{1,0:T(8,128)(2,1)} %get-tuple-element.15.v_ref, bf16[768,1024]{1,0:T(8,128)(2,1)} %get-tuple-element.16.own_ref, f32[768,128]{1,0:T(8,128)} %get-tuple-element.13.after_ref.lse_ref), custom_call_target="tpu_custom_call" | custom-call | flops 4831838208 | bytes 6291456 | tf_op jit(solution)/shard_map/context_anchor/pallas_call | solution.py:271
  67.1 0.0 all-to-all-done.2.in_ref
  67.1 0.7 final_sum.1
Async XLA Ops:
  0.6 4.7 %collective-permute-start = (bf16[768,128]{1,0:T(8,128)(2,1)}, bf16[768,128]{1,0:T(8,128)(2,1)S(1)}, u32[]{:S(2)}, u32[]{:S(2)}) collective-permute-start(bf16[768,128]{1,0:T(8,128)(2,1)} %k_ref.1), channel_id=1, source_target_pairs={{0,8},{8,0},{1,9},{9,1},{2,10},{10,2},{3,11},{11,3},{4,12},{12,4},... | collective-permute-start | bytes 589832 | tf_op jit(solution)/shard_map/ppermute | solution.py:340
  4.0 1.7 %collective-permute-start.1 = (bf16[768,128]{1,0:T(8,128)(2,1)}, bf16[768,128]{1,0:T(8,128)(2,1)S(1)}, u32[]{:S(2)}, u32[]{:S(2)}) collective-permute-start(bf16[768,128]{1,0:T(8,128)(2,1)} %v_ref.1), channel_id=1, source_target_pairs={{0,8},{8,0},{1,9},{9,1},{2,10},{10,2},{3,11},{11,3},{4,12},{12,4},... | collective-permute-start | bytes 589832 | tf_op jit(solution)/shard_map/ppermute | solution.py:340
  10.7 17.2 %all-to-all-start = ((bf16[16,192,128]{2,1,0:T(8,128)(2,1)}), bf16[16,192,128]{2,1,0:T(8,128)(2,1)S(1)}, u32[]{:S(2)}, u32[]{:S(2)}) async-start(bf16[16,192,128]{2,1,0:T(8,128)(2,1)} %query_attention.1.after_ref), calls=%async_computation | async-start | bytes 1572864 | tf_op jit(solution)/shard_map/all_to_all | solution.py:344
  27.9 20.3 %copy-start = (bf16[1024,256]{1,0:T(8,128)(2,1)S(1)}, bf16[1024,256]{1,0:T(8,128)(2,1)}, u32[]{:S(2)}) copy-start(bf16[1024,256]{1,0:T(8,128)(2,1)} %w_ref.1) | copy-start | bytes 1572868
  43.9 4.2 %collective-permute-start.2 = (bf16[16,176,128]{2,1,0:T(8,128)(2,1)S(1)}, bf16[16,176,128]{2,1,0:T(8,128)(2,1)S(1)}, u32[]{:S(2)}, u32[]{:S(2)}) collective-permute-start(bf16[16,176,128]{2,1,0:T(8,128)(2,1)S(1)} %all_to_all.15.mine_ref), channel_id=1, source_target_pairs={{0,8},{8,0},{1,9},{9,1},{2,10},{10,2},{3,11},{11,3},{4,12},{12,4},... | collective-permute-start | bytes 2162696 | tf_op jit(solution)/shard_map/ppermute | solution.py:340
  49.5 17.6 %all-to-all-start.2 = ((bf16[8,64,256]{2,1,0:T(8,128)(2,1)}), bf16[8,64,256]{2,1,0:T(8,128)(2,1)S(1)}, u32[]{:S(2)}, u32[]{:S(2)}) async-start(bf16[8,64,256]{2,1,0:T(8,128)(2,1)} %get-tuple-element.17), calls=%async_computation.2 | async-start | bytes 524288 | tf_op jit(solution)/shard_map/all_to_all | solution.py:344

commit v14 on v13

--- a/solution.py
+++ b/solution.py
@@ -17,8 +17,8 @@
 SEND2 = HEAD + ANCHOR_ROWS
 HIDDEN = 1e30
 Z_ORDER = [[7, 0, 1, 2, 3, 4, 5, 6]]
-PLANE_ORDER = [[8, 9, 10, 11, 12, 13, 14, 15, 0, 1, 2, 3, 4, 5, 6, 7]]
-ROOT = 8
+PLANE_ORDER = [[10, 11, 12, 13, 14, 15, 0, 1, 2, 3, 4, 5, 6, 7, 8, 9]]
+ROOT = 6
 LOG2_SCALE = 1.4426950408889634 * HEAD ** (-0.5)
 BF = jnp.bfloat16
 F32 = jnp.float32

time: 68.2 us -> 67.3 us (0.987)
  waiting for transfers between devices: 5.93 us -> 4.61 us
    all_to_all x2, waiting for transfers between devices: 3.88 us -> 2.57 us  [exchange(): lax.all_to_all(value, axes, 0, 0, axis_index_groups=order, tiled=True)]
    all_to_all x2, starting transfers between devices: 14.8 us -> 16 us  [exchange(): lax.all_to_all(value, axes, 0, 0, axis_index_groups=order, tiled=True)]
where the time goes in v14:
time: 67.3 us; the launch traced here: 66.8 us
  Pallas kernels  25.1 us (37%)
  starting transfers between devices  21.2 us (32%)
  blocking collectives  15.3 us (23%)
  waiting for transfers between devices  4.61 us (7%)
  between operations  0.68 us (1%)
    pallas_call x7, Pallas kernels, run(): pl.pallas_call(kernel, grid=grid, in_specs=in_specs, out_specs=out_specs,...  25.1 us
    all_to_all x2, starting transfers between devices, exchange(): lax.all_to_all(value, axes, 0, 0, axis_index_groups=order, tiled=True)  16 us
    all_to_all x1, blocking collectives, exchange(): lax.all_to_all(value, axes, 0, 0, axis_index_groups=order, tiled=True)  15.3 us
    ppermute x3, starting transfers between devices, swap(): return lax.ppermute(value, 'c', [(0, 1), (1, 0)])  5.17 us
    all_to_all x2, waiting for transfers between devices, exchange(): lax.all_to_all(value, axes, 0, 0, axis_index_groups=order, tiled=True)  2.57 us
    ppermute x3, waiting for transfers between devices, swap(): return lax.ppermute(value, 'c', [(0, 1), (1, 0)])  2.05 us
  transfers between devices with their start and end apart: 5, of which 3 were waited for; matrix products, arithmetic and copies ran while one was open for 0% of the time, Pallas kernels for 26%

profile of v14, /device:TPU:1, one launch (start us, length us, event | category | flops | bytes accessed | tf_op | source)
XLA Modules:
  0.0 66.8 jit_solution(7351987753703228955)
XLA Ops:
  0.6 3.3 %collective-permute-start = (bf16[768,128]{1,0:T(8,128)(2,1)}, bf16[768,128]{1,0:T(8,128)(2,1)S(1)}, u32[]{:S(2)}, u32[]{:S(2)}) collective-permute-start(bf16[768,128]{1,0:T(8,128)(2,1)} %k_ref.1), channel_id=1, source_target_pairs={{0,8},{8,0},{1,9},{9,1},{2,10},{10,2},{3,11},{11,3},{4,12},{12,4},... | collective-permute-start | bytes 589832 | tf_op jit(solution)/shard_map/ppermute | solution.py:340
  4.0 0.1 collective-permute-start.1
  4.1 1.3 %prep.1 = (bf16[256,1024]{1,0:T(8,128)(2,1)S(1)}, bf16[768,128]{1,0:T(8,128)(2,1)S(1)}, bf16[768,256]{1,0:T(8,128)(2,1)S(1)}) custom-call(bf16[512,1024]{1,0:T(8,128)(2,1)} %q_hbm.1, bf16[768,128]{1,0:T(8,128)(2,1)} %k_ref.1, bf16[768,128]{1,0:T(8,128)(2,1)} %v_ref.1), custom_call_target="tpu_custom_call" | custom-call | flops 262144 | bytes 2097152 | tf_op jit(solution)/shard_map/prep/pallas_call | solution.py:271
  5.4 0.0 collective-permute-done.kp_ref
  5.4 0.2 collective-permute-done.1.vp_ref
  5.6 5.1 %query_attention.1.after_ref = bf16[16,192,128]{2,1,0:T(8,128)(2,1)} custom-call(bf16[256,1024]{1,0:T(8,128)(2,1)S(1)} %get-tuple-element.10.q_ref, bf16[768,128]{1,0:T(8,128)(2,1)S(1)} %get-tuple-element.11.k_ref, bf16[768,256]{1,0:T(8,128)(2,1)S(1)} %get-tuple-element.12.values_ref, bf16[768,128]{1,0:T(8,128)(2,1)S(1)} %collective-permute-done.kp_ref, ...), custom_call_target="tpu_custom_call" | custom-call | flops 3221225472 | bytes 3145728 | tf_op jit(solution)/shard_map/query_attention/pallas_call | solution.py:271
  10.7 7.1 %all-to-all-start = ((bf16[16,192,128]{2,1,0:T(8,128)(2,1)}), bf16[16,192,128]{2,1,0:T(8,128)(2,1)S(1)}, u32[]{:S(2)}, u32[]{:S(2)}) async-start(bf16[16,192,128]{2,1,0:T(8,128)(2,1)} %query_attention.1.after_ref), calls=%async_computation | async-start | bytes 1572864 | tf_op jit(solution)/shard_map/all_to_all | solution.py:344
  17.8 7.5 %context_own.1 = (bf16[768,1024]{1,0:T(8,128)(2,1)}, f32[768,128]{1,0:T(8,128)}) custom-call(bf16[768,1024]{1,0:T(8,128)(2,1)} %q_ref.3, bf16[768,128]{1,0:T(8,128)(2,1)} %k_ref.1, bf16[768,128]{1,0:T(8,128)(2,1)} %v_ref.1, bf16[16,192,128]{2,1,0:T(8,128)(2,1)} %query_attention.1.after_ref), custom_call_target="tpu_custom_call" | custom-call | flops 3221225472 | bytes 4194304 | tf_op jit(solution)/shard_map/context_own/pallas_call | solution.py:271
  25.3 2.6 %all-to-all-done.in_ref = bf16[16,192,128]{2,1,0:T(8,128)(2,1)S(1)} async-done(((bf16[16,192,128]{2,1,0:T(8,128)(2,1)}), bf16[16,192,128]{2,1,0:T(8,128)(2,1)S(1)}, u32[]{:S(2)}, u32[]{:S(2)}) %all-to-all-start) | async-done | bytes 786464 | tf_op jit(solution)/shard_map/all_to_all | solution.py:344
  27.8 0.0 copy-start
  27.8 0.5 combine.1
  28.4 15.3 %all_to_all.15.mine_ref = bf16[16,176,128]{2,1,0:T(8,128)(2,1)S(1)} all-to-all(bf16[16,176,128]{2,1,0:T(8,128)(2,1)S(1)} %combine.1), channel_id=1, replica_groups={{160,224,48,112,176,240,0,64,128,192,16,80,144,208,32,96},{161,225,49,1..., dimensions={0} | all-to-all | bytes 1441792 | tf_op jit(solution)/shard_map/all_to_all | solution.py:344
  43.7 1.7 %collective-permute-start.2 = (bf16[16,176,128]{2,1,0:T(8,128)(2,1)S(1)}, bf16[16,176,128]{2,1,0:T(8,128)(2,1)S(1)}, u32[]{:S(2)}, u32[]{:S(2)}) collective-permute-start(bf16[16,176,128]{2,1,0:T(8,128)(2,1)S(1)} %all_to_all.15.mine_ref), channel_id=1, source_target_pairs={{0,8},{8,0},{1,9},{9,1},{2,10},{10,2},{3,11},{11,3},{4,12},{12,4},... | collective-permute-start | bytes 2162696 | tf_op jit(solution)/shard_map/ppermute | solution.py:340
  45.4 1.8 %collective-permute-done.2.other_ref = bf16[16,176,128]{2,1,0:T(8,128)(2,1)S(1)} collective-permute-done((bf16[16,176,128]{2,1,0:T(8,128)(2,1)S(1)}, bf16[16,176,128]{2,1,0:T(8,128)(2,1)S(1)}, u32[]{:S(2)}, u32[]{:S(2)}) %collective-permute-start.2) | collective-permute-done | bytes 720928 | tf_op jit(solution)/shard_map/ppermute | solution.py:340
  47.3 0.0 copy-done
  47.3 1.3 %project.1 = (bf16[8,64,256]{2,1,0:T(8,128)(2,1)}, bf16[768,128]{1,0:T(8,128)(2,1)}, bf16[768,128]{1,0:T(8,128)(2,1)}) custom-call(bf16[16,176,128]{2,1,0:T(8,128)(2,1)S(1)} %all_to_all.15.mine_ref, bf16[16,176,128]{2,1,0:T(8,128)(2,1)S(1)} %collective-permute-done.2.other_ref, bf16[1024,256]{1,0:T(8,128)(2,1)S(1)} %copy-done), custom_call_target="tpu_custom_call" | custom-call | flops 268435456 | bytes 2097152 | tf_op jit(solution)/shard_map/project/pallas_call | solution.py:271
  48.6 8.9 %all-to-all-start.2 = ((bf16[8,64,256]{2,1,0:T(8,128)(2,1)}), bf16[8,64,256]{2,1,0:T(8,128)(2,1)S(1)}, u32[]{:S(2)}, u32[]{:S(2)}) async-start(bf16[8,64,256]{2,1,0:T(8,128)(2,1)} %get-tuple-element.17), calls=%async_computation.2 | async-start | bytes 524288 | tf_op jit(solution)/shard_map/all_to_all | solution.py:344
  57.5 8.7 %context_anchor.1 = bf16[768,1024]{1,0:T(8,128)(2,1)} custom-call(bf16[768,1024]{1,0:T(8,128)(2,1)} %q_ref.3, bf16[768,128]{1,0:T(8,128)(2,1)} %get-tuple-element.14.k_ref, bf16[768,128]{1,0:T(8,128)(2,1)} %get-tuple-element.15.v_ref, bf16[768,1024]{1,0:T(8,128)(2,1)} %get-tuple-element.16.own_ref, f32[768,128]{1,0:T(8,128)} %get-tuple-element.13.after_ref.lse_ref), custom_call_target="tpu_custom_call" | custom-call | flops 4831838208 | bytes 6291456 | tf_op jit(solution)/shard_map/context_anchor/pallas_call | solution.py:271
  66.2 0.0 all-to-all-done.2.in_ref
  66.2 0.7 final_sum.1
Async XLA Ops:
  0.6 4.7 %collective-permute-start = (bf16[768,128]{1,0:T(8,128)(2,1)}, bf16[768,128]{1,0:T(8,128)(2,1)S(1)}, u32[]{:S(2)}, u32[]{:S(2)}) collective-permute-start(bf16[768,128]{1,0:T(8,128)(2,1)} %k_ref.1), channel_id=1, source_target_pairs={{0,8},{8,0},{1,9},{9,1},{2,10},{10,2},{3,11},{11,3},{4,12},{12,4},... | collective-permute-start | bytes 589832 | tf_op jit(solution)/shard_map/ppermute | solution.py:340
  4.0 1.7 %collective-permute-start.1 = (bf16[768,128]{1,0:T(8,128)(2,1)}, bf16[768,128]{1,0:T(8,128)(2,1)S(1)}, u32[]{:S(2)}, u32[]{:S(2)}) collective-permute-start(bf16[768,128]{1,0:T(8,128)(2,1)} %v_ref.1), channel_id=1, source_target_pairs={{0,8},{8,0},{1,9},{9,1},{2,10},{10,2},{3,11},{11,3},{4,12},{12,4},... | collective-permute-start | bytes 589832 | tf_op jit(solution)/shard_map/ppermute | solution.py:340
  10.7 17.1 %all-to-all-start = ((bf16[16,192,128]{2,1,0:T(8,128)(2,1)}), bf16[16,192,128]{2,1,0:T(8,128)(2,1)S(1)}, u32[]{:S(2)}, u32[]{:S(2)}) async-start(bf16[16,192,128]{2,1,0:T(8,128)(2,1)} %query_attention.1.after_ref), calls=%async_computation | async-start | bytes 1572864 | tf_op jit(solution)/shard_map/all_to_all | solution.py:344
  27.8 19.4 %copy-start = (bf16[1024,256]{1,0:T(8,128)(2,1)S(1)}, bf16[1024,256]{1,0:T(8,128)(2,1)}, u32[]{:S(2)}) copy-start(bf16[1024,256]{1,0:T(8,128)(2,1)} %w_ref.1) | copy-start | bytes 1572868
  43.7 3.6 %collective-permute-start.2 = (bf16[16,176,128]{2,1,0:T(8,128)(2,1)S(1)}, bf16[16,176,128]{2,1,0:T(8,128)(2,1)S(1)}, u32[]{:S(2)}, u32[]{:S(2)}) collective-permute-start(bf16[16,176,128]{2,1,0:T(8,128)(2,1)S(1)} %all_to_all.15.mine_ref), channel_id=1, source_target_pairs={{0,8},{8,0},{1,9},{9,1},{2,10},{10,2},{3,11},{11,3},{4,12},{12,4},... | collective-permute-start | bytes 2162696 | tf_op jit(solution)/shard_map/ppermute | solution.py:340
  48.6 17.6 %all-to-all-start.2 = ((bf16[8,64,256]{2,1,0:T(8,128)(2,1)}), bf16[8,64,256]{2,1,0:T(8,128)(2,1)S(1)}, u32[]{:S(2)}, u32[]{:S(2)}) async-start(bf16[8,64,256]{2,1,0:T(8,128)(2,1)} %get-tuple-element.17), calls=%async_computation.2 | async-start | bytes 524288 | tf_op jit(solution)/shard_map/all_to_all | solution.py:344
